TPU v7x, 32 devices: a whole 2x2x4 slice. The times are simulated.
32 devices in a mesh: row: 16 (over z, y, core), col: 2 (over x).
Axes of the slice: x: 2, y: 2, z: 4, core: 2. Of those that a mesh axis runs over, the one named last changes fastest.
Arguments:
- hamiltonian: float32 [3072, 3072], P('row', 'col'), may hold values from -2 to 2, as said below
- vectors: float32 [3072, 512], P(('row', 'col')), may hold values from -6 to 6
Outputs:
- filtered: float32 [3072, 512], P(('row', 'col'))
Inputs may be any that keep to these rules, and one draw needn't show every extreme that they name: `hamiltonian`: exactly symmetric, with a diagonal part and a dense part of comparable weight.
All inputs are finite; a program needn't handle non-finite values.
Results may differ from a plain program's by a relative error of at most 0.0001.
Values sent between devices are 32-bit elements; how exact they have to be, the bound alone decides.
No kernel may reach another device: no remote copies, remote signals or barrier semaphores. Data moves between devices by JAX's collectives and lax.ppermute only.
A program may use at most 64 MiB of HBM per device.

v0:
```python
import jax
import jax.numpy as jnp
from jax import lax
from jax.sharding import PartitionSpec as P

DEGREE = 2


center = 0.6
half_width = 1.8


def transposed_product(left, right):
    return lax.dot_general(
        left,
        right,
        (((0,), (0,)), ((), ())),
        precision=lax.Precision.HIGHEST,
        preferred_element_type=jnp.float32,
    )


def plain_product(left, right):
    return jnp.dot(left, right, precision=lax.Precision.HIGHEST, preferred_element_type=jnp.float32)


def on_device(hamiltonian, vectors):
    row_index = lax.axis_index("row")
    col_index = lax.axis_index("col")
    rows_block, cols_block = hamiltonian.shape
    global_rows = row_index * rows_block + lax.iota(jnp.int32, rows_block)
    global_cols = col_index * cols_block + lax.iota(jnp.int32, cols_block)
    on_diagonal = global_rows[:, None] == global_cols[None, :]
    shifted = hamiltonian - jnp.where(on_diagonal, jnp.float32(center), jnp.float32(0.0))
    older = vectors
    recent = vectors
    for degree in range(1, DEGREE + 1):
        if degree % 2 == 1:
            row_block = lax.all_gather(recent, "col", axis=0, tiled=True)
            total = lax.psum(transposed_product(shifted, row_block), "row")
        else:
            partial_sum = plain_product(shifted, recent)
            total = lax.psum_scatter(partial_sum, "col", scatter_dimension=0, tiled=True)
        if degree == 1:
            fresh = total * (1.0 / half_width)
        else:
            fresh = 2.0 / half_width * total - older
        older = recent
        recent = fresh
    return recent


def solution(mesh):
    return jax.shard_map(
        on_device,
        mesh=mesh,
        in_specs=(P("row", "col"), P(("row", "col"), None)),
        out_specs=P(("row", "col"), None),
        check_vma=False,
    )
```

profile of v0, /device:TPU:0, one launch (start us, length us, event | category | flops | bytes accessed | tf_op | source)
XLA Modules:
  0.0 152.1 jit_solution(3164160389957467732)
XLA Ops:
  6.5 0.0 all-reduce.2.cloned.1.call-start
  6.5 8.8 %all_gather.3 = f32[192,512]{1,0:T(8,128)S(1)} all-gather(f32[96,512]{1,0:T(8,128)} %param.3), channel_id=1, replica_groups=mesh['row'=16,'col'=2] {'col'}, dimensions={0}, use_global_device_ids=true | all-gather | bytes 589824 | tf_op jit(solution)/shard_map/all_gather | solution.py:39
  15.3 5.8 %fusion.3 = f32[1536,512]{1,0:T(8,128)} fusion(f32[192,512]{1,0:T(8,128)S(1)} %all_gather.3, f32[192,1536]{1,0:T(8,128)} %param.2, s32[1536]{0:T(1024)S(1)} %iota_add_fusion, s32[192]{0:T(256)S(1)} %iota_add_fusion.1), kind=kOutput, calls=%fused_computation.4 | convolution fusion | flops 1812824064 | bytes 4725504 | tf_op jit(solution)/shard_map/dot_general | solution.py:14
  21.1 0.0 copy-start
  21.1 0.0 all-reduce.2.cloned.1.call-update
  21.1 0.0 copy-start.1
  21.1 0.0 reduce-scatter.2.cloned.1.call-start
  21.2 105.0 %all-reduce.2.cloned.1.call-done = f32[1536,512]{1,0:T(8,128)} async-done(((f32[1536,512]{1,0:T(8,128)}), f32[1536,512]{1,0:T(8,128)}) %all-reduce.2.cloned.1.call-update) | async-done | bytes 3145744 | tf_op jit(solution)/shard_map/psum | solution.py:40
  126.2 0.0 copy-done
  126.2 5.1 %fusion = f32[192,512]{1,0:T(8,128)} fusion(f32[1536,512]{1,0:T(8,128)} %all-reduce.2.cloned.1.call-done, f32[192,1536]{1,0:T(8,128)S(1)} %copy-done, s32[1536]{0:T(1024)S(1)} %iota_add_fusion, s32[192]{0:T(256)S(1)} %iota_add_fusion.1), kind=kOutput, calls=%fused_computation | convolution fusion | flops 1813610496 | bytes 4725504 | tf_op jit(solution)/shard_map/dot_general | solution.py:24
  131.2 0.0 reduce-scatter.2.cloned.1.call-update
  131.3 12.4 %reduce-scatter.2.cloned.1.call-done = f32[96,512]{1,0:T(8,128)} async-done(((f32[192,512]{1,0:T(8,128)}), f32[96,512]{1,0:T(8,128)}) %reduce-scatter.2.cloned.1.call-update) | async-done | bytes 196624 | tf_op jit(solution)/shard_map/reduce_scatter | solution.py:43
  143.7 0.0 copy-done.1
  143.7 1.6 %multiply_subtract_fusion = f32[96,512]{1,0:T(8,128)} fusion(f32[96,512]{1,0:T(8,128)S(1)} %copy-done.1, f32[96,512]{1,0:T(8,128)} %reduce-scatter.2.cloned.1.call-done), kind=kLoop, calls=%fused_computation.13 | loop fusion | flops 98304 | bytes 589824 | tf_op jit(solution)/shard_map/sub | solution.py:47
  (2 shorter events, 0.0 us)
Async XLA Ops:
  6.5 119.6 %all-reduce.2.cloned.1.call-start = ((), (), s32[]{:S(2)}) async-start(), calls=%async_computation.1 | async-start | bytes 6291456 | tf_op jit(solution)/shard_map/psum | solution.py:40
  21.1 105.1 %copy-start = (f32[192,1536]{1,0:T(8,128)S(1)}, f32[192,1536]{1,0:T(8,128)}, u32[]{:S(2)}) copy-start(f32[192,1536]{1,0:T(8,128)} %param.2) | copy-start | bytes 3538948
  21.1 122.6 %copy-start.1 = (f32[96,512]{1,0:T(8,128)S(1)}, f32[96,512]{1,0:T(8,128)}, u32[]{:S(2)}) copy-start(f32[96,512]{1,0:T(8,128)} %param.3) | copy-start | bytes 589828
  21.1 122.6 %reduce-scatter.2.cloned.1.call-start = ((), (), s32[]{:S(2)}) async-start(), calls=%async_computation.2 | async-start | bytes 589824 | tf_op jit(solution)/shard_map/reduce_scatter | solution.py:43
Sparse Core Ops, SparseCore 0:
  21.2 104.8 all-reduce.1
  131.4 12.2 reduce-scatter.1
where the time goes:
time: 152 us
  waiting for transfers between devices  117 us (77%)
  between operations  13.4 us (9%)
  matrix products  10.8 us (7%)
  blocking collectives  8.77 us (6%)
  other arithmetic  1.64 us (1%)
    psum x1, waiting for transfers between devices, on_device(): total = lax.psum(transposed_product(shifted, row_block), 'row')  105 us
    reduce_scatter x1, waiting for transfers between devices, on_device(): lax.psum_scatter(partial_sum, 'col', scatter_dimension=0, tiled=True)  12.4 us
    all_gather x1, blocking collectives, on_device(): row_block = lax.all_gather(recent, 'col', axis=0, tiled=True)  8.77 us
    dot_general x1, matrix products, transposed_product(): lax.dot_general(left, right, (((0,), (0,)), ((), ())), precision=lax.Prec...  5.75 us
    dot_general x1, matrix products, plain_product(): jnp.dot(left, right, precision=lax.Precision.HIGHEST, preferred_element_t...  5.07 us
  transfers between devices with their start and end apart: 2, of which 2 were waited for; matrix products, arithmetic and copies ran while one was open for 0% of the time, Pallas kernels for 0%

commit v1 on v0

v1 whole, which is shorter than its diff:
```python
import jax
import jax.numpy as jnp
from jax import lax
from jax.sharding import PartitionSpec as P

DEGREE = 2
CHUNKS = 1

center = 0.6
half_width = 1.8


def product(left, right, left_dim):
    return lax.dot_general(
        left,
        right,
        (((left_dim,), (0,)), ((), ())),
        precision=lax.Precision.HIGH,
        preferred_element_type=jnp.float32,
    )


def on_device(rows, cols, hamiltonian, vectors):
    row_index = lax.axis_index("row")
    col_index = lax.axis_index("col")
    rows_block, cols_block = hamiltonian.shape
    part, width = vectors.shape
    half, quarter = width // 2, cols_block // 4
    core = row_index % 2
    place = (row_index // 2) % 4

    def exchange(block, row_mask, col_mask):
        mask = row_mask * cols + col_mask
        pairs = [(i, i ^ mask) for i in range(rows * cols)]
        return lax.ppermute(block, ("row", "col"), pairs)

    own_half = lax.dynamic_slice(vectors, (0, core * half), (part, half))
    other_half = lax.dynamic_slice(vectors, (0, (1 - core) * half), (part, half))
    pieces = []
    for k in range(cols):
        pieces.append(exchange(own_half, 0, k) if k else own_half)
        pieces.append(exchange(other_half, 1, k))
    block = jnp.concatenate(pieces, axis=0)

    global_rows = row_index * rows_block + lax.iota(jnp.int32, rows_block)
    global_cols = col_index * cols_block + lax.iota(jnp.int32, cols_block)
    on_diagonal = global_rows[:, None] == global_cols[None, :]
    shifted = hamiltonian - jnp.where(on_diagonal, jnp.float32(center), jnp.float32(0.0))
    shifted = jnp.concatenate(
        [lax.dynamic_slice(shifted, (0, (place ^ k) * quarter), (rows_block, quarter)) for k in (0, 2, 1, 3)], axis=1
    )
    mine = jnp.concatenate(
        [lax.dynamic_slice(shifted, ((col_index ^ k) * part, 0), (part, cols_block)) for k in range(cols)], axis=0
    )
    paired = exchange(mine, 1, 0)
    matrix = jnp.concatenate(
        [piece[k * part : (k + 1) * part] for k in range(cols) for piece in (mine, paired)], axis=0
    )
    kept, given = matrix[:, : 2 * quarter], matrix[:, 2 * quarter :]
    taken = exchange(given, 2, 0)
    square = jnp.concatenate([kept, taken], axis=0)

    span = half // CHUNKS
    chunks = [block[:, c * span : (c + 1) * span] for c in range(CHUNKS)]
    results = []
    for chunk in chunks:
        total = product(kept[:, :quarter], chunk, 0)
        others = [
            exchange(product(part_of, chunk, 0), 2 * k, 0)
            for k, part_of in ((3, given[:, quarter:]), (1, given[:, :quarter]), (2, kept[:, quarter:]))
        ]
        for term in others:
            total = total + term
        mask = 8
        while mask < rows:
            total = total + exchange(total, mask, 0)
            mask *= 2
        fresh = total * (1.0 / half_width)
        second = jnp.concatenate([fresh, exchange(fresh, 4, 0)], axis=0)
        partial = product(square, second, 1)
        total = partial[: 2 * part]
        terms = []
        for k in range(1, 2 * cols):
            terms.append(exchange(partial[2 * part * k : 2 * part * (k + 1)], 2 * (k // cols), k % cols))
        for term in terms:
            total = total + term
        results.append(total)
    total = jnp.concatenate(results, axis=1)
    own = total[:part]
    other = exchange(total[part:], 1, 0)
    first = jnp.where(core == 0, own, other)
    last = jnp.where(core == 0, other, own)
    return 2.0 / half_width * jnp.concatenate([first, last], axis=1) - vectors


def solution(mesh):
    rows, cols = mesh.shape["row"], mesh.shape["col"]

    def local(hamiltonian, vectors):
        return on_device(rows, cols, hamiltonian, vectors)

    return jax.shard_map(
        local,
        mesh=mesh,
        in_specs=(P("row", "col"), P(("row", "col"), None)),
        out_specs=P(("row", "col"), None),
        check_vma=False,
    )
```

time: 152 us -> 79.2 us (0.52)
  waiting for transfers between devices: 117 us -> 54.7 us
  starting transfers between devices: 0.04 us -> 16.1 us
  between operations: 13.4 us -> 0.16 us
  blocking collectives: 8.77 us -> 0 us
  matrix products: 10.8 us -> 3.77 us
    psum x1 -> x0, waiting for transfers between devices: 105 us -> none  [on_device(): total = lax.psum(transposed_product(shifted, row_block), 'row')]
    ppermute x0 -> x14, waiting for transfers between devices: none -> 54.7 us  [exchange(): return lax.ppermute(block, ('row', 'col'), pairs)]
    ppermute x0 -> x14, starting transfers between devices: none -> 16.1 us  [exchange(): return lax.ppermute(block, ('row', 'col'), pairs)]
    reduce_scatter x1 -> x0, waiting for transfers between devices: 12.4 us -> none  [on_device(): lax.psum_scatter(partial_sum, 'col', scatter_dimension=0, tiled=True)]
    all_gather x1 -> x0, blocking collectives: 8.77 us -> none  [on_device(): row_block = lax.all_gather(recent, 'col', axis=0, tiled=True)]
    dot_general x2 -> x5, matrix products: 10.8 us -> 3.77 us  [product(): lax.dot_general(left, right, (((left_dim,), (0,)), ((), ())), precision=l...]
  transfers between devices with their start and end apart: 2 -> 14, of which waited for: 2 -> 11; matrix products, arithmetic and copies ran while one was open for 0% -> 4% of each run, Pallas kernels for 0% -> 0%
where the time goes in v1:
time: 79.2 us; the launch traced here: 78.9 us
  waiting for transfers between devices  54.7 us (69%)
  starting transfers between devices  16.1 us (20%)
  matrix products  3.77 us (5%)
  other arithmetic  2.68 us (3%)
  local copies, waits for them, and re-layouts  1.45 us (2%)
    ppermute x14, waiting for transfers between devices, exchange(): return lax.ppermute(block, ('row', 'col'), pairs)  54.7 us
    ppermute x14, starting transfers between devices, exchange(): return lax.ppermute(block, ('row', 'col'), pairs)  16.1 us
    dot_general x5, matrix products, product(): lax.dot_general(left, right, (((left_dim,), (0,)), ((), ())), precision=l...  3.77 us
  transfers between devices with their start and end apart: 14, of which 11 were waited for; matrix products, arithmetic and copies ran while one was open for 4% of the time, Pallas kernels for 0%

profile of v1, /device:TPU:0, one launch (start us, length us, event | category | flops | bytes accessed | tf_op | source)
XLA Modules:
  0.0 78.9 jit_solution(7388980112062940767)
XLA Ops:
  0.0 1.4 %select_subtract_fusion = f32[192,1536]{1,0:T(8,128)S(1)} fusion(f32[192,1536]{1,0:T(8,128)} %param.2, s32[1536]{0:T(1024)S(1)} %iota_add_fusion, s32[192]{0:T(256)S(1)} %iota_add_fusion.1), kind=kLoop, calls=%fused_computation.10 | loop fusion | flops 884736 | bytes 2366208 | tf_op jit(solution)/shard_map/sub | solution.py:48
  2.5 1.0 %constant_dynamic-slice_fusion.1 = (f32[96,256]{1,0:T(8,128)S(1)}, f32[96,256]{1,0:T(8,128)S(1)}) fusion(f32[96,512]{1,0:T(8,128)} %param.3, s32[]{:T(128)S(6)} %select_n.66, s32[]{:T(128)S(6)} %select_n.67), kind=kLoop, calls=%fused_computation.32 | loop fusion | bytes 393224 | tf_op jit(solution)/shard_map/dynamic_slice | solution.py:37
  3.4 2.7 %collective-permute-start.4 = (f32[96,256]{1,0:T(8,128)S(1)}, f32[96,256]{1,0:T(8,128)S(1)}, u32[]{:S(2)}, u32[]{:S(2)}) collective-permute-start(f32[96,256]{1,0:T(8,128)S(1)} %get-tuple-element.21), channel_id=1, source_target_pairs={{0,3},{1,2},{2,1},{3,0},{4,7},{5,6},{6,5},{7,4},{8,11},{9,10},{10,... | collective-permute-start | bytes 294920 | tf_op jit(solution)/shard_map/ppermute | solution.py:35
  6.8 2.4 %collective-permute-done.4 = f32[96,256]{1,0:T(8,128)S(1)} collective-permute-done((f32[96,256]{1,0:T(8,128)S(1)}, f32[96,256]{1,0:T(8,128)S(1)}, u32[]{:S(2)}, u32[]{:S(2)}) %collective-permute-start.4) | collective-permute-done | bytes 98336 | tf_op jit(solution)/shard_map/ppermute | solution.py:35
  9.2 2.3 %collective-permute-done.3 = f32[96,256]{1,0:T(8,128)S(1)} collective-permute-done((f32[96,256]{1,0:T(8,128)S(1)}, f32[96,256]{1,0:T(8,128)S(1)}, u32[]{:S(2)}, u32[]{:S(2)}) %collective-permute-start.3) | collective-permute-done | bytes 98336 | tf_op jit(solution)/shard_map/ppermute | solution.py:35
  12.2 1.8 %collective-permute-start.7 = (f32[384,256]{1,0:T(8,128)S(1)}, f32[384,256]{1,0:T(8,128)S(1)}, u32[]{:S(2)}, u32[]{:S(2)}) collective-permute-start(f32[384,256]{1,0:T(8,128)S(1)} %fusion.9), channel_id=1, source_target_pairs={{0,8},{1,9},{2,10},{3,11},{4,12},{5,13},{6,14},{7,15},{8,0},{9,1},... | collective-permute-start | bytes 1179656 | tf_op jit(solution)/shard_map/ppermute | solution.py:35
  14.7 1.5 %collective-permute-start.5 = (f32[384,256]{1,0:T(8,128)S(1)}, f32[384,256]{1,0:T(8,128)S(1)}, u32[]{:S(2)}, u32[]{:S(2)}) collective-permute-start(f32[384,256]{1,0:T(8,128)S(1)} %fusion.13), channel_id=1, source_target_pairs={{0,12},{1,13},{2,14},{3,15},{4,8},{5,9},{6,10},{7,11},{8,4},{9,5},... | collective-permute-start | bytes 1179656 | tf_op jit(solution)/shard_map/ppermute | solution.py:35
  17.4 1.8 %collective-permute-start.1 = (f32[384,768]{1,0:T(8,128)S(1)}, f32[384,768]{1,0:T(8,128)S(1)}, u32[]{:S(2)}, u32[]{:S(2)}) collective-permute-start(f32[384,768]{1,0:T(8,128)S(1)} %get-tuple-element.6), channel_id=1, source_target_pairs={{0,4},{1,5},{2,6},{3,7},{4,0},{5,1},{6,2},{7,3},{8,12},{9,13},{10,... | collective-permute-start | bytes 3538952 | tf_op jit(solution)/shard_map/ppermute | solution.py:35
  19.2 5.1 %collective-permute-done.7 = f32[384,256]{1,0:T(8,128)S(1)} collective-permute-done((f32[384,256]{1,0:T(8,128)S(1)}, f32[384,256]{1,0:T(8,128)S(1)}, u32[]{:S(2)}, u32[]{:S(2)}) %collective-permute-start.7) | collective-permute-done | bytes 393248 | tf_op jit(solution)/shard_map/ppermute | solution.py:35
  24.3 8.4 %collective-permute-done.5 = f32[384,256]{1,0:T(8,128)S(1)} collective-permute-done((f32[384,256]{1,0:T(8,128)S(1)}, f32[384,256]{1,0:T(8,128)S(1)}, u32[]{:S(2)}, u32[]{:S(2)}) %collective-permute-start.5) | collective-permute-done | bytes 393248 | tf_op jit(solution)/shard_map/ppermute | solution.py:35
  32.7 4.7 %collective-permute-done.6 = f32[384,256]{1,0:T(8,128)S(1)} collective-permute-done((f32[384,256]{1,0:T(8,128)S(1)}, f32[384,256]{1,0:T(8,128)S(1)}, u32[]{:S(2)}, u32[]{:S(2)}) %collective-permute-start.6) | collective-permute-done | bytes 393248 | tf_op jit(solution)/shard_map/ppermute | solution.py:35
  38.1 2.7 %collective-permute-start.8 = (f32[384,256]{1,0:T(8,128)S(1)}, f32[384,256]{1,0:T(8,128)S(1)}, u32[]{:S(2)}, u32[]{:S(2)}) collective-permute-start(f32[384,256]{1,0:T(8,128)S(1)} %fusion.5), channel_id=1, source_target_pairs={{0,16},{1,17},{2,18},{3,19},{4,20},{5,21},{6,22},{7,23},{8,24},{9,... | collective-permute-start | bytes 1179656 | tf_op jit(solution)/shard_map/ppermute | solution.py:35
  40.7 14.1 %collective-permute-done.8 = f32[384,256]{1,0:T(8,128)S(1)} collective-permute-done((f32[384,256]{1,0:T(8,128)S(1)}, f32[384,256]{1,0:T(8,128)S(1)}, u32[]{:S(2)}, u32[]{:S(2)}) %collective-permute-start.8) | collective-permute-done | bytes 393248 | tf_op jit(solution)/shard_map/ppermute | solution.py:35
  54.9 0.7 collective-permute-start.9
  55.6 9.3 %collective-permute-done.9 = f32[384,256]{1,0:T(8,128)S(1)} collective-permute-done((f32[384,256]{1,0:T(8,128)S(1)}, f32[384,256]{1,0:T(8,128)S(1)}, u32[]{:S(2)}, u32[]{:S(2)}) %collective-permute-start.9) | collective-permute-done | bytes 393248 | tf_op jit(solution)/shard_map/ppermute | solution.py:35
  64.9 1.1 %fusion = f32[768,256]{1,0:T(8,128)S(1)} fusion(f32[384,768]{1,0:T(8,128)S(1)} %collective-permute-done.1, f32[384,768]{1,0:T(8,128)S(1)} %get-tuple-element.5, f32[384,256]{1,0:T(8,128)S(1)} %collective-permute-done.9, f32[384,256]{1,0:T(8,128)S(1)} %add_multiply_fusion), kind=kOutput, calls=%fused_computation.1 | convolution fusion | flops 906756096 | bytes 3932160 | tf_op jit(solution)/shard_map/dot_general | solution.py:14
  66.1 1.2 %collective-permute-start.10 = (f32[192,256]{1,0:T(8,128)S(1)}, f32[192,256]{1,0:T(8,128)S(1)}, u32[]{:S(2)}, u32[]{:S(2)}) collective-permute-start(f32[192,256]{1,0:T(8,128)S(1)} %get-tuple-element.15), channel_id=1, source_target_pairs={{0,1},{1,0},{2,3},{3,2},{4,5},{5,4},{6,7},{7,6},{8,9},{9,8},{10,11... | collective-permute-start | bytes 589832 | tf_op jit(solution)/shard_map/ppermute | solution.py:35
  67.3 0.9 %collective-permute-start.12 = (f32[192,256]{1,0:T(8,128)S(1)}, f32[192,256]{1,0:T(8,128)S(1)}, u32[]{:S(2)}, u32[]{:S(2)}) collective-permute-start(f32[192,256]{1,0:T(8,128)S(1)} %get-tuple-element.16), channel_id=1, source_target_pairs={{0,5},{1,4},{2,7},{3,6},{4,1},{5,0},{6,3},{7,2},{8,13},{9,12},{10,... | collective-permute-start | bytes 589832 | tf_op jit(solution)/shard_map/ppermute | solution.py:35
  68.2 1.4 %collective-permute-start.11 = (f32[192,256]{1,0:T(8,128)S(1)}, f32[192,256]{1,0:T(8,128)S(1)}, u32[]{:S(2)}, u32[]{:S(2)}) collective-permute-start(f32[192,256]{1,0:T(8,128)S(1)} %get-tuple-element.17), channel_id=1, source_target_pairs={{0,4},{1,5},{2,6},{3,7},{4,0},{5,1},{6,2},{7,3},{8,12},{9,13},{10,... | collective-permute-start | bytes 589832 | tf_op jit(solution)/shard_map/ppermute | solution.py:35
  69.6 3.4 %collective-permute-done.10 = f32[192,256]{1,0:T(8,128)S(1)} collective-permute-done((f32[192,256]{1,0:T(8,128)S(1)}, f32[192,256]{1,0:T(8,128)S(1)}, u32[]{:S(2)}, u32[]{:S(2)}) %collective-permute-start.10) | collective-permute-done | bytes 196640 | tf_op jit(solution)/shard_map/ppermute | solution.py:35
  73.1 2.3 %collective-permute-done.12 = f32[192,256]{1,0:T(8,128)S(1)} collective-permute-done((f32[192,256]{1,0:T(8,128)S(1)}, f32[192,256]{1,0:T(8,128)S(1)}, u32[]{:S(2)}, u32[]{:S(2)}) %collective-permute-start.12) | collective-permute-done | bytes 196640 | tf_op jit(solution)/shard_map/ppermute | solution.py:35
  75.4 1.4 %collective-permute-done.11 = f32[192,256]{1,0:T(8,128)S(1)} collective-permute-done((f32[192,256]{1,0:T(8,128)S(1)}, f32[192,256]{1,0:T(8,128)S(1)}, u32[]{:S(2)}, u32[]{:S(2)}) %collective-permute-start.11) | collective-permute-done | bytes 196640 | tf_op jit(solution)/shard_map/ppermute | solution.py:35
  76.9 1.3 %collective-permute-done.13 = f32[96,256]{1,0:T(8,128)S(1)} collective-permute-done((f32[96,256]{1,0:T(8,128)S(1)}, f32[96,256]{1,0:T(8,128)S(1)}, u32[]{:S(2)}, u32[]{:S(2)}) %collective-permute-start.13) | collective-permute-done | bytes 98336 | tf_op jit(solution)/shard_map/ppermute | solution.py:35
  78.2 0.7 fusion.18
  (28 shorter events, 5.2 us)
Async XLA Ops:
  1.9 4.7 %collective-permute-start = (f32[192,1536]{1,0:T(8,128)S(1)}, f32[192,1536]{1,0:T(8,128)S(1)}, u32[]{:S(2)}, u32[]{:S(2)}) collective-permute-start(f32[192,1536]{1,0:T(8,128)S(1)} %pad_maximum_fusion.2), channel_id=1, source_target_pairs={{0,2},{1,3},{2,0},{3,1},{4,6},{5,7},{6,4},{7,5},{8,10},{9,11},{10,... | collective-permute-start | bytes 3538952 | tf_op jit(solution)/shard_map/ppermute | solution.py:35
  3.4 5.8 %collective-permute-start.4 = (f32[96,256]{1,0:T(8,128)S(1)}, f32[96,256]{1,0:T(8,128)S(1)}, u32[]{:S(2)}, u32[]{:S(2)}) collective-permute-start(f32[96,256]{1,0:T(8,128)S(1)} %get-tuple-element.21), channel_id=1, source_target_pairs={{0,3},{1,2},{2,1},{3,0},{4,7},{5,6},{6,5},{7,4},{8,11},{9,10},{10,... | collective-permute-start | bytes 294920 | tf_op jit(solution)/shard_map/ppermute | solution.py:35
  6.1 3.1 %collective-permute-start.2 = (f32[96,256]{1,0:T(8,128)S(1)}, f32[96,256]{1,0:T(8,128)S(1)}, u32[]{:S(2)}, u32[]{:S(2)}) collective-permute-start(f32[96,256]{1,0:T(8,128)S(1)} %get-tuple-element.21), channel_id=1, source_target_pairs={{0,2},{1,3},{2,0},{3,1},{4,6},{5,7},{6,4},{7,5},{8,10},{9,11},{10,... | collective-permute-start | bytes 294920 | tf_op jit(solution)/shard_map/ppermute | solution.py:35
  6.1 5.4 %collective-permute-start.3 = (f32[96,256]{1,0:T(8,128)S(1)}, f32[96,256]{1,0:T(8,128)S(1)}, u32[]{:S(2)}, u32[]{:S(2)}) collective-permute-start(f32[96,256]{1,0:T(8,128)S(1)} %get-tuple-element.20), channel_id=1, source_target_pairs={{0,1},{1,0},{2,3},{3,2},{4,5},{5,4},{6,7},{7,6},{8,9},{9,8},{10,11... | collective-permute-start | bytes 294920 | tf_op jit(solution)/shard_map/ppermute | solution.py:35
  12.2 12.1 %collective-permute-start.7 = (f32[384,256]{1,0:T(8,128)S(1)}, f32[384,256]{1,0:T(8,128)S(1)}, u32[]{:S(2)}, u32[]{:S(2)}) collective-permute-start(f32[384,256]{1,0:T(8,128)S(1)} %fusion.9), channel_id=1, source_target_pairs={{0,8},{1,9},{2,10},{3,11},{4,12},{5,13},{6,14},{7,15},{8,0},{9,1},... | collective-permute-start | bytes 1179656 | tf_op jit(solution)/shard_map/ppermute | solution.py:35
  14.7 17.9 %collective-permute-start.5 = (f32[384,256]{1,0:T(8,128)S(1)}, f32[384,256]{1,0:T(8,128)S(1)}, u32[]{:S(2)}, u32[]{:S(2)}) collective-permute-start(f32[384,256]{1,0:T(8,128)S(1)} %fusion.13), channel_id=1, source_target_pairs={{0,12},{1,13},{2,14},{3,15},{4,8},{5,9},{6,10},{7,11},{8,4},{9,5},... | collective-permute-start | bytes 1179656 | tf_op jit(solution)/shard_map/ppermute | solution.py:35
  16.8 20.5 %collective-permute-start.6 = (f32[384,256]{1,0:T(8,128)S(1)}, f32[384,256]{1,0:T(8,128)S(1)}, u32[]{:S(2)}, u32[]{:S(2)}) collective-permute-start(f32[384,256]{1,0:T(8,128)S(1)} %fusion.11), channel_id=1, source_target_pairs={{0,4},{1,5},{2,6},{3,7},{4,0},{5,1},{6,2},{7,3},{8,12},{9,13},{10,... | collective-permute-start | bytes 1179656 | tf_op jit(solution)/shard_map/ppermute | solution.py:35
  17.4 47.5 %collective-permute-start.1 = (f32[384,768]{1,0:T(8,128)S(1)}, f32[384,768]{1,0:T(8,128)S(1)}, u32[]{:S(2)}, u32[]{:S(2)}) collective-permute-start(f32[384,768]{1,0:T(8,128)S(1)} %get-tuple-element.6), channel_id=1, source_target_pairs={{0,4},{1,5},{2,6},{3,7},{4,0},{5,1},{6,2},{7,3},{8,12},{9,13},{10,... | collective-permute-start | bytes 3538952 | tf_op jit(solution)/shard_map/ppermute | solution.py:35
  38.1 16.7 %collective-permute-start.8 = (f32[384,256]{1,0:T(8,128)S(1)}, f32[384,256]{1,0:T(8,128)S(1)}, u32[]{:S(2)}, u32[]{:S(2)}) collective-permute-start(f32[384,256]{1,0:T(8,128)S(1)} %fusion.5), channel_id=1, source_target_pairs={{0,16},{1,17},{2,18},{3,19},{4,20},{5,21},{6,22},{7,23},{8,24},{9,... | collective-permute-start | bytes 1179656 | tf_op jit(solution)/shard_map/ppermute | solution.py:35
  54.9 10.0 %collective-permute-start.9 = (f32[384,256]{1,0:T(8,128)S(1)}, f32[384,256]{1,0:T(8,128)S(1)}, u32[]{:S(2)}, u32[]{:S(2)}) collective-permute-start(f32[384,256]{1,0:T(8,128)S(1)} %add_multiply_fusion), channel_id=1, source_target_pairs={{0,8},{1,9},{2,10},{3,11},{4,12},{5,13},{6,14},{7,15},{8,0},{9,1},... | collective-permute-start | bytes 1179656 | tf_op jit(solution)/shard_map/ppermute | solution.py:35
  66.0 12.2 %copy-start = (f32[96,512]{1,0:T(8,128)S(1)}, f32[96,512]{1,0:T(8,128)}, u32[]{:S(2)}) copy-start(f32[96,512]{1,0:T(8,128)} %param.3) | copy-start | bytes 589828
  66.1 7.0 %collective-permute-start.10 = (f32[192,256]{1,0:T(8,128)S(1)}, f32[192,256]{1,0:T(8,128)S(1)}, u32[]{:S(2)}, u32[]{:S(2)}) collective-permute-start(f32[192,256]{1,0:T(8,128)S(1)} %get-tuple-element.15), channel_id=1, source_target_pairs={{0,1},{1,0},{2,3},{3,2},{4,5},{5,4},{6,7},{7,6},{8,9},{9,8},{10,11... | collective-permute-start | bytes 589832 | tf_op jit(solution)/shard_map/ppermute | solution.py:35
  67.3 8.1 %collective-permute-start.12 = (f32[192,256]{1,0:T(8,128)S(1)}, f32[192,256]{1,0:T(8,128)S(1)}, u32[]{:S(2)}, u32[]{:S(2)}) collective-permute-start(f32[192,256]{1,0:T(8,128)S(1)} %get-tuple-element.16), channel_id=1, source_target_pairs={{0,5},{1,4},{2,7},{3,6},{4,1},{5,0},{6,3},{7,2},{8,13},{9,12},{10,... | collective-permute-start | bytes 589832 | tf_op jit(solution)/shard_map/ppermute | solution.py:35
  68.2 8.5 %collective-permute-start.11 = (f32[192,256]{1,0:T(8,128)S(1)}, f32[192,256]{1,0:T(8,128)S(1)}, u32[]{:S(2)}, u32[]{:S(2)}) collective-permute-start(f32[192,256]{1,0:T(8,128)S(1)} %get-tuple-element.17), channel_id=1, source_target_pairs={{0,4},{1,5},{2,6},{3,7},{4,0},{5,1},{6,2},{7,3},{8,12},{9,13},{10,... | collective-permute-start | bytes 589832 | tf_op jit(solution)/shard_map/ppermute | solution.py:35
  76.8 1.4 %collective-permute-start.13 = (f32[96,256]{1,0:T(8,128)S(1)}, f32[96,256]{1,0:T(8,128)S(1)}, u32[]{:S(2)}, u32[]{:S(2)}) collective-permute-start(f32[96,256]{1,0:T(8,128)S(1)} %slice.73), channel_id=1, source_target_pairs={{0,2},{1,3},{2,0},{3,1},{4,6},{5,7},{6,4},{7,5},{8,10},{9,11},{10,... | collective-permute-start | bytes 294920 | tf_op jit(solution)/shard_map/ppermute | solution.py:35

commit v2 on v1

v2 whole, which is shorter than its diff:
```python
import jax
import jax.numpy as jnp
from jax import lax
from jax.sharding import PartitionSpec as P

DEGREE = 2
CHUNKS = 2

center = 0.6
half_width = 1.8


def product(left, right, left_dim):
    return lax.dot_general(
        left,
        right,
        (((left_dim,), (0,)), ((), ())),
        precision=lax.Precision.HIGH,
        preferred_element_type=jnp.float32,
    )


def after(value, *earlier):
    return lax.optimization_barrier((value, *earlier))[0]


def on_device(rows, cols, hamiltonian, vectors):
    row_index = lax.axis_index("row")
    col_index = lax.axis_index("col")
    rows_block, cols_block = hamiltonian.shape
    part, width = vectors.shape
    half, quarter = width // 2, cols_block // 4
    span = half // CHUNKS
    core = row_index % 2
    place = (row_index // 2) % 4

    def exchange(block, row_masks, col_mask):
        masks = row_masks if isinstance(row_masks, tuple) else (row_masks, row_masks)
        pairs = [(i, i ^ (masks[i // cols % 2] * cols + col_mask)) for i in range(rows * cols)]
        return lax.ppermute(block, ("row", "col"), pairs)

    partner = exchange(hamiltonian, 1, 0)
    order = [place, place ^ (2 - core), place ^ (1 + core), place ^ 3]

    def prepared(block, block_row):
        global_rows = block_row * rows_block + lax.iota(jnp.int32, rows_block)
        global_cols = col_index * cols_block + lax.iota(jnp.int32, cols_block)
        on_diagonal = global_rows[:, None] == global_cols[None, :]
        shifted = block - jnp.where(on_diagonal, jnp.float32(center), jnp.float32(0.0))
        placed = jnp.concatenate(
            [lax.dynamic_slice(shifted, (0, q * quarter), (rows_block, quarter)) for q in order], axis=1
        )
        return [lax.dynamic_slice(placed, ((col_index ^ k) * part, 0), (part, cols_block)) for k in range(cols)]

    ours, theirs = prepared(hamiltonian, row_index), prepared(partner, row_index ^ 1)
    matrix = jnp.concatenate([block for k in range(cols) for block in (ours[k], theirs[k])], axis=0)

    chunks = []
    for c in range(CHUNKS):
        own = lax.dynamic_slice(vectors, (0, core * half + c * span), (part, span))
        other = lax.dynamic_slice(vectors, (0, (1 - core) * half + c * span), (part, span))
        if c:
            own, other, _ = lax.optimization_barrier((own, other, matrix))
        pieces = []
        for k in range(cols):
            pieces.append(exchange(own, 0, k) if k else own)
            pieces.append(exchange(other, 1, k))
        chunks.append(jnp.concatenate(pieces, axis=0))

    results = []
    given = partial = None
    for chunk in chunks:
        if results:
            chunk = after(chunk, given)
        given = product(matrix[:, 2 * quarter :], chunk, 0)
        received = exchange(given, (2, 4), 0)
        passed = product(matrix[:, quarter : 2 * quarter], chunk, 0) + received[quarter:]
        total = product(matrix[:, :quarter], chunk, 0) + received[:quarter]
        total = total + exchange(passed, (4, 2), 0)
        mask = 8
        while mask < rows:
            total = total + exchange(total, mask, 0)
            mask *= 2
        fresh = total * (1.0 / half_width)
        fresh = jnp.concatenate([fresh, exchange(fresh, (4, 2), 0)], axis=0)
        fresh = jnp.concatenate([fresh, exchange(fresh, (2, 4), 0)], axis=0)
        if results:
            fresh = after(fresh, partial)
        partial = product(matrix, fresh, 1)
        total = partial[: 2 * part]
        for term in [exchange(partial[2 * part * k : 2 * part * (k + 1)], 0, k) for k in range(1, cols)]:
            total = total + term
        results.append(total)
    total = jnp.concatenate(results, axis=1)
    own = total[:part]
    other = exchange(total[part:], 1, 0)
    first = jnp.where(core == 0, own, other)
    last = jnp.where(core == 0, other, own)
    return 2.0 / half_width * jnp.concatenate([first, last], axis=1) - vectors


def solution(mesh):
    rows, cols = mesh.shape["row"], mesh.shape["col"]

    def local(hamiltonian, vectors):
        return on_device(rows, cols, hamiltonian, vectors)

    return jax.shard_map(
        local,
        mesh=mesh,
        in_specs=(P("row", "col"), P(("row", "col"), None)),
        out_specs=P(("row", "col"), None),
        check_vma=False,
    )
```

time: 79.2 us -> 70.8 us (0.89)
  waiting for transfers between devices: 54.7 us -> 31.1 us
  starting transfers between devices: 16.1 us -> 27.7 us
  matrix products: 3.77 us -> 7.18 us
    ppermute x14 -> x20, waiting for transfers between devices: 54.7 us -> 31.1 us  [exchange(): return lax.ppermute(block, ('row', 'col'), pairs)]
    ppermute x14 -> x20, starting transfers between devices: 16.1 us -> 27.7 us  [exchange(): return lax.ppermute(block, ('row', 'col'), pairs)]
    dot_general x5 -> x8, matrix products: 3.77 us -> 7.18 us  [product(): lax.dot_general(left, right, (((left_dim,), (0,)), ((), ())), precision=l...]
  transfers between devices with their start and end apart: 14 -> 20, of which waited for: 11 -> 12; matrix products, arithmetic and copies ran while one was open for 4% -> 15% of each run, Pallas kernels for 0% -> 0%
where the time goes in v2:
time: 70.8 us; the launch traced here: 70.5 us
  waiting for transfers between devices  31.1 us (44%)
  starting transfers between devices  27.7 us (39%)
  matrix products  7.18 us (10%)
  other arithmetic  2.94 us (4%)
  local copies, waits for them, and re-layouts  1.35 us (2%)
    ppermute x20, waiting for transfers between devices, exchange(): return lax.ppermute(block, ('row', 'col'), pairs)  31.1 us
    ppermute x20, starting transfers between devices, exchange(): return lax.ppermute(block, ('row', 'col'), pairs)  27.7 us
    dot_general x8, matrix products, product(): lax.dot_general(left, right, (((left_dim,), (0,)), ((), ())), precision=l...  7.18 us
    sub x1, other arithmetic, prepared(): block - jnp.where(on_diagonal, jnp.float32(center), jnp.float32(0.0))  1.57 us
  transfers between devices with their start and end apart: 20, of which 12 were waited for; matrix products, arithmetic and copies ran while one was open for 15% of the time, Pallas kernels for 0%

profile of v2, /device:TPU:0, one launch (start us, length us, event | category | flops | bytes accessed | tf_op | source)
XLA Modules:
  0.0 70.5 jit_solution(13119064146126929471)
XLA Ops:
  1.5 2.6 %collective-permute-start.3 = (f32[96,128]{1,0:T(8,128)S(1)}, f32[96,128]{1,0:T(8,128)S(1)}, u32[]{:S(2)}, u32[]{:S(2)}) collective-permute-start(f32[96,128]{1,0:T(8,128)S(1)} %get-tuple-element.29), channel_id=1, source_target_pairs={{0,3},{1,2},{2,1},{3,0},{4,7},{5,6},{6,5},{7,4},{8,11},{9,10},{10,... | collective-permute-start | bytes 147464 | tf_op jit(solution)/shard_map/ppermute | solution.py:40
  4.5 1.6 %select_subtract_fusion.1 = (f32[192,1536]{1,0:T(8,128)S(1)}, f32[192,1536]{1,0:T(8,128)S(1)}) fusion(f32[192,1536]{1,0:T(8,128)} %param.2, s32[1536]{0:T(1024)S(1)} %iota_add_fusion, s32[192]{0:T(256)S(1)} %iota_add_fusion.2, f32[192,1536]{1,0:T(8,128)S(1)} %collective-permute-done, s32[192]{0:T(256)S(1)} %iota_add_fusion.1), kind=kLoop, calls=%fused_computation.4 | loop fusion | flops 1769472 | bytes 4726272 | tf_op jit(solution)/shard_map/sub | solution.py:49
  7.1 1.7 %collective-permute-start.12 = (f32[96,128]{1,0:T(8,128)S(1)}, f32[96,128]{1,0:T(8,128)S(1)}, u32[]{:S(2)}, u32[]{:S(2)}) collective-permute-start(f32[96,128]{1,0:T(8,128)S(1)} %get-tuple-element.10), channel_id=1, source_target_pairs={{0,3},{1,2},{2,1},{3,0},{4,7},{5,6},{6,5},{7,4},{8,11},{9,10},{10,... | collective-permute-start | bytes 147464 | tf_op jit(solution)/shard_map/ppermute | solution.py:40
  10.3 1.7 %collective-permute-start.4 = (f32[768,128]{1,0:T(8,128)S(1)}, f32[768,128]{1,0:T(8,128)S(1)}, u32[]{:S(2)}, u32[]{:S(2)}) collective-permute-start(f32[768,128]{1,0:T(8,128)S(1)} %fusion.3), channel_id=1, source_target_pairs={{0,4},{1,5},{2,10},{3,11},{4,0},{5,1},{6,14},{7,15},{8,12},{9,13},... | collective-permute-start | bytes 1179656 | tf_op jit(solution)/shard_map/ppermute | solution.py:40
  14.1 1.6 %collective-permute-start.13 = (f32[768,128]{1,0:T(8,128)S(1)}, f32[768,128]{1,0:T(8,128)S(1)}, u32[]{:S(2)}, u32[]{:S(2)}) collective-permute-start(f32[768,128]{1,0:T(8,128)S(1)} %fusion.1), channel_id=1, source_target_pairs={{0,4},{1,5},{2,10},{3,11},{4,0},{5,1},{6,14},{7,15},{8,12},{9,13},... | collective-permute-start | bytes 1179656 | tf_op jit(solution)/shard_map/ppermute | solution.py:40
  16.3 1.9 %collective-permute-done.4 = f32[768,128]{1,0:T(8,128)S(1)} collective-permute-done((f32[768,128]{1,0:T(8,128)S(1)}, f32[768,128]{1,0:T(8,128)S(1)}, u32[]{:S(2)}, u32[]{:S(2)}) %collective-permute-start.4) | collective-permute-done | bytes 393248 | tf_op jit(solution)/shard_map/ppermute | solution.py:40
  18.9 1.8 %collective-permute-start.5 = (f32[384,128]{1,0:T(8,128)S(1)}, f32[384,128]{1,0:T(8,128)S(1)}, u32[]{:S(2)}, u32[]{:S(2)}) collective-permute-start(f32[384,128]{1,0:T(8,128)S(1)} %convolution_add_fusion), channel_id=1, source_target_pairs={{0,8},{1,9},{2,6},{3,7},{4,12},{5,13},{6,2},{7,3},{8,0},{9,1},{10,... | collective-permute-start | bytes 589832 | tf_op jit(solution)/shard_map/ppermute | solution.py:40
  20.7 3.5 %collective-permute-done.13 = f32[768,128]{1,0:T(8,128)S(1)} collective-permute-done((f32[768,128]{1,0:T(8,128)S(1)}, f32[768,128]{1,0:T(8,128)S(1)}, u32[]{:S(2)}, u32[]{:S(2)}) %collective-permute-start.13) | collective-permute-done | bytes 393248 | tf_op jit(solution)/shard_map/ppermute | solution.py:40
  24.8 1.8 %collective-permute-start.14 = (f32[384,128]{1,0:T(8,128)S(1)}, f32[384,128]{1,0:T(8,128)S(1)}, u32[]{:S(2)}, u32[]{:S(2)}) collective-permute-start(f32[384,128]{1,0:T(8,128)S(1)} %slice_add_fusion), channel_id=1, source_target_pairs={{0,8},{1,9},{2,6},{3,7},{4,12},{5,13},{6,2},{7,3},{8,0},{9,1},{10,... | collective-permute-start | bytes 589832 | tf_op jit(solution)/shard_map/ppermute | solution.py:40
  27.3 2.7 %collective-permute-start.6 = (f32[384,128]{1,0:T(8,128)S(1)}, f32[384,128]{1,0:T(8,128)S(1)}, u32[]{:S(2)}, u32[]{:S(2)}) collective-permute-start(f32[384,128]{1,0:T(8,128)S(1)} %fusion), channel_id=1, source_target_pairs={{0,16},{1,17},{2,18},{3,19},{4,20},{5,21},{6,22},{7,23},{8,24},{9,... | collective-permute-start | bytes 589832 | tf_op jit(solution)/shard_map/ppermute | solution.py:40
  30.0 2.6 %collective-permute-done.14 = f32[384,128]{1,0:T(8,128)S(1)} collective-permute-done((f32[384,128]{1,0:T(8,128)S(1)}, f32[384,128]{1,0:T(8,128)S(1)}, u32[]{:S(2)}, u32[]{:S(2)}) %collective-permute-start.14) | collective-permute-done | bytes 196640 | tf_op jit(solution)/shard_map/ppermute | solution.py:40
  32.6 2.9 %collective-permute-start.15 = (f32[384,128]{1,0:T(8,128)S(1)}, f32[384,128]{1,0:T(8,128)S(1)}, u32[]{:S(2)}, u32[]{:S(2)}) collective-permute-start(f32[384,128]{1,0:T(8,128)S(1)} %fusion.17), channel_id=1, source_target_pairs={{0,16},{1,17},{2,18},{3,19},{4,20},{5,21},{6,22},{7,23},{8,24},{9,... | collective-permute-start | bytes 589832 | tf_op jit(solution)/shard_map/ppermute | solution.py:40
  35.5 7.9 %collective-permute-done.6 = f32[384,128]{1,0:T(8,128)S(1)} collective-permute-done((f32[384,128]{1,0:T(8,128)S(1)}, f32[384,128]{1,0:T(8,128)S(1)}, u32[]{:S(2)}, u32[]{:S(2)}) %collective-permute-start.6) | collective-permute-done | bytes 196640 | tf_op jit(solution)/shard_map/ppermute | solution.py:40
  43.5 2.4 %collective-permute-done.15 = f32[384,128]{1,0:T(8,128)S(1)} collective-permute-done((f32[384,128]{1,0:T(8,128)S(1)}, f32[384,128]{1,0:T(8,128)S(1)}, u32[]{:S(2)}, u32[]{:S(2)}) %collective-permute-start.15) | collective-permute-done | bytes 196640 | tf_op jit(solution)/shard_map/ppermute | solution.py:40
  46.6 3.2 %collective-permute-done.7 = f32[384,128]{1,0:T(8,128)S(1)} collective-permute-done((f32[384,128]{1,0:T(8,128)S(1)}, f32[384,128]{1,0:T(8,128)S(1)}, u32[]{:S(2)}, u32[]{:S(2)}) %collective-permute-start.7) | collective-permute-done | bytes 196640 | tf_op jit(solution)/shard_map/ppermute | solution.py:40
  49.8 2.7 %collective-permute-start.8 = (f32[768,128]{1,0:T(8,128)S(1)}, f32[768,128]{1,0:T(8,128)S(1)}, u32[]{:S(2)}, u32[]{:S(2)}) collective-permute-start(f32[768,128]{1,0:T(8,128)S(1)} %pad_maximum_fusion.4), channel_id=1, source_target_pairs={{0,4},{1,5},{2,10},{3,11},{4,0},{5,1},{6,14},{7,15},{8,12},{9,13},... | collective-permute-start | bytes 1179656 | tf_op jit(solution)/shard_map/ppermute | solution.py:40
  52.6 1.4 %collective-permute-done.16 = f32[384,128]{1,0:T(8,128)S(1)} collective-permute-done((f32[384,128]{1,0:T(8,128)S(1)}, f32[384,128]{1,0:T(8,128)S(1)}, u32[]{:S(2)}, u32[]{:S(2)}) %collective-permute-start.16) | collective-permute-done | bytes 196640 | tf_op jit(solution)/shard_map/ppermute | solution.py:40
  54.0 2.7 %collective-permute-start.17 = (f32[768,128]{1,0:T(8,128)S(1)}, f32[768,128]{1,0:T(8,128)S(1)}, u32[]{:S(2)}, u32[]{:S(2)}) collective-permute-start(f32[768,128]{1,0:T(8,128)S(1)} %pad_maximum_fusion.5), channel_id=1, source_target_pairs={{0,4},{1,5},{2,10},{3,11},{4,0},{5,1},{6,14},{7,15},{8,12},{9,13},... | collective-permute-start | bytes 1179656 | tf_op jit(solution)/shard_map/ppermute | solution.py:40
  56.8 1.5 %collective-permute-done.8 = f32[768,128]{1,0:T(8,128)S(1)} collective-permute-done((f32[768,128]{1,0:T(8,128)S(1)}, f32[768,128]{1,0:T(8,128)S(1)}, u32[]{:S(2)}, u32[]{:S(2)}) %collective-permute-start.8) | collective-permute-done | bytes 393248 | tf_op jit(solution)/shard_map/ppermute | solution.py:40
  59.4 1.6 %collective-permute-start.9 = (f32[192,128]{1,0:T(8,128)S(1)}, f32[192,128]{1,0:T(8,128)S(1)}, u32[]{:S(2)}, u32[]{:S(2)}) collective-permute-start(f32[192,128]{1,0:T(8,128)S(1)} %slice.61), channel_id=1, source_target_pairs={{0,1},{1,0},{2,3},{3,2},{4,5},{5,4},{6,7},{7,6},{8,9},{9,8},{10,11... | collective-permute-start | bytes 294920 | tf_op jit(solution)/shard_map/ppermute | solution.py:40
  61.0 1.5 %collective-permute-done.17 = f32[768,128]{1,0:T(8,128)S(1)} collective-permute-done((f32[768,128]{1,0:T(8,128)S(1)}, f32[768,128]{1,0:T(8,128)S(1)}, u32[]{:S(2)}, u32[]{:S(2)}) %collective-permute-start.17) | collective-permute-done | bytes 393248 | tf_op jit(solution)/shard_map/ppermute | solution.py:40
  63.7 1.6 %collective-permute-start.18 = (f32[192,128]{1,0:T(8,128)S(1)}, f32[192,128]{1,0:T(8,128)S(1)}, u32[]{:S(2)}, u32[]{:S(2)}) collective-permute-start(f32[192,128]{1,0:T(8,128)S(1)} %slice.65), channel_id=1, source_target_pairs={{0,1},{1,0},{2,3},{3,2},{4,5},{5,4},{6,7},{7,6},{8,9},{9,8},{10,11... | collective-permute-start | bytes 294920 | tf_op jit(solution)/shard_map/ppermute | solution.py:40
  65.3 3.1 %collective-permute-done.18 = f32[192,128]{1,0:T(8,128)S(1)} collective-permute-done((f32[192,128]{1,0:T(8,128)S(1)}, f32[192,128]{1,0:T(8,128)S(1)}, u32[]{:S(2)}, u32[]{:S(2)}) %collective-permute-start.18) | collective-permute-done | bytes 98336 | tf_op jit(solution)/shard_map/ppermute | solution.py:40
  68.5 1.3 %collective-permute-done.19 = f32[96,256]{1,0:T(8,128)S(1)} collective-permute-done((f32[96,256]{1,0:T(8,128)S(1)}, f32[96,256]{1,0:T(8,128)S(1)}, u32[]{:S(2)}, u32[]{:S(2)}) %collective-permute-start.19) | collective-permute-done | bytes 98336 | tf_op jit(solution)/shard_map/ppermute | solution.py:40
  (51 shorter events, 13.1 us)
Async XLA Ops:
  0.0 4.5 %collective-permute-start = (f32[192,1536]{1,0:T(8,128)}, f32[192,1536]{1,0:T(8,128)S(1)}, u32[]{:S(2)}, u32[]{:S(2)}) collective-permute-start(f32[192,1536]{1,0:T(8,128)} %param.2), channel_id=1, source_target_pairs={{0,2},{1,3},{2,0},{3,1},{4,6},{5,7},{6,4},{7,5},{8,10},{9,11},{10,... | collective-permute-start | bytes 3538952 | tf_op jit(solution)/shard_map/ppermute | solution.py:40
  1.3 7.4 %collective-permute-start.1 = (f32[96,128]{1,0:T(8,128)S(1)}, f32[96,128]{1,0:T(8,128)S(1)}, u32[]{:S(2)}, u32[]{:S(2)}) collective-permute-start(f32[96,128]{1,0:T(8,128)S(1)} %get-tuple-element.29), channel_id=1, source_target_pairs={{0,2},{1,3},{2,0},{3,1},{4,6},{5,7},{6,4},{7,5},{8,10},{9,11},{10,... | collective-permute-start | bytes 147464 | tf_op jit(solution)/shard_map/ppermute | solution.py:40
  1.5 7.7 %collective-permute-start.3 = (f32[96,128]{1,0:T(8,128)S(1)}, f32[96,128]{1,0:T(8,128)S(1)}, u32[]{:S(2)}, u32[]{:S(2)}) collective-permute-start(f32[96,128]{1,0:T(8,128)S(1)} %get-tuple-element.29), channel_id=1, source_target_pairs={{0,3},{1,2},{2,1},{3,0},{4,7},{5,6},{6,5},{7,4},{8,11},{9,10},{10,... | collective-permute-start | bytes 147464 | tf_op jit(solution)/shard_map/ppermute | solution.py:40
  4.1 5.1 %collective-permute-start.2 = (f32[96,128]{1,0:T(8,128)S(1)}, f32[96,128]{1,0:T(8,128)S(1)}, u32[]{:S(2)}, u32[]{:S(2)}) collective-permute-start(f32[96,128]{1,0:T(8,128)S(1)} %get-tuple-element.27), channel_id=1, source_target_pairs={{0,1},{1,0},{2,3},{3,2},{4,5},{5,4},{6,7},{7,6},{8,9},{9,8},{10,11... | collective-permute-start | bytes 147464 | tf_op jit(solution)/shard_map/ppermute | solution.py:40
  6.9 5.2 %collective-permute-start.10 = (f32[96,128]{1,0:T(8,128)S(1)}, f32[96,128]{1,0:T(8,128)S(1)}, u32[]{:S(2)}, u32[]{:S(2)}) collective-permute-start(f32[96,128]{1,0:T(8,128)S(1)} %get-tuple-element.10), channel_id=1, source_target_pairs={{0,2},{1,3},{2,0},{3,1},{4,6},{5,7},{6,4},{7,5},{8,10},{9,11},{10,... | collective-permute-start | bytes 147464 | tf_op jit(solution)/shard_map/ppermute | solution.py:40
  7.1 5.8 %collective-permute-start.12 = (f32[96,128]{1,0:T(8,128)S(1)}, f32[96,128]{1,0:T(8,128)S(1)}, u32[]{:S(2)}, u32[]{:S(2)}) collective-permute-start(f32[96,128]{1,0:T(8,128)S(1)} %get-tuple-element.10), channel_id=1, source_target_pairs={{0,3},{1,2},{2,1},{3,0},{4,7},{5,6},{6,5},{7,4},{8,11},{9,10},{10,... | collective-permute-start | bytes 147464 | tf_op jit(solution)/shard_map/ppermute | solution.py:40
  8.8 4.1 %collective-permute-start.11 = (f32[96,128]{1,0:T(8,128)S(1)}, f32[96,128]{1,0:T(8,128)S(1)}, u32[]{:S(2)}, u32[]{:S(2)}) collective-permute-start(f32[96,128]{1,0:T(8,128)S(1)} %get-tuple-element.9), channel_id=1, source_target_pairs={{0,1},{1,0},{2,3},{3,2},{4,5},{5,4},{6,7},{7,6},{8,9},{9,8},{10,11... | collective-permute-start | bytes 147464 | tf_op jit(solution)/shard_map/ppermute | solution.py:40
  10.3 7.8 %collective-permute-start.4 = (f32[768,128]{1,0:T(8,128)S(1)}, f32[768,128]{1,0:T(8,128)S(1)}, u32[]{:S(2)}, u32[]{:S(2)}) collective-permute-start(f32[768,128]{1,0:T(8,128)S(1)} %fusion.3), channel_id=1, source_target_pairs={{0,4},{1,5},{2,10},{3,11},{4,0},{5,1},{6,14},{7,15},{8,12},{9,13},... | collective-permute-start | bytes 1179656 | tf_op jit(solution)/shard_map/ppermute | solution.py:40
  14.1 10.1 %collective-permute-start.13 = (f32[768,128]{1,0:T(8,128)S(1)}, f32[768,128]{1,0:T(8,128)S(1)}, u32[]{:S(2)}, u32[]{:S(2)}) collective-permute-start(f32[768,128]{1,0:T(8,128)S(1)} %fusion.1), channel_id=1, source_target_pairs={{0,4},{1,5},{2,10},{3,11},{4,0},{5,1},{6,14},{7,15},{8,12},{9,13},... | collective-permute-start | bytes 1179656 | tf_op jit(solution)/shard_map/ppermute | solution.py:40
  18.9 7.8 %collective-permute-start.5 = (f32[384,128]{1,0:T(8,128)S(1)}, f32[384,128]{1,0:T(8,128)S(1)}, u32[]{:S(2)}, u32[]{:S(2)}) collective-permute-start(f32[384,128]{1,0:T(8,128)S(1)} %convolution_add_fusion), channel_id=1, source_target_pairs={{0,8},{1,9},{2,6},{3,7},{4,12},{5,13},{6,2},{7,3},{8,0},{9,1},{10,... | collective-permute-start | bytes 589832 | tf_op jit(solution)/shard_map/ppermute | solution.py:40
  24.8 7.7 %collective-permute-start.14 = (f32[384,128]{1,0:T(8,128)S(1)}, f32[384,128]{1,0:T(8,128)S(1)}, u32[]{:S(2)}, u32[]{:S(2)}) collective-permute-start(f32[384,128]{1,0:T(8,128)S(1)} %slice_add_fusion), channel_id=1, source_target_pairs={{0,8},{1,9},{2,6},{3,7},{4,12},{5,13},{6,2},{7,3},{8,0},{9,1},{10,... | collective-permute-start | bytes 589832 | tf_op jit(solution)/shard_map/ppermute | solution.py:40
  27.3 16.0 %collective-permute-start.6 = (f32[384,128]{1,0:T(8,128)S(1)}, f32[384,128]{1,0:T(8,128)S(1)}, u32[]{:S(2)}, u32[]{:S(2)}) collective-permute-start(f32[384,128]{1,0:T(8,128)S(1)} %fusion), channel_id=1, source_target_pairs={{0,16},{1,17},{2,18},{3,19},{4,20},{5,21},{6,22},{7,23},{8,24},{9,... | collective-permute-start | bytes 589832 | tf_op jit(solution)/shard_map/ppermute | solution.py:40
  32.6 13.2 %collective-permute-start.15 = (f32[384,128]{1,0:T(8,128)S(1)}, f32[384,128]{1,0:T(8,128)S(1)}, u32[]{:S(2)}, u32[]{:S(2)}) collective-permute-start(f32[384,128]{1,0:T(8,128)S(1)} %fusion.17), channel_id=1, source_target_pairs={{0,16},{1,17},{2,18},{3,19},{4,20},{5,21},{6,22},{7,23},{8,24},{9,... | collective-permute-start | bytes 589832 | tf_op jit(solution)/shard_map/ppermute | solution.py:40
  43.4 6.4 %collective-permute-start.7 = (f32[384,128]{1,0:T(8,128)S(1)}, f32[384,128]{1,0:T(8,128)S(1)}, u32[]{:S(2)}, u32[]{:S(2)}) collective-permute-start(f32[384,128]{1,0:T(8,128)S(1)} %add_multiply_fusion.1), channel_id=1, source_target_pairs={{0,8},{1,9},{2,6},{3,7},{4,12},{5,13},{6,2},{7,3},{8,0},{9,1},{10,... | collective-permute-start | bytes 589832 | tf_op jit(solution)/shard_map/ppermute | solution.py:40
  45.9 8.1 %collective-permute-start.16 = (f32[384,128]{1,0:T(8,128)S(1)}, f32[384,128]{1,0:T(8,128)S(1)}, u32[]{:S(2)}, u32[]{:S(2)}) collective-permute-start(f32[384,128]{1,0:T(8,128)S(1)} %add_multiply_fusion), channel_id=1, source_target_pairs={{0,8},{1,9},{2,6},{3,7},{4,12},{5,13},{6,2},{7,3},{8,0},{9,1},{10,... | collective-permute-start | bytes 589832 | tf_op jit(solution)/shard_map/ppermute | solution.py:40
  49.8 8.5 %collective-permute-start.8 = (f32[768,128]{1,0:T(8,128)S(1)}, f32[768,128]{1,0:T(8,128)S(1)}, u32[]{:S(2)}, u32[]{:S(2)}) collective-permute-start(f32[768,128]{1,0:T(8,128)S(1)} %pad_maximum_fusion.4), channel_id=1, source_target_pairs={{0,4},{1,5},{2,10},{3,11},{4,0},{5,1},{6,14},{7,15},{8,12},{9,13},... | collective-permute-start | bytes 1179656 | tf_op jit(solution)/shard_map/ppermute | solution.py:40
  54.0 8.5 %collective-permute-start.17 = (f32[768,128]{1,0:T(8,128)S(1)}, f32[768,128]{1,0:T(8,128)S(1)}, u32[]{:S(2)}, u32[]{:S(2)}) collective-permute-start(f32[768,128]{1,0:T(8,128)S(1)} %pad_maximum_fusion.5), channel_id=1, source_target_pairs={{0,4},{1,5},{2,10},{3,11},{4,0},{5,1},{6,14},{7,15},{8,12},{9,13},... | collective-permute-start | bytes 1179656 | tf_op jit(solution)/shard_map/ppermute | solution.py:40
  59.4 5.8 %collective-permute-start.9 = (f32[192,128]{1,0:T(8,128)S(1)}, f32[192,128]{1,0:T(8,128)S(1)}, u32[]{:S(2)}, u32[]{:S(2)}) collective-permute-start(f32[192,128]{1,0:T(8,128)S(1)} %slice.61), channel_id=1, source_target_pairs={{0,1},{1,0},{2,3},{3,2},{4,5},{5,4},{6,7},{7,6},{8,9},{9,8},{10,11... | collective-permute-start | bytes 294920 | tf_op jit(solution)/shard_map/ppermute | solution.py:40
  63.7 6.1 %copy-start = (f32[96,512]{1,0:T(8,128)S(1)}, f32[96,512]{1,0:T(8,128)}, u32[]{:S(2)}) copy-start(f32[96,512]{1,0:T(8,128)} %param.3) | copy-start | bytes 589828
  63.7 4.7 %collective-permute-start.18 = (f32[192,128]{1,0:T(8,128)S(1)}, f32[192,128]{1,0:T(8,128)S(1)}, u32[]{:S(2)}, u32[]{:S(2)}) collective-permute-start(f32[192,128]{1,0:T(8,128)S(1)} %slice.65), channel_id=1, source_target_pairs={{0,1},{1,0},{2,3},{3,2},{4,5},{5,4},{6,7},{7,6},{8,9},{9,8},{10,11... | collective-permute-start | bytes 294920 | tf_op jit(solution)/shard_map/ppermute | solution.py:40
  68.4 1.4 %collective-permute-start.19 = (f32[96,256]{1,0:T(8,128)S(1)}, f32[96,256]{1,0:T(8,128)S(1)}, u32[]{:S(2)}, u32[]{:S(2)}) collective-permute-start(f32[96,256]{1,0:T(8,128)S(1)} %pad_maximum_fusion.8), channel_id=1, source_target_pairs={{0,2},{1,3},{2,0},{3,1},{4,6},{5,7},{6,4},{7,5},{8,10},{9,11},{10,... | collective-permute-start | bytes 294920 | tf_op jit(solution)/shard_map/ppermute | solution.py:40

commit v3 on v2

--- a/solution.py
+++ b/solution.py
@@ -72,18 +72,19 @@
     for chunk in chunks:
         if results:
             chunk = after(chunk, given)
-        given = product(matrix[:, 2 * quarter :], chunk, 0)
-        received = exchange(given, (2, 4), 0)
-        passed = product(matrix[:, quarter : 2 * quarter], chunk, 0) + received[quarter:]
-        total = product(matrix[:, :quarter], chunk, 0) + received[:quarter]
-        total = total + exchange(passed, (4, 2), 0)
+        given = product(matrix[:, quarter:], chunk, 0)
+        sent = [given[i * quarter : (i + 1) * quarter] for i in (1, 0, 2)]
+        MASKS = [((4, 2), (2, 4), (6, 6))[i] for i in (1, 0, 2)]
+        received = [exchange(block, masks, 0) for block, masks in zip(sent, MASKS)]
+        total = product(matrix[:, :quarter], chunk, 0)
+        for term in received:
+            total = total + term
         mask = 8
         while mask < rows:
             total = total + exchange(total, mask, 0)
             mask *= 2
         fresh = total * (1.0 / half_width)
-        fresh = jnp.concatenate([fresh, exchange(fresh, (4, 2), 0)], axis=0)
-        fresh = jnp.concatenate([fresh, exchange(fresh, (2, 4), 0)], axis=0)
+        fresh = jnp.concatenate([fresh, *[exchange(fresh, masks, 0) for masks in ((4, 2), (2, 4), (6, 6))]], axis=0)
         if results:
             fresh = after(fresh, partial)
         partial = product(matrix, fresh, 1)

time: 70.8 us -> 67.8 us (0.958)
  waiting for transfers between devices: 31.1 us -> 27.1 us
  starting transfers between devices: 27.7 us -> 29.3 us
    ppermute x20 -> x24, waiting for transfers between devices: 31.1 us -> 27.1 us  [exchange(): return lax.ppermute(block, ('row', 'col'), pairs)]
    ppermute x20 -> x24, starting transfers between devices: 27.7 us -> 29.3 us  [exchange(): return lax.ppermute(block, ('row', 'col'), pairs)]
    dot_general x8 -> x6, matrix products: 7.18 us -> 6.69 us  [product(): lax.dot_general(left, right, (((left_dim,), (0,)), ((), ())), precision=l...]
  transfers between devices with their start and end apart: 20 -> 24, of which waited for: 12 -> 11; matrix products, arithmetic and copies ran while one was open for 15% -> 15% of each run, Pallas kernels for 0% -> 0%
where the time goes in v3:
time: 67.8 us; the launch traced here: 67.6 us
  starting transfers between devices  29.3 us (43%)
  waiting for transfers between devices  27.1 us (40%)
  matrix products  6.69 us (10%)
  other arithmetic  2.87 us (4%)
  local copies, waits for them, and re-layouts  1.43 us (2%)
    ppermute x24, starting transfers between devices, exchange(): return lax.ppermute(block, ('row', 'col'), pairs)  29.3 us
    ppermute x24, waiting for transfers between devices, exchange(): return lax.ppermute(block, ('row', 'col'), pairs)  27.1 us
    dot_general x6, matrix products, product(): lax.dot_general(left, right, (((left_dim,), (0,)), ((), ())), precision=l...  6.69 us
    sub x1, other arithmetic, prepared(): block - jnp.where(on_diagonal, jnp.float32(center), jnp.float32(0.0))  1.57 us
  transfers between devices with their start and end apart: 24, of which 11 were waited for; matrix products, arithmetic and copies ran while one was open for 15% of the time, Pallas kernels for 0%

profile of v3, /device:TPU:0, one launch (start us, length us, event | category | flops | bytes accessed | tf_op | source)
XLA Modules:
  0.0 67.6 jit_solution(17696253415200269724)
XLA Ops:
  1.5 2.6 %collective-permute-start.3 = (f32[96,128]{1,0:T(8,128)S(1)}, f32[96,128]{1,0:T(8,128)S(1)}, u32[]{:S(2)}, u32[]{:S(2)}) collective-permute-start(f32[96,128]{1,0:T(8,128)S(1)} %get-tuple-element.35), channel_id=1, source_target_pairs={{0,3},{1,2},{2,1},{3,0},{4,7},{5,6},{6,5},{7,4},{8,11},{9,10},{10,... | collective-permute-start | bytes 147464 | tf_op jit(solution)/shard_map/ppermute | solution.py:40
  4.5 1.6 %select_subtract_fusion.1 = (f32[192,1536]{1,0:T(8,128)S(1)}, f32[192,1536]{1,0:T(8,128)S(1)}) fusion(f32[192,1536]{1,0:T(8,128)} %param.2, s32[1536]{0:T(1024)S(1)} %iota_add_fusion, s32[192]{0:T(256)S(1)} %iota_add_fusion.2, f32[192,1536]{1,0:T(8,128)S(1)} %collective-permute-done, s32[192]{0:T(256)S(1)} %iota_add_fusion.1), kind=kLoop, calls=%fused_computation.8 | loop fusion | flops 1769472 | bytes 4726272 | tf_op jit(solution)/shard_map/sub | solution.py:49
  7.1 1.7 %collective-permute-start.14 = (f32[96,128]{1,0:T(8,128)S(1)}, f32[96,128]{1,0:T(8,128)S(1)}, u32[]{:S(2)}, u32[]{:S(2)}) collective-permute-start(f32[96,128]{1,0:T(8,128)S(1)} %get-tuple-element.10), channel_id=1, source_target_pairs={{0,3},{1,2},{2,1},{3,0},{4,7},{5,6},{6,5},{7,4},{8,11},{9,10},{10,... | collective-permute-start | bytes 147464 | tf_op jit(solution)/shard_map/ppermute | solution.py:40
  9.2 1.6 %fusion.2 = f32[1152,128]{1,0:T(8,128)S(1)} fusion(f32[384,1536]{1,0:T(8,128)S(1)} %pad_maximum_fusion, f32[96,128]{1,0:T(8,128)S(1)} %collective-permute-done.3, f32[96,128]{1,0:T(8,128)S(1)} %collective-permute-done.2, f32[96,128]{1,0:T(8,128)S(1)} %collective-permute-done.1, f32[96,128]{1,0:T(8,128)S(1)} %get-tuple-element.33), kind=kOutput, calls=%fused_computation.3 | convolution fusion | flops 339886080 | bytes 2555904 | tf_op jit(solution)/shard_map/dot_general | solution.py:14
  10.8 1.7 %collective-permute-start.4 = (f32[384,128]{1,0:T(8,128)S(1)}, f32[384,128]{1,0:T(8,128)S(1)}, u32[]{:S(2)}, u32[]{:S(2)}) collective-permute-start(f32[384,128]{1,0:T(8,128)S(1)} %get-tuple-element.25), channel_id=1, source_target_pairs={{0,4},{1,5},{2,10},{3,11},{4,0},{5,1},{6,14},{7,15},{8,12},{9,13},... | collective-permute-start | bytes 589832 | tf_op jit(solution)/shard_map/ppermute | solution.py:40
  12.6 1.6 %collective-permute-start.5 = (f32[384,128]{1,0:T(8,128)S(1)}, f32[384,128]{1,0:T(8,128)S(1)}, u32[]{:S(2)}, u32[]{:S(2)}) collective-permute-start(f32[384,128]{1,0:T(8,128)S(1)} %get-tuple-element.27), channel_id=1, source_target_pairs={{0,8},{1,9},{2,6},{3,7},{4,12},{5,13},{6,2},{7,3},{8,0},{9,1},{10,... | collective-permute-start | bytes 589832 | tf_op jit(solution)/shard_map/ppermute | solution.py:40
  14.4 1.6 %fusion = f32[1152,128]{1,0:T(8,128)S(1)} fusion(f32[384,128]{1,0:T(8,128)S(1)} %pad_maximum_fusion.5, f32[384,1536]{1,0:T(8,128)S(1)} %pad_maximum_fusion), kind=kOutput, calls=%fused_computation.1 | convolution fusion | flops 339738624 | bytes 2555904 | tf_op jit(solution)/shard_map/dot_general | solution.py:14
  16.0 1.7 %collective-permute-start.15 = (f32[384,128]{1,0:T(8,128)S(1)}, f32[384,128]{1,0:T(8,128)S(1)}, u32[]{:S(2)}, u32[]{:S(2)}) collective-permute-start(f32[384,128]{1,0:T(8,128)S(1)} %get-tuple-element.28), channel_id=1, source_target_pairs={{0,4},{1,5},{2,10},{3,11},{4,0},{5,1},{6,14},{7,15},{8,12},{9,13},... | collective-permute-start | bytes 589832 | tf_op jit(solution)/shard_map/ppermute | solution.py:40
  17.8 1.6 %collective-permute-start.16 = (f32[384,128]{1,0:T(8,128)S(1)}, f32[384,128]{1,0:T(8,128)S(1)}, u32[]{:S(2)}, u32[]{:S(2)}) collective-permute-start(f32[384,128]{1,0:T(8,128)S(1)} %get-tuple-element.30), channel_id=1, source_target_pairs={{0,8},{1,9},{2,6},{3,7},{4,12},{5,13},{6,2},{7,3},{8,0},{9,1},{10,... | collective-permute-start | bytes 589832 | tf_op jit(solution)/shard_map/ppermute | solution.py:40
  19.6 4.3 %collective-permute-start.17 = (f32[384,128]{1,0:T(8,128)S(1)}, f32[384,128]{1,0:T(8,128)S(1)}, u32[]{:S(2)}, u32[]{:S(2)}) collective-permute-start(f32[384,128]{1,0:T(8,128)S(1)} %get-tuple-element.29), channel_id=1, source_target_pairs={{0,12},{1,13},{2,14},{3,15},{4,8},{5,9},{6,10},{7,11},{8,4},{9,5},... | collective-permute-start | bytes 589832 | tf_op jit(solution)/shard_map/ppermute | solution.py:40
  25.1 2.8 %collective-permute-start.7 = (f32[384,128]{1,0:T(8,128)S(1)}, f32[384,128]{1,0:T(8,128)S(1)}, u32[]{:S(2)}, u32[]{:S(2)}) collective-permute-start(f32[384,128]{1,0:T(8,128)S(1)} %fusion.7), channel_id=1, source_target_pairs={{0,16},{1,17},{2,18},{3,19},{4,20},{5,21},{6,22},{7,23},{8,24},{9,... | collective-permute-start | bytes 589832 | tf_op jit(solution)/shard_map/ppermute | solution.py:40
  27.9 4.9 %collective-permute-done.16 = f32[384,128]{1,0:T(8,128)S(1)} collective-permute-done((f32[384,128]{1,0:T(8,128)S(1)}, f32[384,128]{1,0:T(8,128)S(1)}, u32[]{:S(2)}, u32[]{:S(2)}) %collective-permute-start.16) | collective-permute-done | bytes 196640 | tf_op jit(solution)/shard_map/ppermute | solution.py:40
  32.8 2.8 %collective-permute-done.17 = f32[384,128]{1,0:T(8,128)S(1)} collective-permute-done((f32[384,128]{1,0:T(8,128)S(1)}, f32[384,128]{1,0:T(8,128)S(1)}, u32[]{:S(2)}, u32[]{:S(2)}) %collective-permute-start.17) | collective-permute-done | bytes 196640 | tf_op jit(solution)/shard_map/ppermute | solution.py:40
  36.4 4.6 %collective-permute-start.10 = (f32[384,128]{1,0:T(8,128)S(1)}, f32[384,128]{1,0:T(8,128)S(1)}, u32[]{:S(2)}, u32[]{:S(2)}) collective-permute-start(f32[384,128]{1,0:T(8,128)S(1)} %add_multiply_fusion.1), channel_id=1, source_target_pairs={{0,12},{1,13},{2,14},{3,15},{4,8},{5,9},{6,10},{7,11},{8,4},{9,5},... | collective-permute-start | bytes 589832 | tf_op jit(solution)/shard_map/ppermute | solution.py:40
  41.7 4.8 %collective-permute-done.18 = f32[384,128]{1,0:T(8,128)S(1)} collective-permute-done((f32[384,128]{1,0:T(8,128)S(1)}, f32[384,128]{1,0:T(8,128)S(1)}, u32[]{:S(2)}, u32[]{:S(2)}) %collective-permute-start.18) | collective-permute-done | bytes 196640 | tf_op jit(solution)/shard_map/ppermute | solution.py:40
  46.7 2.3 %collective-permute-done.10 = f32[384,128]{1,0:T(8,128)S(1)} collective-permute-done((f32[384,128]{1,0:T(8,128)S(1)}, f32[384,128]{1,0:T(8,128)S(1)}, u32[]{:S(2)}, u32[]{:S(2)}) %collective-permute-start.10) | collective-permute-done | bytes 196640 | tf_op jit(solution)/shard_map/ppermute | solution.py:40
  50.1 3.1 %collective-permute-done.8 = f32[384,128]{1,0:T(8,128)S(1)} collective-permute-done((f32[384,128]{1,0:T(8,128)S(1)}, f32[384,128]{1,0:T(8,128)S(1)}, u32[]{:S(2)}, u32[]{:S(2)}) %collective-permute-start.8) | collective-permute-done | bytes 196640 | tf_op jit(solution)/shard_map/ppermute | solution.py:40
  54.3 1.6 %collective-permute-start.11 = (f32[192,128]{1,0:T(8,128)S(1)}, f32[192,128]{1,0:T(8,128)S(1)}, u32[]{:S(2)}, u32[]{:S(2)}) collective-permute-start(f32[192,128]{1,0:T(8,128)S(1)} %slice.64), channel_id=1, source_target_pairs={{0,1},{1,0},{2,3},{3,2},{4,5},{5,4},{6,7},{7,6},{8,9},{9,8},{10,11... | collective-permute-start | bytes 294920 | tf_op jit(solution)/shard_map/ppermute | solution.py:40
  55.9 1.5 %collective-permute-done.19 = f32[384,128]{1,0:T(8,128)S(1)} collective-permute-done((f32[384,128]{1,0:T(8,128)S(1)}, f32[384,128]{1,0:T(8,128)S(1)}, u32[]{:S(2)}, u32[]{:S(2)}) %collective-permute-start.19) | collective-permute-done | bytes 196640 | tf_op jit(solution)/shard_map/ppermute | solution.py:40
  57.4 2.2 %collective-permute-done.21 = f32[384,128]{1,0:T(8,128)S(1)} collective-permute-done((f32[384,128]{1,0:T(8,128)S(1)}, f32[384,128]{1,0:T(8,128)S(1)}, u32[]{:S(2)}, u32[]{:S(2)}) %collective-permute-start.21) | collective-permute-done | bytes 196640 | tf_op jit(solution)/shard_map/ppermute | solution.py:40
  59.6 1.1 %fusion.23 = f32[384,128]{1,0:T(8,128)S(1)} fusion(f32[1536,128]{1,0:T(8,128)S(1)} %pad_maximum_fusion.3, f32[96,1536]{1,0:T(8,128)S(1)} %get-tuple-element.16, f32[96,1536]{1,0:T(8,128)S(1)} %get-tuple-element.14, f32[96,1536]{1,0:T(8,128)S(1)} %get-tuple-element.15, f32[96,1536]{1,0:T(8,128)S(1)} %get-tuple-element.13), kind=kOutput, calls=%fused_computation.62 | convolution fusion | flops 454754304 | bytes 3342336 | tf_op jit(solution)/shard_map/dot_general | solution.py:14
  60.8 1.3 %collective-permute-start.22 = (f32[192,128]{1,0:T(8,128)S(1)}, f32[192,128]{1,0:T(8,128)S(1)}, u32[]{:S(2)}, u32[]{:S(2)}) collective-permute-start(f32[192,128]{1,0:T(8,128)S(1)} %slice.69), channel_id=1, source_target_pairs={{0,1},{1,0},{2,3},{3,2},{4,5},{5,4},{6,7},{7,6},{8,9},{9,8},{10,11... | collective-permute-start | bytes 294920 | tf_op jit(solution)/shard_map/ppermute | solution.py:40
  62.1 3.4 %collective-permute-done.22 = f32[192,128]{1,0:T(8,128)S(1)} collective-permute-done((f32[192,128]{1,0:T(8,128)S(1)}, f32[192,128]{1,0:T(8,128)S(1)}, u32[]{:S(2)}, u32[]{:S(2)}) %collective-permute-start.22) | collective-permute-done | bytes 98336 | tf_op jit(solution)/shard_map/ppermute | solution.py:40
  65.6 1.3 %collective-permute-done.23 = f32[96,256]{1,0:T(8,128)S(1)} collective-permute-done((f32[96,256]{1,0:T(8,128)S(1)}, f32[96,256]{1,0:T(8,128)S(1)}, u32[]{:S(2)}, u32[]{:S(2)}) %collective-permute-start.23) | collective-permute-done | bytes 98336 | tf_op jit(solution)/shard_map/ppermute | solution.py:40
  (56 shorter events, 9.6 us)
Async XLA Ops:
  0.0 4.5 %collective-permute-start = (f32[192,1536]{1,0:T(8,128)}, f32[192,1536]{1,0:T(8,128)S(1)}, u32[]{:S(2)}, u32[]{:S(2)}) collective-permute-start(f32[192,1536]{1,0:T(8,128)} %param.2), channel_id=1, source_target_pairs={{0,2},{1,3},{2,0},{3,1},{4,6},{5,7},{6,4},{7,5},{8,10},{9,11},{10,... | collective-permute-start | bytes 3538952 | tf_op jit(solution)/shard_map/ppermute | solution.py:40
  1.3 7.4 %collective-permute-start.1 = (f32[96,128]{1,0:T(8,128)S(1)}, f32[96,128]{1,0:T(8,128)S(1)}, u32[]{:S(2)}, u32[]{:S(2)}) collective-permute-start(f32[96,128]{1,0:T(8,128)S(1)} %get-tuple-element.35), channel_id=1, source_target_pairs={{0,2},{1,3},{2,0},{3,1},{4,6},{5,7},{6,4},{7,5},{8,10},{9,11},{10,... | collective-permute-start | bytes 147464 | tf_op jit(solution)/shard_map/ppermute | solution.py:40
  1.5 7.7 %collective-permute-start.3 = (f32[96,128]{1,0:T(8,128)S(1)}, f32[96,128]{1,0:T(8,128)S(1)}, u32[]{:S(2)}, u32[]{:S(2)}) collective-permute-start(f32[96,128]{1,0:T(8,128)S(1)} %get-tuple-element.35), channel_id=1, source_target_pairs={{0,3},{1,2},{2,1},{3,0},{4,7},{5,6},{6,5},{7,4},{8,11},{9,10},{10,... | collective-permute-start | bytes 147464 | tf_op jit(solution)/shard_map/ppermute | solution.py:40
  4.1 5.1 %collective-permute-start.2 = (f32[96,128]{1,0:T(8,128)S(1)}, f32[96,128]{1,0:T(8,128)S(1)}, u32[]{:S(2)}, u32[]{:S(2)}) collective-permute-start(f32[96,128]{1,0:T(8,128)S(1)} %get-tuple-element.33), channel_id=1, source_target_pairs={{0,1},{1,0},{2,3},{3,2},{4,5},{5,4},{6,7},{7,6},{8,9},{9,8},{10,11... | collective-permute-start | bytes 147464 | tf_op jit(solution)/shard_map/ppermute | solution.py:40
  6.9 7.2 %collective-permute-start.12 = (f32[96,128]{1,0:T(8,128)S(1)}, f32[96,128]{1,0:T(8,128)S(1)}, u32[]{:S(2)}, u32[]{:S(2)}) collective-permute-start(f32[96,128]{1,0:T(8,128)S(1)} %get-tuple-element.10), channel_id=1, source_target_pairs={{0,2},{1,3},{2,0},{3,1},{4,6},{5,7},{6,4},{7,5},{8,10},{9,11},{10,... | collective-permute-start | bytes 147464 | tf_op jit(solution)/shard_map/ppermute | solution.py:40
  7.1 7.3 %collective-permute-start.14 = (f32[96,128]{1,0:T(8,128)S(1)}, f32[96,128]{1,0:T(8,128)S(1)}, u32[]{:S(2)}, u32[]{:S(2)}) collective-permute-start(f32[96,128]{1,0:T(8,128)S(1)} %get-tuple-element.10), channel_id=1, source_target_pairs={{0,3},{1,2},{2,1},{3,0},{4,7},{5,6},{6,5},{7,4},{8,11},{9,10},{10,... | collective-permute-start | bytes 147464 | tf_op jit(solution)/shard_map/ppermute | solution.py:40
  8.8 5.6 %collective-permute-start.13 = (f32[96,128]{1,0:T(8,128)S(1)}, f32[96,128]{1,0:T(8,128)S(1)}, u32[]{:S(2)}, u32[]{:S(2)}) collective-permute-start(f32[96,128]{1,0:T(8,128)S(1)} %get-tuple-element.9), channel_id=1, source_target_pairs={{0,1},{1,0},{2,3},{3,2},{4,5},{5,4},{6,7},{7,6},{8,9},{9,8},{10,11... | collective-permute-start | bytes 147464 | tf_op jit(solution)/shard_map/ppermute | solution.py:40
  10.8 8.8 %collective-permute-start.4 = (f32[384,128]{1,0:T(8,128)S(1)}, f32[384,128]{1,0:T(8,128)S(1)}, u32[]{:S(2)}, u32[]{:S(2)}) collective-permute-start(f32[384,128]{1,0:T(8,128)S(1)} %get-tuple-element.25), channel_id=1, source_target_pairs={{0,4},{1,5},{2,10},{3,11},{4,0},{5,1},{6,14},{7,15},{8,12},{9,13},... | collective-permute-start | bytes 589832 | tf_op jit(solution)/shard_map/ppermute | solution.py:40
  12.6 11.4 %collective-permute-start.5 = (f32[384,128]{1,0:T(8,128)S(1)}, f32[384,128]{1,0:T(8,128)S(1)}, u32[]{:S(2)}, u32[]{:S(2)}) collective-permute-start(f32[384,128]{1,0:T(8,128)S(1)} %get-tuple-element.27), channel_id=1, source_target_pairs={{0,8},{1,9},{2,6},{3,7},{4,12},{5,13},{6,2},{7,3},{8,0},{9,1},{10,... | collective-permute-start | bytes 589832 | tf_op jit(solution)/shard_map/ppermute | solution.py:40
  14.1 10.3 %collective-permute-start.6 = (f32[384,128]{1,0:T(8,128)S(1)}, f32[384,128]{1,0:T(8,128)S(1)}, u32[]{:S(2)}, u32[]{:S(2)}) collective-permute-start(f32[384,128]{1,0:T(8,128)S(1)} %get-tuple-element.26), channel_id=1, source_target_pairs={{0,12},{1,13},{2,14},{3,15},{4,8},{5,9},{6,10},{7,11},{8,4},{9,5},... | collective-permute-start | bytes 589832 | tf_op jit(solution)/shard_map/ppermute | solution.py:40
  16.0 11.9 %collective-permute-start.15 = (f32[384,128]{1,0:T(8,128)S(1)}, f32[384,128]{1,0:T(8,128)S(1)}, u32[]{:S(2)}, u32[]{:S(2)}) collective-permute-start(f32[384,128]{1,0:T(8,128)S(1)} %get-tuple-element.28), channel_id=1, source_target_pairs={{0,4},{1,5},{2,10},{3,11},{4,0},{5,1},{6,14},{7,15},{8,12},{9,13},... | collective-permute-start | bytes 589832 | tf_op jit(solution)/shard_map/ppermute | solution.py:40
  17.8 15.0 %collective-permute-start.16 = (f32[384,128]{1,0:T(8,128)S(1)}, f32[384,128]{1,0:T(8,128)S(1)}, u32[]{:S(2)}, u32[]{:S(2)}) collective-permute-start(f32[384,128]{1,0:T(8,128)S(1)} %get-tuple-element.30), channel_id=1, source_target_pairs={{0,8},{1,9},{2,6},{3,7},{4,12},{5,13},{6,2},{7,3},{8,0},{9,1},{10,... | collective-permute-start | bytes 589832 | tf_op jit(solution)/shard_map/ppermute | solution.py:40
  19.6 15.9 %collective-permute-start.17 = (f32[384,128]{1,0:T(8,128)S(1)}, f32[384,128]{1,0:T(8,128)S(1)}, u32[]{:S(2)}, u32[]{:S(2)}) collective-permute-start(f32[384,128]{1,0:T(8,128)S(1)} %get-tuple-element.29), channel_id=1, source_target_pairs={{0,12},{1,13},{2,14},{3,15},{4,8},{5,9},{6,10},{7,11},{8,4},{9,5},... | collective-permute-start | bytes 589832 | tf_op jit(solution)/shard_map/ppermute | solution.py:40
  25.1 11.3 %collective-permute-start.7 = (f32[384,128]{1,0:T(8,128)S(1)}, f32[384,128]{1,0:T(8,128)S(1)}, u32[]{:S(2)}, u32[]{:S(2)}) collective-permute-start(f32[384,128]{1,0:T(8,128)S(1)} %fusion.7), channel_id=1, source_target_pairs={{0,16},{1,17},{2,18},{3,19},{4,20},{5,21},{6,22},{7,23},{8,24},{9,... | collective-permute-start | bytes 589832 | tf_op jit(solution)/shard_map/ppermute | solution.py:40
  36.3 10.2 %collective-permute-start.18 = (f32[384,128]{1,0:T(8,128)S(1)}, f32[384,128]{1,0:T(8,128)S(1)}, u32[]{:S(2)}, u32[]{:S(2)}) collective-permute-start(f32[384,128]{1,0:T(8,128)S(1)} %fusion.6), channel_id=1, source_target_pairs={{0,16},{1,17},{2,18},{3,19},{4,20},{5,21},{6,22},{7,23},{8,24},{9,... | collective-permute-start | bytes 589832 | tf_op jit(solution)/shard_map/ppermute | solution.py:40
  36.4 12.7 %collective-permute-start.10 = (f32[384,128]{1,0:T(8,128)S(1)}, f32[384,128]{1,0:T(8,128)S(1)}, u32[]{:S(2)}, u32[]{:S(2)}) collective-permute-start(f32[384,128]{1,0:T(8,128)S(1)} %add_multiply_fusion.1), channel_id=1, source_target_pairs={{0,12},{1,13},{2,14},{3,15},{4,8},{5,9},{6,10},{7,11},{8,4},{9,5},... | collective-permute-start | bytes 589832 | tf_op jit(solution)/shard_map/ppermute | solution.py:40
  41.0 12.1 %collective-permute-start.8 = (f32[384,128]{1,0:T(8,128)S(1)}, f32[384,128]{1,0:T(8,128)S(1)}, u32[]{:S(2)}, u32[]{:S(2)}) collective-permute-start(f32[384,128]{1,0:T(8,128)S(1)} %add_multiply_fusion.1), channel_id=1, source_target_pairs={{0,8},{1,9},{2,6},{3,7},{4,12},{5,13},{6,2},{7,3},{8,0},{9,1},{10,... | collective-permute-start | bytes 589832 | tf_op jit(solution)/shard_map/ppermute | solution.py:40
  41.0 12.1 %collective-permute-start.9 = (f32[384,128]{1,0:T(8,128)S(1)}, f32[384,128]{1,0:T(8,128)S(1)}, u32[]{:S(2)}, u32[]{:S(2)}) collective-permute-start(f32[384,128]{1,0:T(8,128)S(1)} %add_multiply_fusion.1), channel_id=1, source_target_pairs={{0,4},{1,5},{2,10},{3,11},{4,0},{5,1},{6,14},{7,15},{8,12},{9,13},... | collective-permute-start | bytes 589832 | tf_op jit(solution)/shard_map/ppermute | solution.py:40
  46.5 10.9 %collective-permute-start.19 = (f32[384,128]{1,0:T(8,128)S(1)}, f32[384,128]{1,0:T(8,128)S(1)}, u32[]{:S(2)}, u32[]{:S(2)}) collective-permute-start(f32[384,128]{1,0:T(8,128)S(1)} %add_multiply_fusion), channel_id=1, source_target_pairs={{0,8},{1,9},{2,6},{3,7},{4,12},{5,13},{6,2},{7,3},{8,0},{9,1},{10,... | collective-permute-start | bytes 589832 | tf_op jit(solution)/shard_map/ppermute | solution.py:40
  46.6 10.8 %collective-permute-start.20 = (f32[384,128]{1,0:T(8,128)S(1)}, f32[384,128]{1,0:T(8,128)S(1)}, u32[]{:S(2)}, u32[]{:S(2)}) collective-permute-start(f32[384,128]{1,0:T(8,128)S(1)} %add_multiply_fusion), channel_id=1, source_target_pairs={{0,4},{1,5},{2,10},{3,11},{4,0},{5,1},{6,14},{7,15},{8,12},{9,13},... | collective-permute-start | bytes 589832 | tf_op jit(solution)/shard_map/ppermute | solution.py:40
  49.1 10.5 %collective-permute-start.21 = (f32[384,128]{1,0:T(8,128)S(1)}, f32[384,128]{1,0:T(8,128)S(1)}, u32[]{:S(2)}, u32[]{:S(2)}) collective-permute-start(f32[384,128]{1,0:T(8,128)S(1)} %add_multiply_fusion), channel_id=1, source_target_pairs={{0,12},{1,13},{2,14},{3,15},{4,8},{5,9},{6,10},{7,11},{8,4},{9,5},... | collective-permute-start | bytes 589832 | tf_op jit(solution)/shard_map/ppermute | solution.py:40
  54.3 7.8 %collective-permute-start.11 = (f32[192,128]{1,0:T(8,128)S(1)}, f32[192,128]{1,0:T(8,128)S(1)}, u32[]{:S(2)}, u32[]{:S(2)}) collective-permute-start(f32[192,128]{1,0:T(8,128)S(1)} %slice.64), channel_id=1, source_target_pairs={{0,1},{1,0},{2,3},{3,2},{4,5},{5,4},{6,7},{7,6},{8,9},{9,8},{10,11... | collective-permute-start | bytes 294920 | tf_op jit(solution)/shard_map/ppermute | solution.py:40
  60.8 4.7 %collective-permute-start.22 = (f32[192,128]{1,0:T(8,128)S(1)}, f32[192,128]{1,0:T(8,128)S(1)}, u32[]{:S(2)}, u32[]{:S(2)}) collective-permute-start(f32[192,128]{1,0:T(8,128)S(1)} %slice.69), channel_id=1, source_target_pairs={{0,1},{1,0},{2,3},{3,2},{4,5},{5,4},{6,7},{7,6},{8,9},{9,8},{10,11... | collective-permute-start | bytes 294920 | tf_op jit(solution)/shard_map/ppermute | solution.py:40
  65.5 1.4 %collective-permute-start.23 = (f32[96,256]{1,0:T(8,128)S(1)}, f32[96,256]{1,0:T(8,128)S(1)}, u32[]{:S(2)}, u32[]{:S(2)}) collective-permute-start(f32[96,256]{1,0:T(8,128)S(1)} %pad_maximum_fusion.8), channel_id=1, source_target_pairs={{0,2},{1,3},{2,0},{3,1},{4,6},{5,7},{6,4},{7,5},{8,10},{9,11},{10,... | collective-permute-start | bytes 294920 | tf_op jit(solution)/shard_map/ppermute | solution.py:40
  (1 other events, 7.2 us)

commit v4 on v3

--- a/solution.py
+++ b/solution.py
@@ -67,34 +67,58 @@
             pieces.append(exchange(other, 1, k))
         chunks.append(jnp.concatenate(pieces, axis=0))
 
-    results = []
-    given = partial = None
+    def together(terms):
+        return lax.optimization_barrier(tuple(terms))
+
+    partners = ((2, 4), (4, 2), (6, 6))
+    quarters = (2, 1, 3)
+    sums = []
+    given = None
     for chunk in chunks:
-        if results:
+        if sums:
             chunk = after(chunk, given)
         given = product(matrix[:, quarter:], chunk, 0)
-        sent = [given[i * quarter : (i + 1) * quarter] for i in (1, 0, 2)]
-        MASKS = [((4, 2), (2, 4), (6, 6))[i] for i in (1, 0, 2)]
-        received = [exchange(block, masks, 0) for block, masks in zip(sent, MASKS)]
+        sent = [given[(i - 1) * quarter : i * quarter] for i in quarters]
+        received = together([exchange(block, masks, 0) for block, masks in zip(sent, partners)])
         total = product(matrix[:, :quarter], chunk, 0)
         for term in received:
             total = total + term
+        sums.append(total)
+
+    partials = []
+    for total in sums:
         mask = 8
         while mask < rows:
             total = total + exchange(total, mask, 0)
             mask *= 2
         fresh = total * (1.0 / half_width)
-        fresh = jnp.concatenate([fresh, *[exchange(fresh, masks, 0) for masks in ((4, 2), (2, 4), (6, 6))]], axis=0)
-        if results:
-            fresh = after(fresh, partial)
-        partial = product(matrix, fresh, 1)
+        received = dict(zip(quarters, [exchange(fresh, masks, 0) for masks in partners]))
+        fresh = jnp.concatenate([fresh, received[1], received[2], received[3]], axis=0)
+        if partials:
+            fresh = after(fresh, partials[-1])
+        partials.append(product(matrix, fresh, 1))
+
+    owns, others, lasts = [], [], []
+    for partial in partials[:-1]:
         total = partial[: 2 * part]
         for term in [exchange(partial[2 * part * k : 2 * part * (k + 1)], 0, k) for k in range(1, cols)]:
             total = total + term
-        results.append(total)
-    total = jnp.concatenate(results, axis=1)
-    own = total[:part]
-    other = exchange(total[part:], 1, 0)
+        owns.append(total[:part])
+        lasts.append(total[part:])
+    partial = partials[-1]
+    moves = [(k, c) for k in range(cols) for c in range(2)][1:]
+    terms = together(
+        [exchange(partial[(2 * k + c) * part : (2 * k + c + 1) * part], c, k) for k, c in moves]
+    )
+    own, other = partial[:part], None
+    for (_, c), term in zip(moves, terms):
+        if c == 0:
+            own = own + term
+        else:
+            other = term if other is None else other + term
+    own = jnp.concatenate([*owns, own], axis=1)
+    others = [exchange(last, 1, 0) for last in lasts]
+    other = jnp.concatenate([*others, other], axis=1)
     first = jnp.where(core == 0, own, other)
     last = jnp.where(core == 0, other, own)
     return 2.0 / half_width * jnp.concatenate([first, last], axis=1) - vectors

time: 67.8 us -> 66.6 us (0.982)
  waiting for transfers between devices: 27.1 us -> 22.5 us
  starting transfers between devices: 29.3 us -> 31.6 us
  matrix products: 6.69 us -> 7.69 us
    ppermute x24 -> x26, waiting for transfers between devices: 27.1 us -> 22.5 us  [exchange(): return lax.ppermute(block, ('row', 'col'), pairs)]
    ppermute x24 -> x26, starting transfers between devices: 29.3 us -> 31.6 us  [exchange(): return lax.ppermute(block, ('row', 'col'), pairs)]
    dot_general x6, matrix products: 6.69 us -> 7.69 us  [product(): lax.dot_general(left, right, (((left_dim,), (0,)), ((), ())), precision=l...]
  transfers between devices with their start and end apart: 24 -> 26, of which waited for: 11 -> 10; matrix products, arithmetic and copies ran while one was open for 15% -> 17% of each run, Pallas kernels for 0% -> 0%
where the time goes in v4:
time: 66.6 us; the launch traced here: 66.4 us
  starting transfers between devices  31.6 us (47%)
  waiting for transfers between devices  22.5 us (34%)
  matrix products  7.69 us (12%)
  other arithmetic  2.89 us (4%)
  local copies, waits for them, and re-layouts  1.45 us (2%)
    ppermute x26, starting transfers between devices, exchange(): return lax.ppermute(block, ('row', 'col'), pairs)  31.6 us
    ppermute x26, waiting for transfers between devices, exchange(): return lax.ppermute(block, ('row', 'col'), pairs)  22.5 us
    dot_general x6, matrix products, product(): lax.dot_general(left, right, (((left_dim,), (0,)), ((), ())), precision=l...  7.69 us
    sub x1, other arithmetic, prepared(): block - jnp.where(on_diagonal, jnp.float32(center), jnp.float32(0.0))  1.57 us
  transfers between devices with their start and end apart: 26, of which 10 were waited for; matrix products, arithmetic and copies ran while one was open for 17% of the time, Pallas kernels for 0%

profile of v4, /device:TPU:0, one launch (start us, length us, event | category | flops | bytes accessed | tf_op | source)
XLA Modules:
  0.0 66.4 jit_solution(9521334988794584325)
XLA Ops:
  1.5 2.6 %collective-permute-start.3 = (f32[96,128]{1,0:T(8,128)S(1)}, f32[96,128]{1,0:T(8,128)S(1)}, u32[]{:S(2)}, u32[]{:S(2)}) collective-permute-start(f32[96,128]{1,0:T(8,128)S(1)} %get-tuple-element.56), channel_id=1, source_target_pairs={{0,3},{1,2},{2,1},{3,0},{4,7},{5,6},{6,5},{7,4},{8,11},{9,10},{10,... | collective-permute-start | bytes 147464 | tf_op jit(solution)/shard_map/ppermute | solution.py:40
  4.5 1.6 %select_subtract_fusion.1 = (f32[192,1536]{1,0:T(8,128)S(1)}, f32[192,1536]{1,0:T(8,128)S(1)}) fusion(f32[192,1536]{1,0:T(8,128)} %param.2, s32[1536]{0:T(1024)S(1)} %iota_add_fusion, s32[192]{0:T(256)S(1)} %iota_add_fusion.2, f32[192,1536]{1,0:T(8,128)S(1)} %collective-permute-done, s32[192]{0:T(256)S(1)} %iota_add_fusion.1), kind=kLoop, calls=%fused_computation.8 | loop fusion | flops 1769472 | bytes 4726272 | tf_op jit(solution)/shard_map/sub | solution.py:49
  7.1 1.7 %collective-permute-start.14 = (f32[96,128]{1,0:T(8,128)S(1)}, f32[96,128]{1,0:T(8,128)S(1)}, u32[]{:S(2)}, u32[]{:S(2)}) collective-permute-start(f32[96,128]{1,0:T(8,128)S(1)} %get-tuple-element.22), channel_id=1, source_target_pairs={{0,3},{1,2},{2,1},{3,0},{4,7},{5,6},{6,5},{7,4},{8,11},{9,10},{10,... | collective-permute-start | bytes 147464 | tf_op jit(solution)/shard_map/ppermute | solution.py:40
  9.2 1.6 %fusion.2 = f32[1152,128]{1,0:T(8,128)S(1)} fusion(f32[384,1536]{1,0:T(8,128)S(1)} %pad_maximum_fusion, f32[96,128]{1,0:T(8,128)S(1)} %collective-permute-done.3, f32[96,128]{1,0:T(8,128)S(1)} %collective-permute-done.2, f32[96,128]{1,0:T(8,128)S(1)} %collective-permute-done.1, f32[96,128]{1,0:T(8,128)S(1)} %get-tuple-element.54), kind=kOutput, calls=%fused_computation.3 | convolution fusion | flops 339886080 | bytes 2555904 | tf_op jit(solution)/shard_map/dot_general | solution.py:14
  10.8 1.7 %collective-permute-start.4 = (f32[384,128]{1,0:T(8,128)S(1)}, f32[384,128]{1,0:T(8,128)S(1)}, u32[]{:S(2)}, u32[]{:S(2)}) collective-permute-start(f32[384,128]{1,0:T(8,128)S(1)} %get-tuple-element.45), channel_id=1, source_target_pairs={{0,4},{1,5},{2,10},{3,11},{4,0},{5,1},{6,14},{7,15},{8,12},{9,13},... | collective-permute-start | bytes 589832 | tf_op jit(solution)/shard_map/ppermute | solution.py:40
  12.5 1.6 %collective-permute-start.5 = (f32[384,128]{1,0:T(8,128)S(1)}, f32[384,128]{1,0:T(8,128)S(1)}, u32[]{:S(2)}, u32[]{:S(2)}) collective-permute-start(f32[384,128]{1,0:T(8,128)S(1)} %get-tuple-element.44), channel_id=1, source_target_pairs={{0,8},{1,9},{2,6},{3,7},{4,12},{5,13},{6,2},{7,3},{8,0},{9,1},{10,... | collective-permute-start | bytes 589832 | tf_op jit(solution)/shard_map/ppermute | solution.py:40
  14.4 1.6 %fusion = f32[1152,128]{1,0:T(8,128)S(1)} fusion(f32[384,128]{1,0:T(8,128)S(1)} %pad_maximum_fusion.5, f32[384,1536]{1,0:T(8,128)S(1)} %pad_maximum_fusion), kind=kOutput, calls=%fused_computation.1 | convolution fusion | flops 339738624 | bytes 2555904 | tf_op jit(solution)/shard_map/dot_general | solution.py:14
  16.0 1.7 %collective-permute-start.15 = (f32[384,128]{1,0:T(8,128)S(1)}, f32[384,128]{1,0:T(8,128)S(1)}, u32[]{:S(2)}, u32[]{:S(2)}) collective-permute-start(f32[384,128]{1,0:T(8,128)S(1)} %get-tuple-element.48), channel_id=1, source_target_pairs={{0,4},{1,5},{2,10},{3,11},{4,0},{5,1},{6,14},{7,15},{8,12},{9,13},... | collective-permute-start | bytes 589832 | tf_op jit(solution)/shard_map/ppermute | solution.py:40
  17.8 1.6 %collective-permute-start.16 = (f32[384,128]{1,0:T(8,128)S(1)}, f32[384,128]{1,0:T(8,128)S(1)}, u32[]{:S(2)}, u32[]{:S(2)}) collective-permute-start(f32[384,128]{1,0:T(8,128)S(1)} %get-tuple-element.47), channel_id=1, source_target_pairs={{0,8},{1,9},{2,6},{3,7},{4,12},{5,13},{6,2},{7,3},{8,0},{9,1},{10,... | collective-permute-start | bytes 589832 | tf_op jit(solution)/shard_map/ppermute | solution.py:40
  20.0 4.0 %collective-permute-start.17 = (f32[384,128]{1,0:T(8,128)S(1)}, f32[384,128]{1,0:T(8,128)S(1)}, u32[]{:S(2)}, u32[]{:S(2)}) collective-permute-start(f32[384,128]{1,0:T(8,128)S(1)} %get-tuple-element.46), channel_id=1, source_target_pairs={{0,12},{1,13},{2,14},{3,15},{4,8},{5,9},{6,10},{7,11},{8,4},{9,5},... | collective-permute-start | bytes 589832 | tf_op jit(solution)/shard_map/ppermute | solution.py:40
  25.1 2.8 %collective-permute-start.7 = (f32[384,128]{1,0:T(8,128)S(1)}, f32[384,128]{1,0:T(8,128)S(1)}, u32[]{:S(2)}, u32[]{:S(2)}) collective-permute-start(f32[384,128]{1,0:T(8,128)S(1)} %fusion.5), channel_id=1, source_target_pairs={{0,16},{1,17},{2,18},{3,19},{4,20},{5,21},{6,22},{7,23},{8,24},{9,... | collective-permute-start | bytes 589832 | tf_op jit(solution)/shard_map/ppermute | solution.py:40
  27.9 4.9 %collective-permute-done.16 = f32[384,128]{1,0:T(8,128)S(1)} collective-permute-done((f32[384,128]{1,0:T(8,128)S(1)}, f32[384,128]{1,0:T(8,128)S(1)}, u32[]{:S(2)}, u32[]{:S(2)}) %collective-permute-start.16) | collective-permute-done | bytes 196640 | tf_op jit(solution)/shard_map/ppermute | solution.py:40
  32.8 2.8 %collective-permute-done.17 = f32[384,128]{1,0:T(8,128)S(1)} collective-permute-done((f32[384,128]{1,0:T(8,128)S(1)}, f32[384,128]{1,0:T(8,128)S(1)}, u32[]{:S(2)}, u32[]{:S(2)}) %collective-permute-start.17) | collective-permute-done | bytes 196640 | tf_op jit(solution)/shard_map/ppermute | solution.py:40
  35.7 5.8 %collective-permute-start.10 = (f32[384,128]{1,0:T(8,128)S(1)}, f32[384,128]{1,0:T(8,128)S(1)}, u32[]{:S(2)}, u32[]{:S(2)}) collective-permute-start(f32[384,128]{1,0:T(8,128)S(1)} %add_multiply_fusion.1), channel_id=1, source_target_pairs={{0,12},{1,13},{2,14},{3,15},{4,8},{5,9},{6,10},{7,11},{8,4},{9,5},... | collective-permute-start | bytes 589832 | tf_op jit(solution)/shard_map/ppermute | solution.py:40
  42.2 3.7 %collective-permute-done.18 = f32[384,128]{1,0:T(8,128)S(1)} collective-permute-done((f32[384,128]{1,0:T(8,128)S(1)}, f32[384,128]{1,0:T(8,128)S(1)}, u32[]{:S(2)}, u32[]{:S(2)}) %collective-permute-start.18) | collective-permute-done | bytes 196640 | tf_op jit(solution)/shard_map/ppermute | solution.py:40
  46.8 1.8 %collective-permute-done.10 = f32[384,128]{1,0:T(8,128)S(1)} collective-permute-done((f32[384,128]{1,0:T(8,128)S(1)}, f32[384,128]{1,0:T(8,128)S(1)}, u32[]{:S(2)}, u32[]{:S(2)}) %collective-permute-start.10) | collective-permute-done | bytes 196640 | tf_op jit(solution)/shard_map/ppermute | solution.py:40
  49.5 2.5 %collective-permute-done.8 = f32[384,128]{1,0:T(8,128)} collective-permute-done((f32[384,128]{1,0:T(8,128)S(1)}, f32[384,128]{1,0:T(8,128)}, u32[]{:S(2)}, u32[]{:S(2)}) %collective-permute-start.8) | collective-permute-done | bytes 196640 | tf_op jit(solution)/shard_map/ppermute | solution.py:40
  52.0 2.1 %fusion.6 = f32[384,128]{1,0:T(8,128)S(1)} fusion(f32[384,128]{1,0:T(8,128)S(1)} %collective-permute-done.10, f32[384,128]{1,0:T(8,128)} %collective-permute-done.9, f32[384,128]{1,0:T(8,128)} %collective-permute-done.8, f32[384,128]{1,0:T(8,128)S(1)} %add_multiply_fusion.1, f32[96,1536]{1,0:T(8,128)S(1)} %get-tuple-element.34, ...), kind=kOutput, calls=%fused_computation.12 | convolution fusion | flops 455344128 | bytes 3342336 | tf_op jit(solution)/shard_map/dot_general | solution.py:14
  54.1 1.5 %collective-permute-start.11 = (f32[192,128]{1,0:T(8,128)S(1)}, f32[192,128]{1,0:T(8,128)S(1)}, u32[]{:S(2)}, u32[]{:S(2)}) collective-permute-start(f32[192,128]{1,0:T(8,128)S(1)} %slice.72), channel_id=1, source_target_pairs={{0,1},{1,0},{2,3},{3,2},{4,5},{5,4},{6,7},{7,6},{8,9},{9,8},{10,11... | collective-permute-start | bytes 294920 | tf_op jit(solution)/shard_map/ppermute | solution.py:40
  56.1 3.0 %collective-permute-done.21 = f32[384,128]{1,0:T(8,128)S(1)} collective-permute-done((f32[384,128]{1,0:T(8,128)S(1)}, f32[384,128]{1,0:T(8,128)S(1)}, u32[]{:S(2)}, u32[]{:S(2)}) %collective-permute-start.21) | collective-permute-done | bytes 196640 | tf_op jit(solution)/shard_map/ppermute | solution.py:40
  59.2 1.1 %fusion.23 = f32[384,128]{1,0:T(8,128)S(1)} fusion(f32[1536,128]{1,0:T(8,128)S(1)} %pad_maximum_fusion.3, f32[96,1536]{1,0:T(8,128)S(1)} %get-tuple-element.34, f32[96,1536]{1,0:T(8,128)S(1)} %get-tuple-element.32, f32[96,1536]{1,0:T(8,128)S(1)} %get-tuple-element.33, f32[96,1536]{1,0:T(8,128)S(1)} %get-tuple-element.31), kind=kOutput, calls=%fused_computation.59 | convolution fusion | flops 454754304 | bytes 3342336 | tf_op jit(solution)/shard_map/dot_general | solution.py:14
  60.4 1.6 %collective-permute-start.23 = (f32[96,128]{1,0:T(8,128)S(1)}, f32[96,128]{1,0:T(8,128)S(1)}, u32[]{:S(2)}, u32[]{:S(2)}) collective-permute-start(f32[96,128]{1,0:T(8,128)S(1)} %get-tuple-element.52), channel_id=1, source_target_pairs={{0,1},{1,0},{2,3},{3,2},{4,5},{5,4},{6,7},{7,6},{8,9},{9,8},{10,11... | collective-permute-start | bytes 147464 | tf_op jit(solution)/shard_map/ppermute | solution.py:40
  62.7 1.8 %collective-permute-done.23 = f32[96,128]{1,0:T(8,128)S(1)} collective-permute-done((f32[96,128]{1,0:T(8,128)S(1)}, f32[96,128]{1,0:T(8,128)S(1)}, u32[]{:S(2)}, u32[]{:S(2)}) %collective-permute-start.23) | collective-permute-done | bytes 49184 | tf_op jit(solution)/shard_map/ppermute | solution.py:40
  64.5 1.1 %collective-permute-done.24 = f32[96,128]{1,0:T(8,128)S(1)} collective-permute-done((f32[96,128]{1,0:T(8,128)S(1)}, f32[96,128]{1,0:T(8,128)S(1)}, u32[]{:S(2)}, u32[]{:S(2)}) %collective-permute-start.24) | collective-permute-done | bytes 49184 | tf_op jit(solution)/shard_map/ppermute | solution.py:40
  (62 shorter events, 10.0 us)
Async XLA Ops:
  0.0 4.5 %collective-permute-start = (f32[192,1536]{1,0:T(8,128)}, f32[192,1536]{1,0:T(8,128)S(1)}, u32[]{:S(2)}, u32[]{:S(2)}) collective-permute-start(f32[192,1536]{1,0:T(8,128)} %param.2), channel_id=1, source_target_pairs={{0,2},{1,3},{2,0},{3,1},{4,6},{5,7},{6,4},{7,5},{8,10},{9,11},{10,... | collective-permute-start | bytes 3538952 | tf_op jit(solution)/shard_map/ppermute | solution.py:40
  1.3 7.4 %collective-permute-start.1 = (f32[96,128]{1,0:T(8,128)S(1)}, f32[96,128]{1,0:T(8,128)S(1)}, u32[]{:S(2)}, u32[]{:S(2)}) collective-permute-start(f32[96,128]{1,0:T(8,128)S(1)} %get-tuple-element.56), channel_id=1, source_target_pairs={{0,2},{1,3},{2,0},{3,1},{4,6},{5,7},{6,4},{7,5},{8,10},{9,11},{10,... | collective-permute-start | bytes 147464 | tf_op jit(solution)/shard_map/ppermute | solution.py:40
  1.5 7.7 %collective-permute-start.3 = (f32[96,128]{1,0:T(8,128)S(1)}, f32[96,128]{1,0:T(8,128)S(1)}, u32[]{:S(2)}, u32[]{:S(2)}) collective-permute-start(f32[96,128]{1,0:T(8,128)S(1)} %get-tuple-element.56), channel_id=1, source_target_pairs={{0,3},{1,2},{2,1},{3,0},{4,7},{5,6},{6,5},{7,4},{8,11},{9,10},{10,... | collective-permute-start | bytes 147464 | tf_op jit(solution)/shard_map/ppermute | solution.py:40
  4.1 5.1 %collective-permute-start.2 = (f32[96,128]{1,0:T(8,128)S(1)}, f32[96,128]{1,0:T(8,128)S(1)}, u32[]{:S(2)}, u32[]{:S(2)}) collective-permute-start(f32[96,128]{1,0:T(8,128)S(1)} %get-tuple-element.54), channel_id=1, source_target_pairs={{0,1},{1,0},{2,3},{3,2},{4,5},{5,4},{6,7},{7,6},{8,9},{9,8},{10,11... | collective-permute-start | bytes 147464 | tf_op jit(solution)/shard_map/ppermute | solution.py:40
  6.9 7.2 %collective-permute-start.12 = (f32[96,128]{1,0:T(8,128)S(1)}, f32[96,128]{1,0:T(8,128)S(1)}, u32[]{:S(2)}, u32[]{:S(2)}) collective-permute-start(f32[96,128]{1,0:T(8,128)S(1)} %get-tuple-element.22), channel_id=1, source_target_pairs={{0,2},{1,3},{2,0},{3,1},{4,6},{5,7},{6,4},{7,5},{8,10},{9,11},{10,... | collective-permute-start | bytes 147464 | tf_op jit(solution)/shard_map/ppermute | solution.py:40
  7.1 7.3 %collective-permute-start.14 = (f32[96,128]{1,0:T(8,128)S(1)}, f32[96,128]{1,0:T(8,128)S(1)}, u32[]{:S(2)}, u32[]{:S(2)}) collective-permute-start(f32[96,128]{1,0:T(8,128)S(1)} %get-tuple-element.22), channel_id=1, source_target_pairs={{0,3},{1,2},{2,1},{3,0},{4,7},{5,6},{6,5},{7,4},{8,11},{9,10},{10,... | collective-permute-start | bytes 147464 | tf_op jit(solution)/shard_map/ppermute | solution.py:40
  8.8 5.6 %collective-permute-start.13 = (f32[96,128]{1,0:T(8,128)S(1)}, f32[96,128]{1,0:T(8,128)S(1)}, u32[]{:S(2)}, u32[]{:S(2)}) collective-permute-start(f32[96,128]{1,0:T(8,128)S(1)} %get-tuple-element.21), channel_id=1, source_target_pairs={{0,1},{1,0},{2,3},{3,2},{4,5},{5,4},{6,7},{7,6},{8,9},{9,8},{10,11... | collective-permute-start | bytes 147464 | tf_op jit(solution)/shard_map/ppermute | solution.py:40
  10.8 9.2 %collective-permute-start.4 = (f32[384,128]{1,0:T(8,128)S(1)}, f32[384,128]{1,0:T(8,128)S(1)}, u32[]{:S(2)}, u32[]{:S(2)}) collective-permute-start(f32[384,128]{1,0:T(8,128)S(1)} %get-tuple-element.45), channel_id=1, source_target_pairs={{0,4},{1,5},{2,10},{3,11},{4,0},{5,1},{6,14},{7,15},{8,12},{9,13},... | collective-permute-start | bytes 589832 | tf_op jit(solution)/shard_map/ppermute | solution.py:40
  12.5 11.4 %collective-permute-start.5 = (f32[384,128]{1,0:T(8,128)S(1)}, f32[384,128]{1,0:T(8,128)S(1)}, u32[]{:S(2)}, u32[]{:S(2)}) collective-permute-start(f32[384,128]{1,0:T(8,128)S(1)} %get-tuple-element.44), channel_id=1, source_target_pairs={{0,8},{1,9},{2,6},{3,7},{4,12},{5,13},{6,2},{7,3},{8,0},{9,1},{10,... | collective-permute-start | bytes 589832 | tf_op jit(solution)/shard_map/ppermute | solution.py:40
  14.1 10.3 %collective-permute-start.6 = (f32[384,128]{1,0:T(8,128)S(1)}, f32[384,128]{1,0:T(8,128)S(1)}, u32[]{:S(2)}, u32[]{:S(2)}) collective-permute-start(f32[384,128]{1,0:T(8,128)S(1)} %get-tuple-element.43), channel_id=1, source_target_pairs={{0,12},{1,13},{2,14},{3,15},{4,8},{5,9},{6,10},{7,11},{8,4},{9,5},... | collective-permute-start | bytes 589832 | tf_op jit(solution)/shard_map/ppermute | solution.py:40
  16.0 11.9 %collective-permute-start.15 = (f32[384,128]{1,0:T(8,128)S(1)}, f32[384,128]{1,0:T(8,128)S(1)}, u32[]{:S(2)}, u32[]{:S(2)}) collective-permute-start(f32[384,128]{1,0:T(8,128)S(1)} %get-tuple-element.48), channel_id=1, source_target_pairs={{0,4},{1,5},{2,10},{3,11},{4,0},{5,1},{6,14},{7,15},{8,12},{9,13},... | collective-permute-start | bytes 589832 | tf_op jit(solution)/shard_map/ppermute | solution.py:40
  17.8 15.0 %collective-permute-start.16 = (f32[384,128]{1,0:T(8,128)S(1)}, f32[384,128]{1,0:T(8,128)S(1)}, u32[]{:S(2)}, u32[]{:S(2)}) collective-permute-start(f32[384,128]{1,0:T(8,128)S(1)} %get-tuple-element.47), channel_id=1, source_target_pairs={{0,8},{1,9},{2,6},{3,7},{4,12},{5,13},{6,2},{7,3},{8,0},{9,1},{10,... | collective-permute-start | bytes 589832 | tf_op jit(solution)/shard_map/ppermute | solution.py:40
  20.0 15.6 %collective-permute-start.17 = (f32[384,128]{1,0:T(8,128)S(1)}, f32[384,128]{1,0:T(8,128)S(1)}, u32[]{:S(2)}, u32[]{:S(2)}) collective-permute-start(f32[384,128]{1,0:T(8,128)S(1)} %get-tuple-element.46), channel_id=1, source_target_pairs={{0,12},{1,13},{2,14},{3,15},{4,8},{5,9},{6,10},{7,11},{8,4},{9,5},... | collective-permute-start | bytes 589832 | tf_op jit(solution)/shard_map/ppermute | solution.py:40
  25.1 10.6 %collective-permute-start.7 = (f32[384,128]{1,0:T(8,128)S(1)}, f32[384,128]{1,0:T(8,128)S(1)}, u32[]{:S(2)}, u32[]{:S(2)}) collective-permute-start(f32[384,128]{1,0:T(8,128)S(1)} %fusion.5), channel_id=1, source_target_pairs={{0,16},{1,17},{2,18},{3,19},{4,20},{5,21},{6,22},{7,23},{8,24},{9,... | collective-permute-start | bytes 589832 | tf_op jit(solution)/shard_map/ppermute | solution.py:40
  35.6 10.2 %collective-permute-start.18 = (f32[384,128]{1,0:T(8,128)S(1)}, f32[384,128]{1,0:T(8,128)S(1)}, u32[]{:S(2)}, u32[]{:S(2)}) collective-permute-start(f32[384,128]{1,0:T(8,128)S(1)} %add_add_fusion), channel_id=1, source_target_pairs={{0,16},{1,17},{2,18},{3,19},{4,20},{5,21},{6,22},{7,23},{8,24},{9,... | collective-permute-start | bytes 589832 | tf_op jit(solution)/shard_map/ppermute | solution.py:40
  35.7 12.9 %collective-permute-start.10 = (f32[384,128]{1,0:T(8,128)S(1)}, f32[384,128]{1,0:T(8,128)S(1)}, u32[]{:S(2)}, u32[]{:S(2)}) collective-permute-start(f32[384,128]{1,0:T(8,128)S(1)} %add_multiply_fusion.1), channel_id=1, source_target_pairs={{0,12},{1,13},{2,14},{3,15},{4,8},{5,9},{6,10},{7,11},{8,4},{9,5},... | collective-permute-start | bytes 589832 | tf_op jit(solution)/shard_map/ppermute | solution.py:40
  41.6 10.4 %collective-permute-start.8 = (f32[384,128]{1,0:T(8,128)S(1)}, f32[384,128]{1,0:T(8,128)}, u32[]{:S(2)}, u32[]{:S(2)}) collective-permute-start(f32[384,128]{1,0:T(8,128)S(1)} %add_multiply_fusion.1), channel_id=1, source_target_pairs={{0,8},{1,9},{2,6},{3,7},{4,12},{5,13},{6,2},{7,3},{8,0},{9,1},{10,... | collective-permute-start | bytes 589832 | tf_op jit(solution)/shard_map/ppermute | solution.py:40
  41.6 10.4 %collective-permute-start.9 = (f32[384,128]{1,0:T(8,128)S(1)}, f32[384,128]{1,0:T(8,128)}, u32[]{:S(2)}, u32[]{:S(2)}) collective-permute-start(f32[384,128]{1,0:T(8,128)S(1)} %add_multiply_fusion.1), channel_id=1, source_target_pairs={{0,4},{1,5},{2,10},{3,11},{4,0},{5,1},{6,14},{7,15},{8,12},{9,13},... | collective-permute-start | bytes 589832 | tf_op jit(solution)/shard_map/ppermute | solution.py:40
  45.9 10.2 %collective-permute-start.19 = (f32[384,128]{1,0:T(8,128)S(1)}, f32[384,128]{1,0:T(8,128)S(1)}, u32[]{:S(2)}, u32[]{:S(2)}) collective-permute-start(f32[384,128]{1,0:T(8,128)S(1)} %add_multiply_fusion), channel_id=1, source_target_pairs={{0,8},{1,9},{2,6},{3,7},{4,12},{5,13},{6,2},{7,3},{8,0},{9,1},{10,... | collective-permute-start | bytes 589832 | tf_op jit(solution)/shard_map/ppermute | solution.py:40
  46.0 10.2 %collective-permute-start.20 = (f32[384,128]{1,0:T(8,128)S(1)}, f32[384,128]{1,0:T(8,128)S(1)}, u32[]{:S(2)}, u32[]{:S(2)}) collective-permute-start(f32[384,128]{1,0:T(8,128)S(1)} %add_multiply_fusion), channel_id=1, source_target_pairs={{0,4},{1,5},{2,10},{3,11},{4,0},{5,1},{6,14},{7,15},{8,12},{9,13},... | collective-permute-start | bytes 589832 | tf_op jit(solution)/shard_map/ppermute | solution.py:40
  48.6 10.5 %collective-permute-start.21 = (f32[384,128]{1,0:T(8,128)S(1)}, f32[384,128]{1,0:T(8,128)S(1)}, u32[]{:S(2)}, u32[]{:S(2)}) collective-permute-start(f32[384,128]{1,0:T(8,128)S(1)} %add_multiply_fusion), channel_id=1, source_target_pairs={{0,12},{1,13},{2,14},{3,15},{4,8},{5,9},{6,10},{7,11},{8,4},{9,5},... | collective-permute-start | bytes 589832 | tf_op jit(solution)/shard_map/ppermute | solution.py:40
  54.1 8.1 %collective-permute-start.11 = (f32[192,128]{1,0:T(8,128)S(1)}, f32[192,128]{1,0:T(8,128)S(1)}, u32[]{:S(2)}, u32[]{:S(2)}) collective-permute-start(f32[192,128]{1,0:T(8,128)S(1)} %slice.72), channel_id=1, source_target_pairs={{0,1},{1,0},{2,3},{3,2},{4,5},{5,4},{6,7},{7,6},{8,9},{9,8},{10,11... | collective-permute-start | bytes 294920 | tf_op jit(solution)/shard_map/ppermute | solution.py:40
  60.4 4.2 %collective-permute-start.23 = (f32[96,128]{1,0:T(8,128)S(1)}, f32[96,128]{1,0:T(8,128)S(1)}, u32[]{:S(2)}, u32[]{:S(2)}) collective-permute-start(f32[96,128]{1,0:T(8,128)S(1)} %get-tuple-element.52), channel_id=1, source_target_pairs={{0,1},{1,0},{2,3},{3,2},{4,5},{5,4},{6,7},{7,6},{8,9},{9,8},{10,11... | collective-permute-start | bytes 147464 | tf_op jit(solution)/shard_map/ppermute | solution.py:40
  61.9 3.7 %collective-permute-start.24 = (f32[96,128]{1,0:T(8,128)S(1)}, f32[96,128]{1,0:T(8,128)S(1)}, u32[]{:S(2)}, u32[]{:S(2)}) collective-permute-start(f32[96,128]{1,0:T(8,128)S(1)} %get-tuple-element.51), channel_id=1, source_target_pairs={{0,3},{1,2},{2,1},{3,0},{4,7},{5,6},{6,5},{7,4},{8,11},{9,10},{10,... | collective-permute-start | bytes 147464 | tf_op jit(solution)/shard_map/ppermute | solution.py:40
  (3 other events, 12.3 us)

commit v5 on v4

--- a/solution.py
+++ b/solution.py
@@ -77,12 +77,18 @@
     for chunk in chunks:
         if sums:
             chunk = after(chunk, given)
-        given = product(matrix[:, quarter:], chunk, 0)
-        sent = [given[(i - 1) * quarter : i * quarter] for i in quarters]
-        received = together([exchange(block, masks, 0) for block, masks in zip(sent, partners)])
-        total = product(matrix[:, :quarter], chunk, 0)
-        for term in received:
-            total = total + term
+            given = product(matrix[:, 2 * quarter :], chunk, 0)
+            crossed = exchange(given[quarter:], partners[0], 0)
+            straight = exchange(given[:quarter], partners[0], 0)
+            passed = product(matrix[:, quarter : 2 * quarter], chunk, 0) + crossed
+            total = product(matrix[:, :quarter], chunk, 0) + straight + exchange(passed, partners[1], 0)
+        else:
+            given = product(matrix[:, quarter:], chunk, 0)
+            sent = [given[(i - 1) * quarter : i * quarter] for i in quarters]
+            received = together([exchange(block, masks, 0) for block, masks in zip(sent, partners)])
+            total = product(matrix[:, :quarter], chunk, 0)
+            for term in received:
+                total = total + term
         sums.append(total)
 
     partials = []
@@ -92,10 +98,13 @@
             total = total + exchange(total, mask, 0)
             mask *= 2
         fresh = total * (1.0 / half_width)
-        received = dict(zip(quarters, [exchange(fresh, masks, 0) for masks in partners]))
-        fresh = jnp.concatenate([fresh, received[1], received[2], received[3]], axis=0)
         if partials:
+            received = dict(zip(quarters, [exchange(fresh, masks, 0) for masks in partners]))
+            fresh = jnp.concatenate([fresh, received[1], received[2], received[3]], axis=0)
             fresh = after(fresh, partials[-1])
+        else:
+            second, first = together([exchange(fresh, partners[1], 0), exchange(fresh, partners[0], 0)])
+            fresh = jnp.concatenate([fresh, second, first, exchange(second, partners[0], 0)], axis=0)
         partials.append(product(matrix, fresh, 1))
 
     owns, others, lasts = [], [], []

time: 66.6 us -> 65.3 us (0.980)
  waiting for transfers between devices: 22.5 us -> 19.5 us
  starting transfers between devices: 31.6 us -> 33.1 us
    ppermute x26, waiting for transfers between devices: 22.5 us -> 19.5 us  [exchange(): return lax.ppermute(block, ('row', 'col'), pairs)]
    ppermute x26, starting transfers between devices: 31.6 us -> 33.1 us  [exchange(): return lax.ppermute(block, ('row', 'col'), pairs)]
    dot_general x6 -> x7, matrix products: 7.69 us -> 7.95 us  [product(): lax.dot_general(left, right, (((left_dim,), (0,)), ((), ())), precision=l...]
  transfers between devices with their start and end apart: 26 -> 26, of which waited for: 10 -> 10; matrix products, arithmetic and copies ran while one was open for 17% -> 18% of each run, Pallas kernels for 0% -> 0%
where the time goes in v5:
time: 65.3 us; the launch traced here: 65.1 us
  starting transfers between devices  33.1 us (51%)
  waiting for transfers between devices  19.5 us (30%)
  matrix products  7.95 us (12%)
  other arithmetic  2.85 us (4%)
  local copies, waits for them, and re-layouts  1.43 us (2%)
    ppermute x26, starting transfers between devices, exchange(): return lax.ppermute(block, ('row', 'col'), pairs)  33.1 us
    ppermute x26, waiting for transfers between devices, exchange(): return lax.ppermute(block, ('row', 'col'), pairs)  19.5 us
    dot_general x7, matrix products, product(): lax.dot_general(left, right, (((left_dim,), (0,)), ((), ())), precision=l...  7.95 us
    sub x1, other arithmetic, prepared(): block - jnp.where(on_diagonal, jnp.float32(center), jnp.float32(0.0))  1.57 us
  transfers between devices with their start and end apart: 26, of which 10 were waited for; matrix products, arithmetic and copies ran while one was open for 18% of the time, Pallas kernels for 0%

profile of v5, /device:TPU:0, one launch (start us, length us, event | category | flops | bytes accessed | tf_op | source)
XLA Modules:
  0.0 65.1 jit_solution(8072956101867871969)
XLA Ops:
  1.5 2.6 %collective-permute-start.3 = (f32[96,128]{1,0:T(8,128)S(1)}, f32[96,128]{1,0:T(8,128)S(1)}, u32[]{:S(2)}, u32[]{:S(2)}) collective-permute-start(f32[96,128]{1,0:T(8,128)S(1)} %get-tuple-element.53), channel_id=1, source_target_pairs={{0,3},{1,2},{2,1},{3,0},{4,7},{5,6},{6,5},{7,4},{8,11},{9,10},{10,... | collective-permute-start | bytes 147464 | tf_op jit(solution)/shard_map/ppermute | solution.py:40
  4.5 1.6 %select_subtract_fusion.1 = (f32[192,1536]{1,0:T(8,128)S(1)}, f32[192,1536]{1,0:T(8,128)S(1)}) fusion(f32[192,1536]{1,0:T(8,128)} %param.2, s32[1536]{0:T(1024)S(1)} %iota_add_fusion, s32[192]{0:T(256)S(1)} %iota_add_fusion.2, f32[192,1536]{1,0:T(8,128)S(1)} %collective-permute-done, s32[192]{0:T(256)S(1)} %iota_add_fusion.1), kind=kLoop, calls=%fused_computation.8 | loop fusion | flops 1769472 | bytes 4726272 | tf_op jit(solution)/shard_map/sub | solution.py:49
  7.1 1.7 %collective-permute-start.14 = (f32[96,128]{1,0:T(8,128)S(1)}, f32[96,128]{1,0:T(8,128)S(1)}, u32[]{:S(2)}, u32[]{:S(2)}) collective-permute-start(f32[96,128]{1,0:T(8,128)S(1)} %get-tuple-element.23), channel_id=1, source_target_pairs={{0,3},{1,2},{2,1},{3,0},{4,7},{5,6},{6,5},{7,4},{8,11},{9,10},{10,... | collective-permute-start | bytes 147464 | tf_op jit(solution)/shard_map/ppermute | solution.py:40
  9.2 1.6 %fusion = f32[1152,128]{1,0:T(8,128)S(1)} fusion(f32[384,1536]{1,0:T(8,128)S(1)} %pad_maximum_fusion, f32[96,128]{1,0:T(8,128)S(1)} %collective-permute-done.3, f32[96,128]{1,0:T(8,128)S(1)} %collective-permute-done.2, f32[96,128]{1,0:T(8,128)S(1)} %collective-permute-done.1, f32[96,128]{1,0:T(8,128)S(1)} %get-tuple-element.51), kind=kOutput, calls=%fused_computation.1 | convolution fusion | flops 339886080 | bytes 2555904 | tf_op jit(solution)/shard_map/dot_general | solution.py:14
  10.8 1.7 %collective-permute-start.4 = (f32[384,128]{1,0:T(8,128)S(1)}, f32[384,128]{1,0:T(8,128)S(1)}, u32[]{:S(2)}, u32[]{:S(2)}) collective-permute-start(f32[384,128]{1,0:T(8,128)S(1)} %get-tuple-element.43), channel_id=1, source_target_pairs={{0,4},{1,5},{2,10},{3,11},{4,0},{5,1},{6,14},{7,15},{8,12},{9,13},... | collective-permute-start | bytes 589832 | tf_op jit(solution)/shard_map/ppermute | solution.py:40
  12.5 1.6 %collective-permute-start.5 = (f32[384,128]{1,0:T(8,128)S(1)}, f32[384,128]{1,0:T(8,128)S(1)}, u32[]{:S(2)}, u32[]{:S(2)}) collective-permute-start(f32[384,128]{1,0:T(8,128)S(1)} %get-tuple-element.42), channel_id=1, source_target_pairs={{0,8},{1,9},{2,6},{3,7},{4,12},{5,13},{6,2},{7,3},{8,0},{9,1},{10,... | collective-permute-start | bytes 589832 | tf_op jit(solution)/shard_map/ppermute | solution.py:40
  14.4 1.2 %fusion.2 = f32[768,128]{1,0:T(8,128)S(1)} fusion(f32[384,128]{1,0:T(8,128)S(1)} %pad_maximum_fusion.5, f32[384,1536]{1,0:T(8,128)S(1)} %pad_maximum_fusion), kind=kOutput, calls=%fused_computation.3 | convolution fusion | flops 226492416 | bytes 1769472 | tf_op jit(solution)/shard_map/dot_general | solution.py:14
  15.6 1.7 %collective-permute-start.16 = (f32[384,128]{1,0:T(8,128)S(1)}, f32[384,128]{1,0:T(8,128)S(1)}, u32[]{:S(2)}, u32[]{:S(2)}) collective-permute-start(f32[384,128]{1,0:T(8,128)S(1)} %get-tuple-element.45), channel_id=1, source_target_pairs={{0,4},{1,5},{2,10},{3,11},{4,0},{5,1},{6,14},{7,15},{8,12},{9,13},... | collective-permute-start | bytes 589832 | tf_op jit(solution)/shard_map/ppermute | solution.py:40
  17.7 2.0 %collective-permute-done.4 = f32[384,128]{1,0:T(8,128)S(1)} collective-permute-done((f32[384,128]{1,0:T(8,128)S(1)}, f32[384,128]{1,0:T(8,128)S(1)}, u32[]{:S(2)}, u32[]{:S(2)}) %collective-permute-start.4) | collective-permute-done | bytes 196640 | tf_op jit(solution)/shard_map/ppermute | solution.py:40
  20.3 4.1 %collective-permute-done.6 = f32[384,128]{1,0:T(8,128)S(1)} collective-permute-done((f32[384,128]{1,0:T(8,128)S(1)}, f32[384,128]{1,0:T(8,128)S(1)}, u32[]{:S(2)}, u32[]{:S(2)}) %collective-permute-start.6) | collective-permute-done | bytes 196640 | tf_op jit(solution)/shard_map/ppermute | solution.py:40
  25.1 2.8 %collective-permute-start.7 = (f32[384,128]{1,0:T(8,128)S(1)}, f32[384,128]{1,0:T(8,128)S(1)}, u32[]{:S(2)}, u32[]{:S(2)}) collective-permute-start(f32[384,128]{1,0:T(8,128)S(1)} %fusion.6), channel_id=1, source_target_pairs={{0,16},{1,17},{2,18},{3,19},{4,20},{5,21},{6,22},{7,23},{8,24},{9,... | collective-permute-start | bytes 589832 | tf_op jit(solution)/shard_map/ppermute | solution.py:40
  28.6 3.7 %collective-permute-start.17 = (f32[384,128]{1,0:T(8,128)S(1)}, f32[384,128]{1,0:T(8,128)S(1)}, u32[]{:S(2)}, u32[]{:S(2)}) collective-permute-start(f32[384,128]{1,0:T(8,128)S(1)} %convolution_add_fusion), channel_id=1, source_target_pairs={{0,8},{1,9},{2,6},{3,7},{4,12},{5,13},{6,2},{7,3},{8,0},{9,1},{10,... | collective-permute-start | bytes 589832 | tf_op jit(solution)/shard_map/ppermute | solution.py:40
  32.3 2.7 %collective-permute-done.7 = f32[384,128]{1,0:T(8,128)S(1)} collective-permute-done((f32[384,128]{1,0:T(8,128)S(1)}, f32[384,128]{1,0:T(8,128)S(1)}, u32[]{:S(2)}, u32[]{:S(2)}) %collective-permute-start.7) | collective-permute-done | bytes 196640 | tf_op jit(solution)/shard_map/ppermute | solution.py:40
  35.4 1.2 %collective-permute-start.9 = (f32[384,128]{1,0:T(8,128)S(1)}, f32[384,128]{1,0:T(8,128)}, u32[]{:S(2)}, u32[]{:S(2)}) collective-permute-start(f32[384,128]{1,0:T(8,128)S(1)} %add_multiply_fusion.1), channel_id=1, source_target_pairs={{0,4},{1,5},{2,10},{3,11},{4,0},{5,1},{6,14},{7,15},{8,12},{9,13},... | collective-permute-start | bytes 589832 | tf_op jit(solution)/shard_map/ppermute | solution.py:40
  38.0 3.4 %collective-permute-start.18 = (f32[384,128]{1,0:T(8,128)S(1)}, f32[384,128]{1,0:T(8,128)S(1)}, u32[]{:S(2)}, u32[]{:S(2)}) collective-permute-start(f32[384,128]{1,0:T(8,128)S(1)} %fusion.5), channel_id=1, source_target_pairs={{0,16},{1,17},{2,18},{3,19},{4,20},{5,21},{6,22},{7,23},{8,24},{9,... | collective-permute-start | bytes 589832 | tf_op jit(solution)/shard_map/ppermute | solution.py:40
  42.4 1.6 %collective-permute-start.10 = (f32[384,128]{1,0:T(8,128)S(1)}, f32[384,128]{1,0:T(8,128)}, u32[]{:S(2)}, u32[]{:S(2)}) collective-permute-start(f32[384,128]{1,0:T(8,128)S(1)} %collective-permute-done.8), channel_id=1, source_target_pairs={{0,4},{1,5},{2,10},{3,11},{4,0},{5,1},{6,14},{7,15},{8,12},{9,13},... | collective-permute-start | bytes 589832 | tf_op jit(solution)/shard_map/ppermute | solution.py:40
  44.0 2.8 %collective-permute-done.18 = f32[384,128]{1,0:T(8,128)S(1)} collective-permute-done((f32[384,128]{1,0:T(8,128)S(1)}, f32[384,128]{1,0:T(8,128)S(1)}, u32[]{:S(2)}, u32[]{:S(2)}) %collective-permute-start.18) | collective-permute-done | bytes 196640 | tf_op jit(solution)/shard_map/ppermute | solution.py:40
  46.8 3.2 %collective-permute-start.19 = (f32[384,128]{1,0:T(8,128)S(1)}, f32[384,128]{1,0:T(8,128)S(1)}, u32[]{:S(2)}, u32[]{:S(2)}) collective-permute-start(f32[384,128]{1,0:T(8,128)S(1)} %add_multiply_fusion), channel_id=1, source_target_pairs={{0,8},{1,9},{2,6},{3,7},{4,12},{5,13},{6,2},{7,3},{8,0},{9,1},{10,... | collective-permute-start | bytes 589832 | tf_op jit(solution)/shard_map/ppermute | solution.py:40
  50.0 1.5 %collective-permute-start.21 = (f32[384,128]{1,0:T(8,128)S(1)}, f32[384,128]{1,0:T(8,128)S(1)}, u32[]{:S(2)}, u32[]{:S(2)}) collective-permute-start(f32[384,128]{1,0:T(8,128)S(1)} %add_multiply_fusion), channel_id=1, source_target_pairs={{0,12},{1,13},{2,14},{3,15},{4,8},{5,9},{6,10},{7,11},{8,4},{9,5},... | collective-permute-start | bytes 589832 | tf_op jit(solution)/shard_map/ppermute | solution.py:40
  51.5 2.1 %fusion.7 = f32[384,128]{1,0:T(8,128)S(1)} fusion(f32[384,128]{1,0:T(8,128)} %collective-permute-done.10, f32[384,128]{1,0:T(8,128)} %collective-permute-done.9, f32[384,128]{1,0:T(8,128)S(1)} %collective-permute-done.8, f32[384,128]{1,0:T(8,128)S(1)} %add_multiply_fusion.1, f32[96,1536]{1,0:T(8,128)S(1)} %get-tuple-element.32, ...), kind=kOutput, calls=%fused_computation.15 | convolution fusion | flops 455344128 | bytes 3342336 | tf_op jit(solution)/shard_map/dot_general | solution.py:14
  53.7 1.6 %collective-permute-start.11 = (f32[192,128]{1,0:T(8,128)S(1)}, f32[192,128]{1,0:T(8,128)S(1)}, u32[]{:S(2)}, u32[]{:S(2)}) collective-permute-start(f32[192,128]{1,0:T(8,128)S(1)} %slice.75), channel_id=1, source_target_pairs={{0,1},{1,0},{2,3},{3,2},{4,5},{5,4},{6,7},{7,6},{8,9},{9,8},{10,11... | collective-permute-start | bytes 294920 | tf_op jit(solution)/shard_map/ppermute | solution.py:40
  55.2 2.5 %collective-permute-done.20 = f32[384,128]{1,0:T(8,128)S(1)} collective-permute-done((f32[384,128]{1,0:T(8,128)S(1)}, f32[384,128]{1,0:T(8,128)S(1)}, u32[]{:S(2)}, u32[]{:S(2)}) %collective-permute-start.20) | collective-permute-done | bytes 196640 | tf_op jit(solution)/shard_map/ppermute | solution.py:40
  59.0 1.6 %collective-permute-start.23 = (f32[96,128]{1,0:T(8,128)S(1)}, f32[96,128]{1,0:T(8,128)S(1)}, u32[]{:S(2)}, u32[]{:S(2)}) collective-permute-start(f32[96,128]{1,0:T(8,128)S(1)} %get-tuple-element.49), channel_id=1, source_target_pairs={{0,1},{1,0},{2,3},{3,2},{4,5},{5,4},{6,7},{7,6},{8,9},{9,8},{10,11... | collective-permute-start | bytes 147464 | tf_op jit(solution)/shard_map/ppermute | solution.py:40
  61.3 1.8 %collective-permute-done.23 = f32[96,128]{1,0:T(8,128)S(1)} collective-permute-done((f32[96,128]{1,0:T(8,128)S(1)}, f32[96,128]{1,0:T(8,128)S(1)}, u32[]{:S(2)}, u32[]{:S(2)}) %collective-permute-start.23) | collective-permute-done | bytes 49184 | tf_op jit(solution)/shard_map/ppermute | solution.py:40
  (62 shorter events, 12.6 us)
Async XLA Ops:
  0.0 4.5 %collective-permute-start = (f32[192,1536]{1,0:T(8,128)}, f32[192,1536]{1,0:T(8,128)S(1)}, u32[]{:S(2)}, u32[]{:S(2)}) collective-permute-start(f32[192,1536]{1,0:T(8,128)} %param.2), channel_id=1, source_target_pairs={{0,2},{1,3},{2,0},{3,1},{4,6},{5,7},{6,4},{7,5},{8,10},{9,11},{10,... | collective-permute-start | bytes 3538952 | tf_op jit(solution)/shard_map/ppermute | solution.py:40
  1.3 7.4 %collective-permute-start.1 = (f32[96,128]{1,0:T(8,128)S(1)}, f32[96,128]{1,0:T(8,128)S(1)}, u32[]{:S(2)}, u32[]{:S(2)}) collective-permute-start(f32[96,128]{1,0:T(8,128)S(1)} %get-tuple-element.53), channel_id=1, source_target_pairs={{0,2},{1,3},{2,0},{3,1},{4,6},{5,7},{6,4},{7,5},{8,10},{9,11},{10,... | collective-permute-start | bytes 147464 | tf_op jit(solution)/shard_map/ppermute | solution.py:40
  1.5 7.7 %collective-permute-start.3 = (f32[96,128]{1,0:T(8,128)S(1)}, f32[96,128]{1,0:T(8,128)S(1)}, u32[]{:S(2)}, u32[]{:S(2)}) collective-permute-start(f32[96,128]{1,0:T(8,128)S(1)} %get-tuple-element.53), channel_id=1, source_target_pairs={{0,3},{1,2},{2,1},{3,0},{4,7},{5,6},{6,5},{7,4},{8,11},{9,10},{10,... | collective-permute-start | bytes 147464 | tf_op jit(solution)/shard_map/ppermute | solution.py:40
  4.1 5.1 %collective-permute-start.2 = (f32[96,128]{1,0:T(8,128)S(1)}, f32[96,128]{1,0:T(8,128)S(1)}, u32[]{:S(2)}, u32[]{:S(2)}) collective-permute-start(f32[96,128]{1,0:T(8,128)S(1)} %get-tuple-element.51), channel_id=1, source_target_pairs={{0,1},{1,0},{2,3},{3,2},{4,5},{5,4},{6,7},{7,6},{8,9},{9,8},{10,11... | collective-permute-start | bytes 147464 | tf_op jit(solution)/shard_map/ppermute | solution.py:40
  6.9 7.2 %collective-permute-start.12 = (f32[96,128]{1,0:T(8,128)S(1)}, f32[96,128]{1,0:T(8,128)S(1)}, u32[]{:S(2)}, u32[]{:S(2)}) collective-permute-start(f32[96,128]{1,0:T(8,128)S(1)} %get-tuple-element.23), channel_id=1, source_target_pairs={{0,2},{1,3},{2,0},{3,1},{4,6},{5,7},{6,4},{7,5},{8,10},{9,11},{10,... | collective-permute-start | bytes 147464 | tf_op jit(solution)/shard_map/ppermute | solution.py:40
  7.1 7.3 %collective-permute-start.14 = (f32[96,128]{1,0:T(8,128)S(1)}, f32[96,128]{1,0:T(8,128)S(1)}, u32[]{:S(2)}, u32[]{:S(2)}) collective-permute-start(f32[96,128]{1,0:T(8,128)S(1)} %get-tuple-element.23), channel_id=1, source_target_pairs={{0,3},{1,2},{2,1},{3,0},{4,7},{5,6},{6,5},{7,4},{8,11},{9,10},{10,... | collective-permute-start | bytes 147464 | tf_op jit(solution)/shard_map/ppermute | solution.py:40
  8.8 5.6 %collective-permute-start.13 = (f32[96,128]{1,0:T(8,128)S(1)}, f32[96,128]{1,0:T(8,128)S(1)}, u32[]{:S(2)}, u32[]{:S(2)}) collective-permute-start(f32[96,128]{1,0:T(8,128)S(1)} %get-tuple-element.22), channel_id=1, source_target_pairs={{0,1},{1,0},{2,3},{3,2},{4,5},{5,4},{6,7},{7,6},{8,9},{9,8},{10,11... | collective-permute-start | bytes 147464 | tf_op jit(solution)/shard_map/ppermute | solution.py:40
  10.8 8.8 %collective-permute-start.4 = (f32[384,128]{1,0:T(8,128)S(1)}, f32[384,128]{1,0:T(8,128)S(1)}, u32[]{:S(2)}, u32[]{:S(2)}) collective-permute-start(f32[384,128]{1,0:T(8,128)S(1)} %get-tuple-element.43), channel_id=1, source_target_pairs={{0,4},{1,5},{2,10},{3,11},{4,0},{5,1},{6,14},{7,15},{8,12},{9,13},... | collective-permute-start | bytes 589832 | tf_op jit(solution)/shard_map/ppermute | solution.py:40
  12.5 7.8 %collective-permute-start.5 = (f32[384,128]{1,0:T(8,128)S(1)}, f32[384,128]{1,0:T(8,128)S(1)}, u32[]{:S(2)}, u32[]{:S(2)}) collective-permute-start(f32[384,128]{1,0:T(8,128)S(1)} %get-tuple-element.42), channel_id=1, source_target_pairs={{0,8},{1,9},{2,6},{3,7},{4,12},{5,13},{6,2},{7,3},{8,0},{9,1},{10,... | collective-permute-start | bytes 589832 | tf_op jit(solution)/shard_map/ppermute | solution.py:40
  14.1 10.3 %collective-permute-start.6 = (f32[384,128]{1,0:T(8,128)S(1)}, f32[384,128]{1,0:T(8,128)S(1)}, u32[]{:S(2)}, u32[]{:S(2)}) collective-permute-start(f32[384,128]{1,0:T(8,128)S(1)} %get-tuple-element.41), channel_id=1, source_target_pairs={{0,12},{1,13},{2,14},{3,15},{4,8},{5,9},{6,10},{7,11},{8,4},{9,5},... | collective-permute-start | bytes 589832 | tf_op jit(solution)/shard_map/ppermute | solution.py:40
  15.6 12.3 %collective-permute-start.16 = (f32[384,128]{1,0:T(8,128)S(1)}, f32[384,128]{1,0:T(8,128)S(1)}, u32[]{:S(2)}, u32[]{:S(2)}) collective-permute-start(f32[384,128]{1,0:T(8,128)S(1)} %get-tuple-element.45), channel_id=1, source_target_pairs={{0,4},{1,5},{2,10},{3,11},{4,0},{5,1},{6,14},{7,15},{8,12},{9,13},... | collective-permute-start | bytes 589832 | tf_op jit(solution)/shard_map/ppermute | solution.py:40
  17.3 19.2 %collective-permute-start.15 = (f32[384,128]{1,0:T(8,128)S(1)}, f32[384,128]{1,0:T(8,128)S(1)}, u32[]{:S(2)}, u32[]{:S(2)}) collective-permute-start(f32[384,128]{1,0:T(8,128)S(1)} %get-tuple-element.44), channel_id=1, source_target_pairs={{0,4},{1,5},{2,10},{3,11},{4,0},{5,1},{6,14},{7,15},{8,12},{9,13},... | collective-permute-start | bytes 589832 | tf_op jit(solution)/shard_map/ppermute | solution.py:40
  25.1 9.9 %collective-permute-start.7 = (f32[384,128]{1,0:T(8,128)S(1)}, f32[384,128]{1,0:T(8,128)S(1)}, u32[]{:S(2)}, u32[]{:S(2)}) collective-permute-start(f32[384,128]{1,0:T(8,128)S(1)} %fusion.6), channel_id=1, source_target_pairs={{0,16},{1,17},{2,18},{3,19},{4,20},{5,21},{6,22},{7,23},{8,24},{9,... | collective-permute-start | bytes 589832 | tf_op jit(solution)/shard_map/ppermute | solution.py:40
  28.6 8.8 %collective-permute-start.17 = (f32[384,128]{1,0:T(8,128)S(1)}, f32[384,128]{1,0:T(8,128)S(1)}, u32[]{:S(2)}, u32[]{:S(2)}) collective-permute-start(f32[384,128]{1,0:T(8,128)S(1)} %convolution_add_fusion), channel_id=1, source_target_pairs={{0,8},{1,9},{2,6},{3,7},{4,12},{5,13},{6,2},{7,3},{8,0},{9,1},{10,... | collective-permute-start | bytes 589832 | tf_op jit(solution)/shard_map/ppermute | solution.py:40
  35.0 7.4 %collective-permute-start.8 = (f32[384,128]{1,0:T(8,128)S(1)}, f32[384,128]{1,0:T(8,128)S(1)}, u32[]{:S(2)}, u32[]{:S(2)}) collective-permute-start(f32[384,128]{1,0:T(8,128)S(1)} %add_multiply_fusion.1), channel_id=1, source_target_pairs={{0,8},{1,9},{2,6},{3,7},{4,12},{5,13},{6,2},{7,3},{8,0},{9,1},{10,... | collective-permute-start | bytes 589832 | tf_op jit(solution)/shard_map/ppermute | solution.py:40
  35.4 7.0 %collective-permute-start.9 = (f32[384,128]{1,0:T(8,128)S(1)}, f32[384,128]{1,0:T(8,128)}, u32[]{:S(2)}, u32[]{:S(2)}) collective-permute-start(f32[384,128]{1,0:T(8,128)S(1)} %add_multiply_fusion.1), channel_id=1, source_target_pairs={{0,4},{1,5},{2,10},{3,11},{4,0},{5,1},{6,14},{7,15},{8,12},{9,13},... | collective-permute-start | bytes 589832 | tf_op jit(solution)/shard_map/ppermute | solution.py:40
  38.0 8.7 %collective-permute-start.18 = (f32[384,128]{1,0:T(8,128)S(1)}, f32[384,128]{1,0:T(8,128)S(1)}, u32[]{:S(2)}, u32[]{:S(2)}) collective-permute-start(f32[384,128]{1,0:T(8,128)S(1)} %fusion.5), channel_id=1, source_target_pairs={{0,16},{1,17},{2,18},{3,19},{4,20},{5,21},{6,22},{7,23},{8,24},{9,... | collective-permute-start | bytes 589832 | tf_op jit(solution)/shard_map/ppermute | solution.py:40
  42.4 9.1 %collective-permute-start.10 = (f32[384,128]{1,0:T(8,128)S(1)}, f32[384,128]{1,0:T(8,128)}, u32[]{:S(2)}, u32[]{:S(2)}) collective-permute-start(f32[384,128]{1,0:T(8,128)S(1)} %collective-permute-done.8), channel_id=1, source_target_pairs={{0,4},{1,5},{2,10},{3,11},{4,0},{5,1},{6,14},{7,15},{8,12},{9,13},... | collective-permute-start | bytes 589832 | tf_op jit(solution)/shard_map/ppermute | solution.py:40
  46.8 8.4 %collective-permute-start.19 = (f32[384,128]{1,0:T(8,128)S(1)}, f32[384,128]{1,0:T(8,128)S(1)}, u32[]{:S(2)}, u32[]{:S(2)}) collective-permute-start(f32[384,128]{1,0:T(8,128)S(1)} %add_multiply_fusion), channel_id=1, source_target_pairs={{0,8},{1,9},{2,6},{3,7},{4,12},{5,13},{6,2},{7,3},{8,0},{9,1},{10,... | collective-permute-start | bytes 589832 | tf_op jit(solution)/shard_map/ppermute | solution.py:40
  50.0 7.8 %collective-permute-start.20 = (f32[384,128]{1,0:T(8,128)S(1)}, f32[384,128]{1,0:T(8,128)S(1)}, u32[]{:S(2)}, u32[]{:S(2)}) collective-permute-start(f32[384,128]{1,0:T(8,128)S(1)} %add_multiply_fusion), channel_id=1, source_target_pairs={{0,4},{1,5},{2,10},{3,11},{4,0},{5,1},{6,14},{7,15},{8,12},{9,13},... | collective-permute-start | bytes 589832 | tf_op jit(solution)/shard_map/ppermute | solution.py:40
  50.0 7.8 %collective-permute-start.21 = (f32[384,128]{1,0:T(8,128)S(1)}, f32[384,128]{1,0:T(8,128)S(1)}, u32[]{:S(2)}, u32[]{:S(2)}) collective-permute-start(f32[384,128]{1,0:T(8,128)S(1)} %add_multiply_fusion), channel_id=1, source_target_pairs={{0,12},{1,13},{2,14},{3,15},{4,8},{5,9},{6,10},{7,11},{8,4},{9,5},... | collective-permute-start | bytes 589832 | tf_op jit(solution)/shard_map/ppermute | solution.py:40
  53.7 7.2 %collective-permute-start.11 = (f32[192,128]{1,0:T(8,128)S(1)}, f32[192,128]{1,0:T(8,128)S(1)}, u32[]{:S(2)}, u32[]{:S(2)}) collective-permute-start(f32[192,128]{1,0:T(8,128)S(1)} %slice.75), channel_id=1, source_target_pairs={{0,1},{1,0},{2,3},{3,2},{4,5},{5,4},{6,7},{7,6},{8,9},{9,8},{10,11... | collective-permute-start | bytes 294920 | tf_op jit(solution)/shard_map/ppermute | solution.py:40
  59.0 4.2 %collective-permute-start.23 = (f32[96,128]{1,0:T(8,128)S(1)}, f32[96,128]{1,0:T(8,128)S(1)}, u32[]{:S(2)}, u32[]{:S(2)}) collective-permute-start(f32[96,128]{1,0:T(8,128)S(1)} %get-tuple-element.49), channel_id=1, source_target_pairs={{0,1},{1,0},{2,3},{3,2},{4,5},{5,4},{6,7},{7,6},{8,9},{9,8},{10,11... | collective-permute-start | bytes 147464 | tf_op jit(solution)/shard_map/ppermute | solution.py:40
  60.6 3.7 %collective-permute-start.24 = (f32[96,128]{1,0:T(8,128)S(1)}, f32[96,128]{1,0:T(8,128)S(1)}, u32[]{:S(2)}, u32[]{:S(2)}) collective-permute-start(f32[96,128]{1,0:T(8,128)S(1)} %get-tuple-element.48), channel_id=1, source_target_pairs={{0,3},{1,2},{2,1},{3,0},{4,7},{5,6},{6,5},{7,4},{8,11},{9,10},{10,... | collective-permute-start | bytes 147464 | tf_op jit(solution)/shard_map/ppermute | solution.py:40
  (3 other events, 11.2 us)

commit v6 on v5

--- a/solution.py
+++ b/solution.py
@@ -99,7 +99,7 @@
             mask *= 2
         fresh = total * (1.0 / half_width)
         if partials:
-            received = dict(zip(quarters, [exchange(fresh, masks, 0) for masks in partners]))
+            received = dict(zip(quarters, together([exchange(fresh, masks, 0) for masks in partners])))
             fresh = jnp.concatenate([fresh, received[1], received[2], received[3]], axis=0)
             fresh = after(fresh, partials[-1])
         else:

time: 65.3 us -> 64.7 us (level)
  no operation moved by 1% of the time
where the time goes in v6:
time: 64.7 us; the launch traced here: 64.5 us
  starting transfers between devices  33 us (51%)
  waiting for transfers between devices  19 us (29%)
  matrix products  7.95 us (12%)
  other arithmetic  2.85 us (4%)
  local copies, waits for them, and re-layouts  1.43 us (2%)
    ppermute x26, starting transfers between devices, exchange(): return lax.ppermute(block, ('row', 'col'), pairs)  33 us
    ppermute x26, waiting for transfers between devices, exchange(): return lax.ppermute(block, ('row', 'col'), pairs)  19 us
    dot_general x7, matrix products, product(): lax.dot_general(left, right, (((left_dim,), (0,)), ((), ())), precision=l...  7.95 us
    sub x1, other arithmetic, prepared(): block - jnp.where(on_diagonal, jnp.float32(center), jnp.float32(0.0))  1.57 us
  transfers between devices with their start and end apart: 26, of which 10 were waited for; matrix products, arithmetic and copies ran while one was open for 18% of the time, Pallas kernels for 0%

profile of v6, /device:TPU:0, one launch (start us, length us, event | category | flops | bytes accessed | tf_op | source)
XLA Modules:
  0.0 64.5 jit_solution(1112002570641058032)
XLA Ops:
  1.5 2.6 %collective-permute-start.3 = (f32[96,128]{1,0:T(8,128)S(1)}, f32[96,128]{1,0:T(8,128)S(1)}, u32[]{:S(2)}, u32[]{:S(2)}) collective-permute-start(f32[96,128]{1,0:T(8,128)S(1)} %get-tuple-element.59), channel_id=1, source_target_pairs={{0,3},{1,2},{2,1},{3,0},{4,7},{5,6},{6,5},{7,4},{8,11},{9,10},{10,... | collective-permute-start | bytes 147464 | tf_op jit(solution)/shard_map/ppermute | solution.py:40
  4.5 1.6 %select_subtract_fusion.1 = (f32[192,1536]{1,0:T(8,128)S(1)}, f32[192,1536]{1,0:T(8,128)S(1)}) fusion(f32[192,1536]{1,0:T(8,128)} %param.2, s32[1536]{0:T(1024)S(1)} %iota_add_fusion, s32[192]{0:T(256)S(1)} %iota_add_fusion.2, f32[192,1536]{1,0:T(8,128)S(1)} %collective-permute-done, s32[192]{0:T(256)S(1)} %iota_add_fusion.1), kind=kLoop, calls=%fused_computation.8 | loop fusion | flops 1769472 | bytes 4726272 | tf_op jit(solution)/shard_map/sub | solution.py:49
  7.1 1.7 %collective-permute-start.14 = (f32[96,128]{1,0:T(8,128)S(1)}, f32[96,128]{1,0:T(8,128)S(1)}, u32[]{:S(2)}, u32[]{:S(2)}) collective-permute-start(f32[96,128]{1,0:T(8,128)S(1)} %get-tuple-element.26), channel_id=1, source_target_pairs={{0,3},{1,2},{2,1},{3,0},{4,7},{5,6},{6,5},{7,4},{8,11},{9,10},{10,... | collective-permute-start | bytes 147464 | tf_op jit(solution)/shard_map/ppermute | solution.py:40
  9.2 1.6 %fusion = f32[1152,128]{1,0:T(8,128)S(1)} fusion(f32[384,1536]{1,0:T(8,128)S(1)} %pad_maximum_fusion, f32[96,128]{1,0:T(8,128)S(1)} %collective-permute-done.3, f32[96,128]{1,0:T(8,128)S(1)} %collective-permute-done.2, f32[96,128]{1,0:T(8,128)S(1)} %collective-permute-done.1, f32[96,128]{1,0:T(8,128)S(1)} %get-tuple-element.57), kind=kOutput, calls=%fused_computation.1 | convolution fusion | flops 339886080 | bytes 2555904 | tf_op jit(solution)/shard_map/dot_general | solution.py:14
  10.8 1.7 %collective-permute-start.4 = (f32[384,128]{1,0:T(8,128)S(1)}, f32[384,128]{1,0:T(8,128)S(1)}, u32[]{:S(2)}, u32[]{:S(2)}) collective-permute-start(f32[384,128]{1,0:T(8,128)S(1)} %get-tuple-element.49), channel_id=1, source_target_pairs={{0,4},{1,5},{2,10},{3,11},{4,0},{5,1},{6,14},{7,15},{8,12},{9,13},... | collective-permute-start | bytes 589832 | tf_op jit(solution)/shard_map/ppermute | solution.py:40
  12.5 1.6 %collective-permute-start.5 = (f32[384,128]{1,0:T(8,128)S(1)}, f32[384,128]{1,0:T(8,128)S(1)}, u32[]{:S(2)}, u32[]{:S(2)}) collective-permute-start(f32[384,128]{1,0:T(8,128)S(1)} %get-tuple-element.48), channel_id=1, source_target_pairs={{0,8},{1,9},{2,6},{3,7},{4,12},{5,13},{6,2},{7,3},{8,0},{9,1},{10,... | collective-permute-start | bytes 589832 | tf_op jit(solution)/shard_map/ppermute | solution.py:40
  14.4 1.2 %fusion.2 = f32[768,128]{1,0:T(8,128)S(1)} fusion(f32[384,128]{1,0:T(8,128)S(1)} %pad_maximum_fusion.5, f32[384,1536]{1,0:T(8,128)S(1)} %pad_maximum_fusion), kind=kOutput, calls=%fused_computation.3 | convolution fusion | flops 226492416 | bytes 1769472 | tf_op jit(solution)/shard_map/dot_general | solution.py:14
  15.6 1.7 %collective-permute-start.16 = (f32[384,128]{1,0:T(8,128)S(1)}, f32[384,128]{1,0:T(8,128)S(1)}, u32[]{:S(2)}, u32[]{:S(2)}) collective-permute-start(f32[384,128]{1,0:T(8,128)S(1)} %get-tuple-element.51), channel_id=1, source_target_pairs={{0,4},{1,5},{2,10},{3,11},{4,0},{5,1},{6,14},{7,15},{8,12},{9,13},... | collective-permute-start | bytes 589832 | tf_op jit(solution)/shard_map/ppermute | solution.py:40
  17.7 2.0 %collective-permute-done.4 = f32[384,128]{1,0:T(8,128)S(1)} collective-permute-done((f32[384,128]{1,0:T(8,128)S(1)}, f32[384,128]{1,0:T(8,128)S(1)}, u32[]{:S(2)}, u32[]{:S(2)}) %collective-permute-start.4) | collective-permute-done | bytes 196640 | tf_op jit(solution)/shard_map/ppermute | solution.py:40
  20.3 4.1 %collective-permute-done.6 = f32[384,128]{1,0:T(8,128)S(1)} collective-permute-done((f32[384,128]{1,0:T(8,128)S(1)}, f32[384,128]{1,0:T(8,128)S(1)}, u32[]{:S(2)}, u32[]{:S(2)}) %collective-permute-start.6) | collective-permute-done | bytes 196640 | tf_op jit(solution)/shard_map/ppermute | solution.py:40
  25.1 2.8 %collective-permute-start.7 = (f32[384,128]{1,0:T(8,128)S(1)}, f32[384,128]{1,0:T(8,128)S(1)}, u32[]{:S(2)}, u32[]{:S(2)}) collective-permute-start(f32[384,128]{1,0:T(8,128)S(1)} %fusion.6), channel_id=1, source_target_pairs={{0,16},{1,17},{2,18},{3,19},{4,20},{5,21},{6,22},{7,23},{8,24},{9,... | collective-permute-start | bytes 589832 | tf_op jit(solution)/shard_map/ppermute | solution.py:40
  28.6 3.7 %collective-permute-start.17 = (f32[384,128]{1,0:T(8,128)S(1)}, f32[384,128]{1,0:T(8,128)S(1)}, u32[]{:S(2)}, u32[]{:S(2)}) collective-permute-start(f32[384,128]{1,0:T(8,128)S(1)} %convolution_add_fusion), channel_id=1, source_target_pairs={{0,8},{1,9},{2,6},{3,7},{4,12},{5,13},{6,2},{7,3},{8,0},{9,1},{10,... | collective-permute-start | bytes 589832 | tf_op jit(solution)/shard_map/ppermute | solution.py:40
  32.3 2.7 %collective-permute-done.7 = f32[384,128]{1,0:T(8,128)S(1)} collective-permute-done((f32[384,128]{1,0:T(8,128)S(1)}, f32[384,128]{1,0:T(8,128)S(1)}, u32[]{:S(2)}, u32[]{:S(2)}) %collective-permute-start.7) | collective-permute-done | bytes 196640 | tf_op jit(solution)/shard_map/ppermute | solution.py:40
  38.0 3.4 %collective-permute-start.18 = (f32[384,128]{1,0:T(8,128)S(1)}, f32[384,128]{1,0:T(8,128)S(1)}, u32[]{:S(2)}, u32[]{:S(2)}) collective-permute-start(f32[384,128]{1,0:T(8,128)S(1)} %fusion.5), channel_id=1, source_target_pairs={{0,16},{1,17},{2,18},{3,19},{4,20},{5,21},{6,22},{7,23},{8,24},{9,... | collective-permute-start | bytes 589832 | tf_op jit(solution)/shard_map/ppermute | solution.py:40
  42.4 1.6 %collective-permute-start.10 = (f32[384,128]{1,0:T(8,128)S(1)}, f32[384,128]{1,0:T(8,128)}, u32[]{:S(2)}, u32[]{:S(2)}) collective-permute-start(f32[384,128]{1,0:T(8,128)S(1)} %collective-permute-done.8), channel_id=1, source_target_pairs={{0,4},{1,5},{2,10},{3,11},{4,0},{5,1},{6,14},{7,15},{8,12},{9,13},... | collective-permute-start | bytes 589832 | tf_op jit(solution)/shard_map/ppermute | solution.py:40
  44.0 2.8 %collective-permute-done.18 = f32[384,128]{1,0:T(8,128)S(1)} collective-permute-done((f32[384,128]{1,0:T(8,128)S(1)}, f32[384,128]{1,0:T(8,128)S(1)}, u32[]{:S(2)}, u32[]{:S(2)}) %collective-permute-start.18) | collective-permute-done | bytes 196640 | tf_op jit(solution)/shard_map/ppermute | solution.py:40
  46.8 1.7 %collective-permute-start.19 = (f32[384,128]{1,0:T(8,128)S(1)}, f32[384,128]{1,0:T(8,128)S(1)}, u32[]{:S(2)}, u32[]{:S(2)}) collective-permute-start(f32[384,128]{1,0:T(8,128)S(1)} %add_multiply_fusion), channel_id=1, source_target_pairs={{0,4},{1,5},{2,10},{3,11},{4,0},{5,1},{6,14},{7,15},{8,12},{9,13},... | collective-permute-start | bytes 589832 | tf_op jit(solution)/shard_map/ppermute | solution.py:40
  48.5 1.6 %collective-permute-start.20 = (f32[384,128]{1,0:T(8,128)S(1)}, f32[384,128]{1,0:T(8,128)S(1)}, u32[]{:S(2)}, u32[]{:S(2)}) collective-permute-start(f32[384,128]{1,0:T(8,128)S(1)} %add_multiply_fusion), channel_id=1, source_target_pairs={{0,8},{1,9},{2,6},{3,7},{4,12},{5,13},{6,2},{7,3},{8,0},{9,1},{10,... | collective-permute-start | bytes 589832 | tf_op jit(solution)/shard_map/ppermute | solution.py:40
  50.1 1.4 %collective-permute-start.21 = (f32[384,128]{1,0:T(8,128)S(1)}, f32[384,128]{1,0:T(8,128)S(1)}, u32[]{:S(2)}, u32[]{:S(2)}) collective-permute-start(f32[384,128]{1,0:T(8,128)S(1)} %add_multiply_fusion), channel_id=1, source_target_pairs={{0,12},{1,13},{2,14},{3,15},{4,8},{5,9},{6,10},{7,11},{8,4},{9,5},... | collective-permute-start | bytes 589832 | tf_op jit(solution)/shard_map/ppermute | solution.py:40
  51.4 2.1 %fusion.7 = f32[384,128]{1,0:T(8,128)S(1)} fusion(f32[384,128]{1,0:T(8,128)} %collective-permute-done.10, f32[384,128]{1,0:T(8,128)} %collective-permute-done.9, f32[384,128]{1,0:T(8,128)S(1)} %collective-permute-done.8, f32[384,128]{1,0:T(8,128)S(1)} %add_multiply_fusion.1, f32[96,1536]{1,0:T(8,128)S(1)} %get-tuple-element.38, ...), kind=kOutput, calls=%fused_computation.15 | convolution fusion | flops 455344128 | bytes 3342336 | tf_op jit(solution)/shard_map/dot_general | solution.py:14
  53.6 1.6 %collective-permute-start.11 = (f32[192,128]{1,0:T(8,128)S(1)}, f32[192,128]{1,0:T(8,128)S(1)}, u32[]{:S(2)}, u32[]{:S(2)}) collective-permute-start(f32[192,128]{1,0:T(8,128)S(1)} %slice.75), channel_id=1, source_target_pairs={{0,1},{1,0},{2,3},{3,2},{4,5},{5,4},{6,7},{7,6},{8,9},{9,8},{10,11... | collective-permute-start | bytes 294920 | tf_op jit(solution)/shard_map/ppermute | solution.py:40
  55.1 2.1 %collective-permute-done.21 = f32[384,128]{1,0:T(8,128)S(1)} collective-permute-done((f32[384,128]{1,0:T(8,128)S(1)}, f32[384,128]{1,0:T(8,128)S(1)}, u32[]{:S(2)}, u32[]{:S(2)}) %collective-permute-start.21) | collective-permute-done | bytes 196640 | tf_op jit(solution)/shard_map/ppermute | solution.py:40
  58.5 1.6 %collective-permute-start.23 = (f32[96,128]{1,0:T(8,128)S(1)}, f32[96,128]{1,0:T(8,128)S(1)}, u32[]{:S(2)}, u32[]{:S(2)}) collective-permute-start(f32[96,128]{1,0:T(8,128)S(1)} %get-tuple-element.55), channel_id=1, source_target_pairs={{0,1},{1,0},{2,3},{3,2},{4,5},{5,4},{6,7},{7,6},{8,9},{9,8},{10,11... | collective-permute-start | bytes 147464 | tf_op jit(solution)/shard_map/ppermute | solution.py:40
  60.8 1.8 %collective-permute-done.23 = f32[96,128]{1,0:T(8,128)S(1)} collective-permute-done((f32[96,128]{1,0:T(8,128)S(1)}, f32[96,128]{1,0:T(8,128)S(1)}, u32[]{:S(2)}, u32[]{:S(2)}) %collective-permute-start.23) | collective-permute-done | bytes 49184 | tf_op jit(solution)/shard_map/ppermute | solution.py:40
  (62 shorter events, 13.8 us)
Async XLA Ops:
  0.0 4.5 %collective-permute-start = (f32[192,1536]{1,0:T(8,128)}, f32[192,1536]{1,0:T(8,128)S(1)}, u32[]{:S(2)}, u32[]{:S(2)}) collective-permute-start(f32[192,1536]{1,0:T(8,128)} %param.2), channel_id=1, source_target_pairs={{0,2},{1,3},{2,0},{3,1},{4,6},{5,7},{6,4},{7,5},{8,10},{9,11},{10,... | collective-permute-start | bytes 3538952 | tf_op jit(solution)/shard_map/ppermute | solution.py:40
  1.3 7.4 %collective-permute-start.1 = (f32[96,128]{1,0:T(8,128)S(1)}, f32[96,128]{1,0:T(8,128)S(1)}, u32[]{:S(2)}, u32[]{:S(2)}) collective-permute-start(f32[96,128]{1,0:T(8,128)S(1)} %get-tuple-element.59), channel_id=1, source_target_pairs={{0,2},{1,3},{2,0},{3,1},{4,6},{5,7},{6,4},{7,5},{8,10},{9,11},{10,... | collective-permute-start | bytes 147464 | tf_op jit(solution)/shard_map/ppermute | solution.py:40
  1.5 7.7 %collective-permute-start.3 = (f32[96,128]{1,0:T(8,128)S(1)}, f32[96,128]{1,0:T(8,128)S(1)}, u32[]{:S(2)}, u32[]{:S(2)}) collective-permute-start(f32[96,128]{1,0:T(8,128)S(1)} %get-tuple-element.59), channel_id=1, source_target_pairs={{0,3},{1,2},{2,1},{3,0},{4,7},{5,6},{6,5},{7,4},{8,11},{9,10},{10,... | collective-permute-start | bytes 147464 | tf_op jit(solution)/shard_map/ppermute | solution.py:40
  4.1 5.1 %collective-permute-start.2 = (f32[96,128]{1,0:T(8,128)S(1)}, f32[96,128]{1,0:T(8,128)S(1)}, u32[]{:S(2)}, u32[]{:S(2)}) collective-permute-start(f32[96,128]{1,0:T(8,128)S(1)} %get-tuple-element.57), channel_id=1, source_target_pairs={{0,1},{1,0},{2,3},{3,2},{4,5},{5,4},{6,7},{7,6},{8,9},{9,8},{10,11... | collective-permute-start | bytes 147464 | tf_op jit(solution)/shard_map/ppermute | solution.py:40
  6.9 7.2 %collective-permute-start.12 = (f32[96,128]{1,0:T(8,128)S(1)}, f32[96,128]{1,0:T(8,128)S(1)}, u32[]{:S(2)}, u32[]{:S(2)}) collective-permute-start(f32[96,128]{1,0:T(8,128)S(1)} %get-tuple-element.26), channel_id=1, source_target_pairs={{0,2},{1,3},{2,0},{3,1},{4,6},{5,7},{6,4},{7,5},{8,10},{9,11},{10,... | collective-permute-start | bytes 147464 | tf_op jit(solution)/shard_map/ppermute | solution.py:40
  7.1 7.3 %collective-permute-start.14 = (f32[96,128]{1,0:T(8,128)S(1)}, f32[96,128]{1,0:T(8,128)S(1)}, u32[]{:S(2)}, u32[]{:S(2)}) collective-permute-start(f32[96,128]{1,0:T(8,128)S(1)} %get-tuple-element.26), channel_id=1, source_target_pairs={{0,3},{1,2},{2,1},{3,0},{4,7},{5,6},{6,5},{7,4},{8,11},{9,10},{10,... | collective-permute-start | bytes 147464 | tf_op jit(solution)/shard_map/ppermute | solution.py:40
  8.8 5.6 %collective-permute-start.13 = (f32[96,128]{1,0:T(8,128)S(1)}, f32[96,128]{1,0:T(8,128)S(1)}, u32[]{:S(2)}, u32[]{:S(2)}) collective-permute-start(f32[96,128]{1,0:T(8,128)S(1)} %get-tuple-element.25), channel_id=1, source_target_pairs={{0,1},{1,0},{2,3},{3,2},{4,5},{5,4},{6,7},{7,6},{8,9},{9,8},{10,11... | collective-permute-start | bytes 147464 | tf_op jit(solution)/shard_map/ppermute | solution.py:40
  10.8 8.8 %collective-permute-start.4 = (f32[384,128]{1,0:T(8,128)S(1)}, f32[384,128]{1,0:T(8,128)S(1)}, u32[]{:S(2)}, u32[]{:S(2)}) collective-permute-start(f32[384,128]{1,0:T(8,128)S(1)} %get-tuple-element.49), channel_id=1, source_target_pairs={{0,4},{1,5},{2,10},{3,11},{4,0},{5,1},{6,14},{7,15},{8,12},{9,13},... | collective-permute-start | bytes 589832 | tf_op jit(solution)/shard_map/ppermute | solution.py:40
  12.5 7.8 %collective-permute-start.5 = (f32[384,128]{1,0:T(8,128)S(1)}, f32[384,128]{1,0:T(8,128)S(1)}, u32[]{:S(2)}, u32[]{:S(2)}) collective-permute-start(f32[384,128]{1,0:T(8,128)S(1)} %get-tuple-element.48), channel_id=1, source_target_pairs={{0,8},{1,9},{2,6},{3,7},{4,12},{5,13},{6,2},{7,3},{8,0},{9,1},{10,... | collective-permute-start | bytes 589832 | tf_op jit(solution)/shard_map/ppermute | solution.py:40
  14.1 10.3 %collective-permute-start.6 = (f32[384,128]{1,0:T(8,128)S(1)}, f32[384,128]{1,0:T(8,128)S(1)}, u32[]{:S(2)}, u32[]{:S(2)}) collective-permute-start(f32[384,128]{1,0:T(8,128)S(1)} %get-tuple-element.47), channel_id=1, source_target_pairs={{0,12},{1,13},{2,14},{3,15},{4,8},{5,9},{6,10},{7,11},{8,4},{9,5},... | collective-permute-start | bytes 589832 | tf_op jit(solution)/shard_map/ppermute | solution.py:40
  15.6 12.3 %collective-permute-start.16 = (f32[384,128]{1,0:T(8,128)S(1)}, f32[384,128]{1,0:T(8,128)S(1)}, u32[]{:S(2)}, u32[]{:S(2)}) collective-permute-start(f32[384,128]{1,0:T(8,128)S(1)} %get-tuple-element.51), channel_id=1, source_target_pairs={{0,4},{1,5},{2,10},{3,11},{4,0},{5,1},{6,14},{7,15},{8,12},{9,13},... | collective-permute-start | bytes 589832 | tf_op jit(solution)/shard_map/ppermute | solution.py:40
  17.3 19.2 %collective-permute-start.15 = (f32[384,128]{1,0:T(8,128)S(1)}, f32[384,128]{1,0:T(8,128)S(1)}, u32[]{:S(2)}, u32[]{:S(2)}) collective-permute-start(f32[384,128]{1,0:T(8,128)S(1)} %get-tuple-element.50), channel_id=1, source_target_pairs={{0,4},{1,5},{2,10},{3,11},{4,0},{5,1},{6,14},{7,15},{8,12},{9,13},... | collective-permute-start | bytes 589832 | tf_op jit(solution)/shard_map/ppermute | solution.py:40
  25.1 9.9 %collective-permute-start.7 = (f32[384,128]{1,0:T(8,128)S(1)}, f32[384,128]{1,0:T(8,128)S(1)}, u32[]{:S(2)}, u32[]{:S(2)}) collective-permute-start(f32[384,128]{1,0:T(8,128)S(1)} %fusion.6), channel_id=1, source_target_pairs={{0,16},{1,17},{2,18},{3,19},{4,20},{5,21},{6,22},{7,23},{8,24},{9,... | collective-permute-start | bytes 589832 | tf_op jit(solution)/shard_map/ppermute | solution.py:40
  28.6 8.8 %collective-permute-start.17 = (f32[384,128]{1,0:T(8,128)S(1)}, f32[384,128]{1,0:T(8,128)S(1)}, u32[]{:S(2)}, u32[]{:S(2)}) collective-permute-start(f32[384,128]{1,0:T(8,128)S(1)} %convolution_add_fusion), channel_id=1, source_target_pairs={{0,8},{1,9},{2,6},{3,7},{4,12},{5,13},{6,2},{7,3},{8,0},{9,1},{10,... | collective-permute-start | bytes 589832 | tf_op jit(solution)/shard_map/ppermute | solution.py:40
  35.0 7.4 %collective-permute-start.8 = (f32[384,128]{1,0:T(8,128)S(1)}, f32[384,128]{1,0:T(8,128)S(1)}, u32[]{:S(2)}, u32[]{:S(2)}) collective-permute-start(f32[384,128]{1,0:T(8,128)S(1)} %add_multiply_fusion.1), channel_id=1, source_target_pairs={{0,8},{1,9},{2,6},{3,7},{4,12},{5,13},{6,2},{7,3},{8,0},{9,1},{10,... | collective-permute-start | bytes 589832 | tf_op jit(solution)/shard_map/ppermute | solution.py:40
  35.4 7.0 %collective-permute-start.9 = (f32[384,128]{1,0:T(8,128)S(1)}, f32[384,128]{1,0:T(8,128)}, u32[]{:S(2)}, u32[]{:S(2)}) collective-permute-start(f32[384,128]{1,0:T(8,128)S(1)} %add_multiply_fusion.1), channel_id=1, source_target_pairs={{0,4},{1,5},{2,10},{3,11},{4,0},{5,1},{6,14},{7,15},{8,12},{9,13},... | collective-permute-start | bytes 589832 | tf_op jit(solution)/shard_map/ppermute | solution.py:40
  38.0 8.7 %collective-permute-start.18 = (f32[384,128]{1,0:T(8,128)S(1)}, f32[384,128]{1,0:T(8,128)S(1)}, u32[]{:S(2)}, u32[]{:S(2)}) collective-permute-start(f32[384,128]{1,0:T(8,128)S(1)} %fusion.5), channel_id=1, source_target_pairs={{0,16},{1,17},{2,18},{3,19},{4,20},{5,21},{6,22},{7,23},{8,24},{9,... | collective-permute-start | bytes 589832 | tf_op jit(solution)/shard_map/ppermute | solution.py:40
  42.4 9.0 %collective-permute-start.10 = (f32[384,128]{1,0:T(8,128)S(1)}, f32[384,128]{1,0:T(8,128)}, u32[]{:S(2)}, u32[]{:S(2)}) collective-permute-start(f32[384,128]{1,0:T(8,128)S(1)} %collective-permute-done.8), channel_id=1, source_target_pairs={{0,4},{1,5},{2,10},{3,11},{4,0},{5,1},{6,14},{7,15},{8,12},{9,13},... | collective-permute-start | bytes 589832 | tf_op jit(solution)/shard_map/ppermute | solution.py:40
  46.8 8.3 %collective-permute-start.19 = (f32[384,128]{1,0:T(8,128)S(1)}, f32[384,128]{1,0:T(8,128)S(1)}, u32[]{:S(2)}, u32[]{:S(2)}) collective-permute-start(f32[384,128]{1,0:T(8,128)S(1)} %add_multiply_fusion), channel_id=1, source_target_pairs={{0,4},{1,5},{2,10},{3,11},{4,0},{5,1},{6,14},{7,15},{8,12},{9,13},... | collective-permute-start | bytes 589832 | tf_op jit(solution)/shard_map/ppermute | solution.py:40
  48.5 6.7 %collective-permute-start.20 = (f32[384,128]{1,0:T(8,128)S(1)}, f32[384,128]{1,0:T(8,128)S(1)}, u32[]{:S(2)}, u32[]{:S(2)}) collective-permute-start(f32[384,128]{1,0:T(8,128)S(1)} %add_multiply_fusion), channel_id=1, source_target_pairs={{0,8},{1,9},{2,6},{3,7},{4,12},{5,13},{6,2},{7,3},{8,0},{9,1},{10,... | collective-permute-start | bytes 589832 | tf_op jit(solution)/shard_map/ppermute | solution.py:40
  50.1 7.1 %collective-permute-start.21 = (f32[384,128]{1,0:T(8,128)S(1)}, f32[384,128]{1,0:T(8,128)S(1)}, u32[]{:S(2)}, u32[]{:S(2)}) collective-permute-start(f32[384,128]{1,0:T(8,128)S(1)} %add_multiply_fusion), channel_id=1, source_target_pairs={{0,12},{1,13},{2,14},{3,15},{4,8},{5,9},{6,10},{7,11},{8,4},{9,5},... | collective-permute-start | bytes 589832 | tf_op jit(solution)/shard_map/ppermute | solution.py:40
  53.6 6.8 %collective-permute-start.11 = (f32[192,128]{1,0:T(8,128)S(1)}, f32[192,128]{1,0:T(8,128)S(1)}, u32[]{:S(2)}, u32[]{:S(2)}) collective-permute-start(f32[192,128]{1,0:T(8,128)S(1)} %slice.75), channel_id=1, source_target_pairs={{0,1},{1,0},{2,3},{3,2},{4,5},{5,4},{6,7},{7,6},{8,9},{9,8},{10,11... | collective-permute-start | bytes 294920 | tf_op jit(solution)/shard_map/ppermute | solution.py:40
  58.5 4.2 %collective-permute-start.23 = (f32[96,128]{1,0:T(8,128)S(1)}, f32[96,128]{1,0:T(8,128)S(1)}, u32[]{:S(2)}, u32[]{:S(2)}) collective-permute-start(f32[96,128]{1,0:T(8,128)S(1)} %get-tuple-element.55), channel_id=1, source_target_pairs={{0,1},{1,0},{2,3},{3,2},{4,5},{5,4},{6,7},{7,6},{8,9},{9,8},{10,11... | collective-permute-start | bytes 147464 | tf_op jit(solution)/shard_map/ppermute | solution.py:40
  60.0 3.7 %collective-permute-start.24 = (f32[96,128]{1,0:T(8,128)S(1)}, f32[96,128]{1,0:T(8,128)S(1)}, u32[]{:S(2)}, u32[]{:S(2)}) collective-permute-start(f32[96,128]{1,0:T(8,128)S(1)} %get-tuple-element.54), channel_id=1, source_target_pairs={{0,3},{1,2},{2,1},{3,0},{4,7},{5,6},{6,5},{7,4},{8,11},{9,10},{10,... | collective-permute-start | bytes 147464 | tf_op jit(solution)/shard_map/ppermute | solution.py:40
  (3 other events, 11.2 us)

commit v7 on v6

--- a/solution.py
+++ b/solution.py
@@ -81,7 +81,8 @@
             crossed = exchange(given[quarter:], partners[0], 0)
             straight = exchange(given[:quarter], partners[0], 0)
             passed = product(matrix[:, quarter : 2 * quarter], chunk, 0) + crossed
-            total = product(matrix[:, :quarter], chunk, 0) + straight + exchange(passed, partners[1], 0)
+            straight, passed = together([straight, exchange(passed, partners[1], 0)])
+            total = product(matrix[:, :quarter], chunk, 0) + straight + passed
         else:
             given = product(matrix[:, quarter:], chunk, 0)
             sent = [given[(i - 1) * quarter : i * quarter] for i in quarters]

time: 64.7 us -> 65.2 us (level)
  waiting for transfers between devices: 19 us -> 22.4 us
  starting transfers between devices: 33 us -> 30.1 us
    ppermute x26, waiting for transfers between devices: 19 us -> 22.4 us  [exchange(): return lax.ppermute(block, ('row', 'col'), pairs)]
    ppermute x26, starting transfers between devices: 33 us -> 30.1 us  [exchange(): return lax.ppermute(block, ('row', 'col'), pairs)]
where the time goes in v7:
time: 65.2 us; the launch traced here: 65 us
  starting transfers between devices  30.1 us (46%)
  waiting for transfers between devices  22.4 us (34%)
  matrix products  7.94 us (12%)
  other arithmetic  2.88 us (4%)
  local copies, waits for them, and re-layouts  1.44 us (2%)
    ppermute x26, starting transfers between devices, exchange(): return lax.ppermute(block, ('row', 'col'), pairs)  30.1 us
    ppermute x26, waiting for transfers between devices, exchange(): return lax.ppermute(block, ('row', 'col'), pairs)  22.4 us
    dot_general x7, matrix products, product(): lax.dot_general(left, right, (((left_dim,), (0,)), ((), ())), precision=l...  7.94 us
    sub x1, other arithmetic, prepared(): block - jnp.where(on_diagonal, jnp.float32(center), jnp.float32(0.0))  1.57 us
  transfers between devices with their start and end apart: 26, of which 10 were waited for; matrix products, arithmetic and copies ran while one was open for 18% of the time, Pallas kernels for 0%

profile of v7, /device:TPU:0, one launch (start us, length us, event | category | flops | bytes accessed | tf_op | source)
XLA Modules:
  0.0 65.0 jit_solution(10007537387915002612)
XLA Ops:
  1.5 2.6 %collective-permute-start.3 = (f32[96,128]{1,0:T(8,128)S(1)}, f32[96,128]{1,0:T(8,128)S(1)}, u32[]{:S(2)}, u32[]{:S(2)}) collective-permute-start(f32[96,128]{1,0:T(8,128)S(1)} %get-tuple-element.63), channel_id=1, source_target_pairs={{0,3},{1,2},{2,1},{3,0},{4,7},{5,6},{6,5},{7,4},{8,11},{9,10},{10,... | collective-permute-start | bytes 147464 | tf_op jit(solution)/shard_map/ppermute | solution.py:40
  4.5 1.6 %select_subtract_fusion.1 = (f32[192,1536]{1,0:T(8,128)S(1)}, f32[192,1536]{1,0:T(8,128)S(1)}) fusion(f32[192,1536]{1,0:T(8,128)} %param.2, s32[1536]{0:T(1024)S(1)} %iota_add_fusion, s32[192]{0:T(256)S(1)} %iota_add_fusion.2, f32[192,1536]{1,0:T(8,128)S(1)} %collective-permute-done, s32[192]{0:T(256)S(1)} %iota_add_fusion.1), kind=kLoop, calls=%fused_computation.8 | loop fusion | flops 1769472 | bytes 4726272 | tf_op jit(solution)/shard_map/sub | solution.py:49
  7.1 1.7 %collective-permute-start.14 = (f32[96,128]{1,0:T(8,128)S(1)}, f32[96,128]{1,0:T(8,128)S(1)}, u32[]{:S(2)}, u32[]{:S(2)}) collective-permute-start(f32[96,128]{1,0:T(8,128)S(1)} %get-tuple-element.28), channel_id=1, source_target_pairs={{0,3},{1,2},{2,1},{3,0},{4,7},{5,6},{6,5},{7,4},{8,11},{9,10},{10,... | collective-permute-start | bytes 147464 | tf_op jit(solution)/shard_map/ppermute | solution.py:40
  9.2 1.6 %fusion = f32[1152,128]{1,0:T(8,128)S(1)} fusion(f32[384,1536]{1,0:T(8,128)S(1)} %pad_maximum_fusion, f32[96,128]{1,0:T(8,128)S(1)} %collective-permute-done.3, f32[96,128]{1,0:T(8,128)S(1)} %collective-permute-done.2, f32[96,128]{1,0:T(8,128)S(1)} %collective-permute-done.1, f32[96,128]{1,0:T(8,128)S(1)} %get-tuple-element.61), kind=kOutput, calls=%fused_computation.1 | convolution fusion | flops 339886080 | bytes 2555904 | tf_op jit(solution)/shard_map/dot_general | solution.py:14
  10.8 1.7 %collective-permute-start.4 = (f32[384,128]{1,0:T(8,128)S(1)}, f32[384,128]{1,0:T(8,128)S(1)}, u32[]{:S(2)}, u32[]{:S(2)}) collective-permute-start(f32[384,128]{1,0:T(8,128)S(1)} %get-tuple-element.53), channel_id=1, source_target_pairs={{0,4},{1,5},{2,10},{3,11},{4,0},{5,1},{6,14},{7,15},{8,12},{9,13},... | collective-permute-start | bytes 589832 | tf_op jit(solution)/shard_map/ppermute | solution.py:40
  12.5 1.6 %collective-permute-start.5 = (f32[384,128]{1,0:T(8,128)S(1)}, f32[384,128]{1,0:T(8,128)S(1)}, u32[]{:S(2)}, u32[]{:S(2)}) collective-permute-start(f32[384,128]{1,0:T(8,128)S(1)} %get-tuple-element.52), channel_id=1, source_target_pairs={{0,8},{1,9},{2,6},{3,7},{4,12},{5,13},{6,2},{7,3},{8,0},{9,1},{10,... | collective-permute-start | bytes 589832 | tf_op jit(solution)/shard_map/ppermute | solution.py:40
  14.4 1.2 %fusion.2 = f32[768,128]{1,0:T(8,128)S(1)} fusion(f32[384,128]{1,0:T(8,128)S(1)} %pad_maximum_fusion.5, f32[384,1536]{1,0:T(8,128)S(1)} %pad_maximum_fusion), kind=kOutput, calls=%fused_computation.3 | convolution fusion | flops 226492416 | bytes 1769472 | tf_op jit(solution)/shard_map/dot_general | solution.py:14
  15.6 1.7 %collective-permute-start.16 = (f32[384,128]{1,0:T(8,128)S(1)}, f32[384,128]{1,0:T(8,128)S(1)}, u32[]{:S(2)}, u32[]{:S(2)}) collective-permute-start(f32[384,128]{1,0:T(8,128)S(1)} %get-tuple-element.54), channel_id=1, source_target_pairs={{0,4},{1,5},{2,10},{3,11},{4,0},{5,1},{6,14},{7,15},{8,12},{9,13},... | collective-permute-start | bytes 589832 | tf_op jit(solution)/shard_map/ppermute | solution.py:40
  18.4 1.3 %collective-permute-done.4 = f32[384,128]{1,0:T(8,128)S(1)} collective-permute-done((f32[384,128]{1,0:T(8,128)S(1)}, f32[384,128]{1,0:T(8,128)S(1)}, u32[]{:S(2)}, u32[]{:S(2)}) %collective-permute-start.4) | collective-permute-done | bytes 196640 | tf_op jit(solution)/shard_map/ppermute | solution.py:40
  20.3 4.1 %collective-permute-done.6 = f32[384,128]{1,0:T(8,128)S(1)} collective-permute-done((f32[384,128]{1,0:T(8,128)S(1)}, f32[384,128]{1,0:T(8,128)S(1)}, u32[]{:S(2)}, u32[]{:S(2)}) %collective-permute-start.6) | collective-permute-done | bytes 196640 | tf_op jit(solution)/shard_map/ppermute | solution.py:40
  25.1 2.8 %collective-permute-start.7 = (f32[384,128]{1,0:T(8,128)S(1)}, f32[384,128]{1,0:T(8,128)S(1)}, u32[]{:S(2)}, u32[]{:S(2)}) collective-permute-start(f32[384,128]{1,0:T(8,128)S(1)} %fusion.5), channel_id=1, source_target_pairs={{0,16},{1,17},{2,18},{3,19},{4,20},{5,21},{6,22},{7,23},{8,24},{9,... | collective-permute-start | bytes 589832 | tf_op jit(solution)/shard_map/ppermute | solution.py:40
  28.6 3.7 %collective-permute-start.17 = (f32[384,128]{1,0:T(8,128)S(1)}, f32[384,128]{1,0:T(8,128)S(1)}, u32[]{:S(2)}, u32[]{:S(2)}) collective-permute-start(f32[384,128]{1,0:T(8,128)S(1)} %convolution_add_fusion), channel_id=1, source_target_pairs={{0,8},{1,9},{2,6},{3,7},{4,12},{5,13},{6,2},{7,3},{8,0},{9,1},{10,... | collective-permute-start | bytes 589832 | tf_op jit(solution)/shard_map/ppermute | solution.py:40
  32.3 2.7 %collective-permute-done.7 = f32[384,128]{1,0:T(8,128)S(1)} collective-permute-done((f32[384,128]{1,0:T(8,128)S(1)}, f32[384,128]{1,0:T(8,128)S(1)}, u32[]{:S(2)}, u32[]{:S(2)}) %collective-permute-start.7) | collective-permute-done | bytes 196640 | tf_op jit(solution)/shard_map/ppermute | solution.py:40
  36.6 2.9 %collective-permute-done.17 = f32[384,128]{1,0:T(8,128)S(1)} collective-permute-done((f32[384,128]{1,0:T(8,128)S(1)}, f32[384,128]{1,0:T(8,128)S(1)}, u32[]{:S(2)}, u32[]{:S(2)}) %collective-permute-start.17) | collective-permute-done | bytes 196640 | tf_op jit(solution)/shard_map/ppermute | solution.py:40
  39.5 1.6 %collective-permute-start.18 = (f32[384,128]{1,0:T(8,128)S(1)}, f32[384,128]{1,0:T(8,128)S(1)}, u32[]{:S(2)}, u32[]{:S(2)}) collective-permute-start(f32[384,128]{1,0:T(8,128)S(1)} %add_add_fusion), channel_id=1, source_target_pairs={{0,16},{1,17},{2,18},{3,19},{4,20},{5,21},{6,22},{7,23},{8,24},{9,... | collective-permute-start | bytes 589832 | tf_op jit(solution)/shard_map/ppermute | solution.py:40
  41.1 1.3 %collective-permute-done.8 = f32[384,128]{1,0:T(8,128)S(1)} collective-permute-done((f32[384,128]{1,0:T(8,128)S(1)}, f32[384,128]{1,0:T(8,128)S(1)}, u32[]{:S(2)}, u32[]{:S(2)}) %collective-permute-start.8) | collective-permute-done | bytes 196640 | tf_op jit(solution)/shard_map/ppermute | solution.py:40
  42.4 1.6 %collective-permute-start.10 = (f32[384,128]{1,0:T(8,128)S(1)}, f32[384,128]{1,0:T(8,128)}, u32[]{:S(2)}, u32[]{:S(2)}) collective-permute-start(f32[384,128]{1,0:T(8,128)S(1)} %collective-permute-done.8), channel_id=1, source_target_pairs={{0,4},{1,5},{2,10},{3,11},{4,0},{5,1},{6,14},{7,15},{8,12},{9,13},... | collective-permute-start | bytes 589832 | tf_op jit(solution)/shard_map/ppermute | solution.py:40
  44.0 4.4 %collective-permute-done.18 = f32[384,128]{1,0:T(8,128)S(1)} collective-permute-done((f32[384,128]{1,0:T(8,128)S(1)}, f32[384,128]{1,0:T(8,128)S(1)}, u32[]{:S(2)}, u32[]{:S(2)}) %collective-permute-start.18) | collective-permute-done | bytes 196640 | tf_op jit(solution)/shard_map/ppermute | solution.py:40
  48.9 3.1 %collective-permute-start.21 = (f32[384,128]{1,0:T(8,128)S(1)}, f32[384,128]{1,0:T(8,128)S(1)}, u32[]{:S(2)}, u32[]{:S(2)}) collective-permute-start(f32[384,128]{1,0:T(8,128)S(1)} %add_multiply_fusion), channel_id=1, source_target_pairs={{0,12},{1,13},{2,14},{3,15},{4,8},{5,9},{6,10},{7,11},{8,4},{9,5},... | collective-permute-start | bytes 589832 | tf_op jit(solution)/shard_map/ppermute | solution.py:40
  51.9 2.1 %fusion.6 = f32[384,128]{1,0:T(8,128)S(1)} fusion(f32[384,128]{1,0:T(8,128)} %collective-permute-done.10, f32[384,128]{1,0:T(8,128)} %copy-done.1, f32[384,128]{1,0:T(8,128)S(1)} %collective-permute-done.8, f32[384,128]{1,0:T(8,128)S(1)} %add_multiply_fusion.1, f32[96,1536]{1,0:T(8,128)S(1)} %get-tuple-element.42, f32[96,1536]{1,0:T(8,128)S(1)} %get-tuple-element.40, ...), kind=kOutput, calls=%fused_computation.13 | convolution fusion | flops 455344128 | bytes 3342336 | tf_op jit(solution)/shard_map/dot_general | solution.py:14
  54.1 1.6 %collective-permute-start.11 = (f32[192,128]{1,0:T(8,128)S(1)}, f32[192,128]{1,0:T(8,128)S(1)}, u32[]{:S(2)}, u32[]{:S(2)}) collective-permute-start(f32[192,128]{1,0:T(8,128)S(1)} %slice.75), channel_id=1, source_target_pairs={{0,1},{1,0},{2,3},{3,2},{4,5},{5,4},{6,7},{7,6},{8,9},{9,8},{10,11... | collective-permute-start | bytes 294920 | tf_op jit(solution)/shard_map/ppermute | solution.py:40
  55.6 2.1 %collective-permute-done.21 = f32[384,128]{1,0:T(8,128)S(1)} collective-permute-done((f32[384,128]{1,0:T(8,128)S(1)}, f32[384,128]{1,0:T(8,128)S(1)}, u32[]{:S(2)}, u32[]{:S(2)}) %collective-permute-start.21) | collective-permute-done | bytes 196640 | tf_op jit(solution)/shard_map/ppermute | solution.py:40
  59.0 1.5 %collective-permute-start.23 = (f32[96,128]{1,0:T(8,128)S(1)}, f32[96,128]{1,0:T(8,128)S(1)}, u32[]{:S(2)}, u32[]{:S(2)}) collective-permute-start(f32[96,128]{1,0:T(8,128)S(1)} %get-tuple-element.59), channel_id=1, source_target_pairs={{0,1},{1,0},{2,3},{3,2},{4,5},{5,4},{6,7},{7,6},{8,9},{9,8},{10,11... | collective-permute-start | bytes 147464 | tf_op jit(solution)/shard_map/ppermute | solution.py:40
  61.3 1.8 %collective-permute-done.23 = f32[96,128]{1,0:T(8,128)S(1)} collective-permute-done((f32[96,128]{1,0:T(8,128)S(1)}, f32[96,128]{1,0:T(8,128)S(1)}, u32[]{:S(2)}, u32[]{:S(2)}) %collective-permute-start.23) | collective-permute-done | bytes 49184 | tf_op jit(solution)/shard_map/ppermute | solution.py:40
  (65 shorter events, 12.5 us)
Async XLA Ops:
  0.0 4.5 %collective-permute-start = (f32[192,1536]{1,0:T(8,128)}, f32[192,1536]{1,0:T(8,128)S(1)}, u32[]{:S(2)}, u32[]{:S(2)}) collective-permute-start(f32[192,1536]{1,0:T(8,128)} %param.2), channel_id=1, source_target_pairs={{0,2},{1,3},{2,0},{3,1},{4,6},{5,7},{6,4},{7,5},{8,10},{9,11},{10,... | collective-permute-start | bytes 3538952 | tf_op jit(solution)/shard_map/ppermute | solution.py:40
  1.3 7.4 %collective-permute-start.1 = (f32[96,128]{1,0:T(8,128)S(1)}, f32[96,128]{1,0:T(8,128)S(1)}, u32[]{:S(2)}, u32[]{:S(2)}) collective-permute-start(f32[96,128]{1,0:T(8,128)S(1)} %get-tuple-element.63), channel_id=1, source_target_pairs={{0,2},{1,3},{2,0},{3,1},{4,6},{5,7},{6,4},{7,5},{8,10},{9,11},{10,... | collective-permute-start | bytes 147464 | tf_op jit(solution)/shard_map/ppermute | solution.py:40
  1.5 7.7 %collective-permute-start.3 = (f32[96,128]{1,0:T(8,128)S(1)}, f32[96,128]{1,0:T(8,128)S(1)}, u32[]{:S(2)}, u32[]{:S(2)}) collective-permute-start(f32[96,128]{1,0:T(8,128)S(1)} %get-tuple-element.63), channel_id=1, source_target_pairs={{0,3},{1,2},{2,1},{3,0},{4,7},{5,6},{6,5},{7,4},{8,11},{9,10},{10,... | collective-permute-start | bytes 147464 | tf_op jit(solution)/shard_map/ppermute | solution.py:40
  4.1 5.1 %collective-permute-start.2 = (f32[96,128]{1,0:T(8,128)S(1)}, f32[96,128]{1,0:T(8,128)S(1)}, u32[]{:S(2)}, u32[]{:S(2)}) collective-permute-start(f32[96,128]{1,0:T(8,128)S(1)} %get-tuple-element.61), channel_id=1, source_target_pairs={{0,1},{1,0},{2,3},{3,2},{4,5},{5,4},{6,7},{7,6},{8,9},{9,8},{10,11... | collective-permute-start | bytes 147464 | tf_op jit(solution)/shard_map/ppermute | solution.py:40
  6.9 7.2 %collective-permute-start.12 = (f32[96,128]{1,0:T(8,128)S(1)}, f32[96,128]{1,0:T(8,128)S(1)}, u32[]{:S(2)}, u32[]{:S(2)}) collective-permute-start(f32[96,128]{1,0:T(8,128)S(1)} %get-tuple-element.28), channel_id=1, source_target_pairs={{0,2},{1,3},{2,0},{3,1},{4,6},{5,7},{6,4},{7,5},{8,10},{9,11},{10,... | collective-permute-start | bytes 147464 | tf_op jit(solution)/shard_map/ppermute | solution.py:40
  7.1 7.3 %collective-permute-start.14 = (f32[96,128]{1,0:T(8,128)S(1)}, f32[96,128]{1,0:T(8,128)S(1)}, u32[]{:S(2)}, u32[]{:S(2)}) collective-permute-start(f32[96,128]{1,0:T(8,128)S(1)} %get-tuple-element.28), channel_id=1, source_target_pairs={{0,3},{1,2},{2,1},{3,0},{4,7},{5,6},{6,5},{7,4},{8,11},{9,10},{10,... | collective-permute-start | bytes 147464 | tf_op jit(solution)/shard_map/ppermute | solution.py:40
  8.8 5.6 %collective-permute-start.13 = (f32[96,128]{1,0:T(8,128)S(1)}, f32[96,128]{1,0:T(8,128)S(1)}, u32[]{:S(2)}, u32[]{:S(2)}) collective-permute-start(f32[96,128]{1,0:T(8,128)S(1)} %get-tuple-element.27), channel_id=1, source_target_pairs={{0,1},{1,0},{2,3},{3,2},{4,5},{5,4},{6,7},{7,6},{8,9},{9,8},{10,11... | collective-permute-start | bytes 147464 | tf_op jit(solution)/shard_map/ppermute | solution.py:40
  10.8 8.8 %collective-permute-start.4 = (f32[384,128]{1,0:T(8,128)S(1)}, f32[384,128]{1,0:T(8,128)S(1)}, u32[]{:S(2)}, u32[]{:S(2)}) collective-permute-start(f32[384,128]{1,0:T(8,128)S(1)} %get-tuple-element.53), channel_id=1, source_target_pairs={{0,4},{1,5},{2,10},{3,11},{4,0},{5,1},{6,14},{7,15},{8,12},{9,13},... | collective-permute-start | bytes 589832 | tf_op jit(solution)/shard_map/ppermute | solution.py:40
  12.5 7.8 %collective-permute-start.5 = (f32[384,128]{1,0:T(8,128)S(1)}, f32[384,128]{1,0:T(8,128)S(1)}, u32[]{:S(2)}, u32[]{:S(2)}) collective-permute-start(f32[384,128]{1,0:T(8,128)S(1)} %get-tuple-element.52), channel_id=1, source_target_pairs={{0,8},{1,9},{2,6},{3,7},{4,12},{5,13},{6,2},{7,3},{8,0},{9,1},{10,... | collective-permute-start | bytes 589832 | tf_op jit(solution)/shard_map/ppermute | solution.py:40
  14.1 10.3 %collective-permute-start.6 = (f32[384,128]{1,0:T(8,128)S(1)}, f32[384,128]{1,0:T(8,128)S(1)}, u32[]{:S(2)}, u32[]{:S(2)}) collective-permute-start(f32[384,128]{1,0:T(8,128)S(1)} %get-tuple-element.51), channel_id=1, source_target_pairs={{0,12},{1,13},{2,14},{3,15},{4,8},{5,9},{6,10},{7,11},{8,4},{9,5},... | collective-permute-start | bytes 589832 | tf_op jit(solution)/shard_map/ppermute | solution.py:40
  15.6 12.3 %collective-permute-start.16 = (f32[384,128]{1,0:T(8,128)S(1)}, f32[384,128]{1,0:T(8,128)S(1)}, u32[]{:S(2)}, u32[]{:S(2)}) collective-permute-start(f32[384,128]{1,0:T(8,128)S(1)} %get-tuple-element.54), channel_id=1, source_target_pairs={{0,4},{1,5},{2,10},{3,11},{4,0},{5,1},{6,14},{7,15},{8,12},{9,13},... | collective-permute-start | bytes 589832 | tf_op jit(solution)/shard_map/ppermute | solution.py:40
  17.3 19.2 %collective-permute-start.15 = (f32[384,128]{1,0:T(8,128)S(1)}, f32[384,128]{1,0:T(8,128)S(1)}, u32[]{:S(2)}, u32[]{:S(2)}) collective-permute-start(f32[384,128]{1,0:T(8,128)S(1)} %get-tuple-element.55), channel_id=1, source_target_pairs={{0,4},{1,5},{2,10},{3,11},{4,0},{5,1},{6,14},{7,15},{8,12},{9,13},... | collective-permute-start | bytes 589832 | tf_op jit(solution)/shard_map/ppermute | solution.py:40
  25.1 9.9 %collective-permute-start.7 = (f32[384,128]{1,0:T(8,128)S(1)}, f32[384,128]{1,0:T(8,128)S(1)}, u32[]{:S(2)}, u32[]{:S(2)}) collective-permute-start(f32[384,128]{1,0:T(8,128)S(1)} %fusion.5), channel_id=1, source_target_pairs={{0,16},{1,17},{2,18},{3,19},{4,20},{5,21},{6,22},{7,23},{8,24},{9,... | collective-permute-start | bytes 589832 | tf_op jit(solution)/shard_map/ppermute | solution.py:40
  28.6 10.9 %collective-permute-start.17 = (f32[384,128]{1,0:T(8,128)S(1)}, f32[384,128]{1,0:T(8,128)S(1)}, u32[]{:S(2)}, u32[]{:S(2)}) collective-permute-start(f32[384,128]{1,0:T(8,128)S(1)} %convolution_add_fusion), channel_id=1, source_target_pairs={{0,8},{1,9},{2,6},{3,7},{4,12},{5,13},{6,2},{7,3},{8,0},{9,1},{10,... | collective-permute-start | bytes 589832 | tf_op jit(solution)/shard_map/ppermute | solution.py:40
  35.0 7.4 %collective-permute-start.8 = (f32[384,128]{1,0:T(8,128)S(1)}, f32[384,128]{1,0:T(8,128)S(1)}, u32[]{:S(2)}, u32[]{:S(2)}) collective-permute-start(f32[384,128]{1,0:T(8,128)S(1)} %add_multiply_fusion.1), channel_id=1, source_target_pairs={{0,8},{1,9},{2,6},{3,7},{4,12},{5,13},{6,2},{7,3},{8,0},{9,1},{10,... | collective-permute-start | bytes 589832 | tf_op jit(solution)/shard_map/ppermute | solution.py:40
  35.4 7.0 %collective-permute-start.9 = (f32[384,128]{1,0:T(8,128)S(1)}, f32[384,128]{1,0:T(8,128)S(1)}, u32[]{:S(2)}, u32[]{:S(2)}) collective-permute-start(f32[384,128]{1,0:T(8,128)S(1)} %add_multiply_fusion.1), channel_id=1, source_target_pairs={{0,4},{1,5},{2,10},{3,11},{4,0},{5,1},{6,14},{7,15},{8,12},{9,13},... | collective-permute-start | bytes 589832 | tf_op jit(solution)/shard_map/ppermute | solution.py:40
  39.5 8.8 %collective-permute-start.18 = (f32[384,128]{1,0:T(8,128)S(1)}, f32[384,128]{1,0:T(8,128)S(1)}, u32[]{:S(2)}, u32[]{:S(2)}) collective-permute-start(f32[384,128]{1,0:T(8,128)S(1)} %add_add_fusion), channel_id=1, source_target_pairs={{0,16},{1,17},{2,18},{3,19},{4,20},{5,21},{6,22},{7,23},{8,24},{9,... | collective-permute-start | bytes 589832 | tf_op jit(solution)/shard_map/ppermute | solution.py:40
  42.4 9.5 %collective-permute-start.10 = (f32[384,128]{1,0:T(8,128)S(1)}, f32[384,128]{1,0:T(8,128)}, u32[]{:S(2)}, u32[]{:S(2)}) collective-permute-start(f32[384,128]{1,0:T(8,128)S(1)} %collective-permute-done.8), channel_id=1, source_target_pairs={{0,4},{1,5},{2,10},{3,11},{4,0},{5,1},{6,14},{7,15},{8,12},{9,13},... | collective-permute-start | bytes 589832 | tf_op jit(solution)/shard_map/ppermute | solution.py:40
  48.4 7.2 %collective-permute-start.19 = (f32[384,128]{1,0:T(8,128)S(1)}, f32[384,128]{1,0:T(8,128)S(1)}, u32[]{:S(2)}, u32[]{:S(2)}) collective-permute-start(f32[384,128]{1,0:T(8,128)S(1)} %add_multiply_fusion), channel_id=1, source_target_pairs={{0,4},{1,5},{2,10},{3,11},{4,0},{5,1},{6,14},{7,15},{8,12},{9,13},... | collective-permute-start | bytes 589832 | tf_op jit(solution)/shard_map/ppermute | solution.py:40
  48.9 6.8 %collective-permute-start.20 = (f32[384,128]{1,0:T(8,128)S(1)}, f32[384,128]{1,0:T(8,128)S(1)}, u32[]{:S(2)}, u32[]{:S(2)}) collective-permute-start(f32[384,128]{1,0:T(8,128)S(1)} %add_multiply_fusion), channel_id=1, source_target_pairs={{0,8},{1,9},{2,6},{3,7},{4,12},{5,13},{6,2},{7,3},{8,0},{9,1},{10,... | collective-permute-start | bytes 589832 | tf_op jit(solution)/shard_map/ppermute | solution.py:40
  48.9 8.8 %collective-permute-start.21 = (f32[384,128]{1,0:T(8,128)S(1)}, f32[384,128]{1,0:T(8,128)S(1)}, u32[]{:S(2)}, u32[]{:S(2)}) collective-permute-start(f32[384,128]{1,0:T(8,128)S(1)} %add_multiply_fusion), channel_id=1, source_target_pairs={{0,12},{1,13},{2,14},{3,15},{4,8},{5,9},{6,10},{7,11},{8,4},{9,5},... | collective-permute-start | bytes 589832 | tf_op jit(solution)/shard_map/ppermute | solution.py:40
  54.1 6.8 %collective-permute-start.11 = (f32[192,128]{1,0:T(8,128)S(1)}, f32[192,128]{1,0:T(8,128)S(1)}, u32[]{:S(2)}, u32[]{:S(2)}) collective-permute-start(f32[192,128]{1,0:T(8,128)S(1)} %slice.75), channel_id=1, source_target_pairs={{0,1},{1,0},{2,3},{3,2},{4,5},{5,4},{6,7},{7,6},{8,9},{9,8},{10,11... | collective-permute-start | bytes 294920 | tf_op jit(solution)/shard_map/ppermute | solution.py:40
  59.0 4.2 %collective-permute-start.23 = (f32[96,128]{1,0:T(8,128)S(1)}, f32[96,128]{1,0:T(8,128)S(1)}, u32[]{:S(2)}, u32[]{:S(2)}) collective-permute-start(f32[96,128]{1,0:T(8,128)S(1)} %get-tuple-element.59), channel_id=1, source_target_pairs={{0,1},{1,0},{2,3},{3,2},{4,5},{5,4},{6,7},{7,6},{8,9},{9,8},{10,11... | collective-permute-start | bytes 147464 | tf_op jit(solution)/shard_map/ppermute | solution.py:40
  60.5 3.7 %collective-permute-start.24 = (f32[96,128]{1,0:T(8,128)S(1)}, f32[96,128]{1,0:T(8,128)S(1)}, u32[]{:S(2)}, u32[]{:S(2)}) collective-permute-start(f32[96,128]{1,0:T(8,128)S(1)} %get-tuple-element.58), channel_id=1, source_target_pairs={{0,3},{1,2},{2,1},{3,0},{4,7},{5,6},{6,5},{7,4},{8,11},{9,10},{10,... | collective-permute-start | bytes 147464 | tf_op jit(solution)/shard_map/ppermute | solution.py:40
  (4 other events, 17.1 us)

commit v8 on v6

--- a/solution.py
+++ b/solution.py
@@ -101,7 +101,6 @@
         if partials:
             received = dict(zip(quarters, together([exchange(fresh, masks, 0) for masks in partners])))
             fresh = jnp.concatenate([fresh, received[1], received[2], received[3]], axis=0)
-            fresh = after(fresh, partials[-1])
         else:
             second, first = together([exchange(fresh, partners[1], 0), exchange(fresh, partners[0], 0)])
             fresh = jnp.concatenate([fresh, second, first, exchange(second, partners[0], 0)], axis=0)

time: 64.7 us -> 70 us (1.082)
  waiting for transfers between devices: 19 us -> 29.4 us
  starting transfers between devices: 33 us -> 27.1 us
  matrix products: 7.95 us -> 8.77 us
    ppermute x26, waiting for transfers between devices: 19 us -> 29.4 us  [exchange(): return lax.ppermute(block, ('row', 'col'), pairs)]
    ppermute x26, starting transfers between devices: 33 us -> 27.1 us  [exchange(): return lax.ppermute(block, ('row', 'col'), pairs)]
    dot_general x7, matrix products: 7.95 us -> 8.77 us  [product(): lax.dot_general(left, right, (((left_dim,), (0,)), ((), ())), precision=l...]
  transfers between devices with their start and end apart: 26 -> 26, of which waited for: 10 -> 9; matrix products, arithmetic and copies ran while one was open for 18% -> 18% of each run, Pallas kernels for 0% -> 0%
where the time goes in v8:
time: 70 us; the launch traced here: 69.7 us
  waiting for transfers between devices  29.4 us (42%)
  starting transfers between devices  27.1 us (39%)
  matrix products  8.77 us (13%)
  other arithmetic  2.8 us (4%)
  local copies, waits for them, and re-layouts  1.43 us (2%)
    ppermute x26, waiting for transfers between devices, exchange(): return lax.ppermute(block, ('row', 'col'), pairs)  29.4 us
    ppermute x26, starting transfers between devices, exchange(): return lax.ppermute(block, ('row', 'col'), pairs)  27.1 us
    dot_general x7, matrix products, product(): lax.dot_general(left, right, (((left_dim,), (0,)), ((), ())), precision=l...  8.77 us
    sub x1, other arithmetic, prepared(): block - jnp.where(on_diagonal, jnp.float32(center), jnp.float32(0.0))  1.57 us
  transfers between devices with their start and end apart: 26, of which 9 were waited for; matrix products, arithmetic and copies ran while one was open for 18% of the time, Pallas kernels for 0%

profile of v8, /device:TPU:0, one launch (start us, length us, event | category | flops | bytes accessed | tf_op | source)
XLA Modules:
  0.0 69.7 jit_solution(12374659180725311315)
XLA Ops:
  1.3 2.7 %collective-permute-start.3 = (f32[96,128]{1,0:T(8,128)S(1)}, f32[96,128]{1,0:T(8,128)S(1)}, u32[]{:S(2)}, u32[]{:S(2)}) collective-permute-start(f32[96,128]{1,0:T(8,128)S(1)} %get-tuple-element.57), channel_id=1, source_target_pairs={{0,3},{1,2},{2,1},{3,0},{4,7},{5,6},{6,5},{7,4},{8,11},{9,10},{10,... | collective-permute-start | bytes 147464 | tf_op jit(solution)/shard_map/ppermute | solution.py:40
  4.5 1.6 %select_subtract_fusion.1 = (f32[192,1536]{1,0:T(8,128)S(1)}, f32[192,1536]{1,0:T(8,128)S(1)}) fusion(f32[192,1536]{1,0:T(8,128)} %param.2, s32[1536]{0:T(1024)S(1)} %iota_add_fusion, s32[192]{0:T(256)S(1)} %iota_add_fusion.2, f32[192,1536]{1,0:T(8,128)S(1)} %collective-permute-done, s32[192]{0:T(256)S(1)} %iota_add_fusion.1), kind=kLoop, calls=%fused_computation.8 | loop fusion | flops 1769472 | bytes 4726272 | tf_op jit(solution)/shard_map/sub | solution.py:49
  7.0 1.5 %collective-permute-start.14 = (f32[96,128]{1,0:T(8,128)S(1)}, f32[96,128]{1,0:T(8,128)S(1)}, u32[]{:S(2)}, u32[]{:S(2)}) collective-permute-start(f32[96,128]{1,0:T(8,128)S(1)} %get-tuple-element.25), channel_id=1, source_target_pairs={{0,3},{1,2},{2,1},{3,0},{4,7},{5,6},{6,5},{7,4},{8,11},{9,10},{10,... | collective-permute-start | bytes 147464 | tf_op jit(solution)/shard_map/ppermute | solution.py:40
  9.2 1.6 %fusion = f32[1152,128]{1,0:T(8,128)S(1)} fusion(f32[384,1536]{1,0:T(8,128)S(1)} %pad_maximum_fusion, f32[96,128]{1,0:T(8,128)S(1)} %collective-permute-done.3, f32[96,128]{1,0:T(8,128)S(1)} %collective-permute-done.2, f32[96,128]{1,0:T(8,128)S(1)} %collective-permute-done.1, f32[96,128]{1,0:T(8,128)S(1)} %get-tuple-element.55), kind=kOutput, calls=%fused_computation.1 | convolution fusion | flops 339886080 | bytes 2555904 | tf_op jit(solution)/shard_map/dot_general | solution.py:14
  10.8 2.7 %collective-permute-start.6 = (f32[384,128]{1,0:T(8,128)S(1)}, f32[384,128]{1,0:T(8,128)S(1)}, u32[]{:S(2)}, u32[]{:S(2)}) collective-permute-start(f32[384,128]{1,0:T(8,128)S(1)} %get-tuple-element.45), channel_id=1, source_target_pairs={{0,12},{1,13},{2,14},{3,15},{4,8},{5,9},{6,10},{7,11},{8,4},{9,5},... | collective-permute-start | bytes 589832 | tf_op jit(solution)/shard_map/ppermute | solution.py:40
  15.6 1.6 %collective-permute-start.15 = (f32[384,128]{1,0:T(8,128)S(1)}, f32[384,128]{1,0:T(8,128)S(1)}, u32[]{:S(2)}, u32[]{:S(2)}) collective-permute-start(f32[384,128]{1,0:T(8,128)S(1)} %get-tuple-element.48), channel_id=1, source_target_pairs={{0,4},{1,5},{2,10},{3,11},{4,0},{5,1},{6,14},{7,15},{8,12},{9,13},... | collective-permute-start | bytes 589832 | tf_op jit(solution)/shard_map/ppermute | solution.py:40
  17.7 1.9 %collective-permute-done.6 = f32[384,128]{1,0:T(8,128)S(1)} collective-permute-done((f32[384,128]{1,0:T(8,128)S(1)}, f32[384,128]{1,0:T(8,128)S(1)}, u32[]{:S(2)}, u32[]{:S(2)}) %collective-permute-start.6) | collective-permute-done | bytes 196640 | tf_op jit(solution)/shard_map/ppermute | solution.py:40
  19.6 4.4 %collective-permute-done.5 = f32[384,128]{1,0:T(8,128)S(1)} collective-permute-done((f32[384,128]{1,0:T(8,128)S(1)}, f32[384,128]{1,0:T(8,128)S(1)}, u32[]{:S(2)}, u32[]{:S(2)}) %collective-permute-start.5) | collective-permute-done | bytes 196640 | tf_op jit(solution)/shard_map/ppermute | solution.py:40
  24.6 2.7 %collective-permute-start.7 = (f32[384,128]{1,0:T(8,128)S(1)}, f32[384,128]{1,0:T(8,128)S(1)}, u32[]{:S(2)}, u32[]{:S(2)}) collective-permute-start(f32[384,128]{1,0:T(8,128)S(1)} %fusion.6), channel_id=1, source_target_pairs={{0,16},{1,17},{2,18},{3,19},{4,20},{5,21},{6,22},{7,23},{8,24},{9,... | collective-permute-start | bytes 589832 | tf_op jit(solution)/shard_map/ppermute | solution.py:40
  28.0 1.6 %collective-permute-start.17 = (f32[384,128]{1,0:T(8,128)S(1)}, f32[384,128]{1,0:T(8,128)S(1)}, u32[]{:S(2)}, u32[]{:S(2)}) collective-permute-start(f32[384,128]{1,0:T(8,128)S(1)} %convolution_add_fusion), channel_id=1, source_target_pairs={{0,8},{1,9},{2,6},{3,7},{4,12},{5,13},{6,2},{7,3},{8,0},{9,1},{10,... | collective-permute-start | bytes 589832 | tf_op jit(solution)/shard_map/ppermute | solution.py:40
  29.6 6.1 %collective-permute-done.7 = f32[384,128]{1,0:T(8,128)S(1)} collective-permute-done((f32[384,128]{1,0:T(8,128)S(1)}, f32[384,128]{1,0:T(8,128)S(1)}, u32[]{:S(2)}, u32[]{:S(2)}) %collective-permute-start.7) | collective-permute-done | bytes 196640 | tf_op jit(solution)/shard_map/ppermute | solution.py:40
  35.6 1.6 %collective-permute-start.9 = (f32[384,128]{1,0:T(8,128)S(1)}, f32[384,128]{1,0:T(8,128)S(1)}, u32[]{:S(2)}, u32[]{:S(2)}) collective-permute-start(f32[384,128]{1,0:T(8,128)S(1)} %add_multiply_fusion.1), channel_id=1, source_target_pairs={{0,4},{1,5},{2,10},{3,11},{4,0},{5,1},{6,14},{7,15},{8,12},{9,13},... | collective-permute-start | bytes 589832 | tf_op jit(solution)/shard_map/ppermute | solution.py:40
  37.9 2.7 %collective-permute-start.18 = (f32[384,128]{1,0:T(8,128)S(1)}, f32[384,128]{1,0:T(8,128)S(1)}, u32[]{:S(2)}, u32[]{:S(2)}) collective-permute-start(f32[384,128]{1,0:T(8,128)S(1)} %fusion.5), channel_id=1, source_target_pairs={{0,16},{1,17},{2,18},{3,19},{4,20},{5,21},{6,22},{7,23},{8,24},{9,... | collective-permute-start | bytes 589832 | tf_op jit(solution)/shard_map/ppermute | solution.py:40
  40.6 2.3 %collective-permute-done.9 = f32[384,128]{1,0:T(8,128)S(1)} collective-permute-done((f32[384,128]{1,0:T(8,128)S(1)}, f32[384,128]{1,0:T(8,128)S(1)}, u32[]{:S(2)}, u32[]{:S(2)}) %collective-permute-start.9) | collective-permute-done | bytes 196640 | tf_op jit(solution)/shard_map/ppermute | solution.py:40
  42.9 4.2 %collective-permute-done.8 = f32[384,128]{1,0:T(8,128)S(1)} collective-permute-done((f32[384,128]{1,0:T(8,128)S(1)}, f32[384,128]{1,0:T(8,128)S(1)}, u32[]{:S(2)}, u32[]{:S(2)}) %collective-permute-start.8) | collective-permute-done | bytes 196640 | tf_op jit(solution)/shard_map/ppermute | solution.py:40
  47.1 2.4 %collective-permute-done.18 = f32[384,128]{1,0:T(8,128)S(1)} collective-permute-done((f32[384,128]{1,0:T(8,128)S(1)}, f32[384,128]{1,0:T(8,128)S(1)}, u32[]{:S(2)}, u32[]{:S(2)}) %collective-permute-start.18) | collective-permute-done | bytes 196640 | tf_op jit(solution)/shard_map/ppermute | solution.py:40
  49.5 1.6 %collective-permute-start.21 = (f32[384,128]{1,0:T(8,128)S(1)}, f32[384,128]{1,0:T(8,128)S(1)}, u32[]{:S(2)}, u32[]{:S(2)}) collective-permute-start(f32[384,128]{1,0:T(8,128)S(1)} %add_multiply_fusion), channel_id=1, source_target_pairs={{0,12},{1,13},{2,14},{3,15},{4,8},{5,9},{6,10},{7,11},{8,4},{9,5},... | collective-permute-start | bytes 589832 | tf_op jit(solution)/shard_map/ppermute | solution.py:40
  51.1 1.4 %collective-permute-start.20 = (f32[384,128]{1,0:T(8,128)S(1)}, f32[384,128]{1,0:T(8,128)S(1)}, u32[]{:S(2)}, u32[]{:S(2)}) collective-permute-start(f32[384,128]{1,0:T(8,128)S(1)} %add_multiply_fusion), channel_id=1, source_target_pairs={{0,8},{1,9},{2,6},{3,7},{4,12},{5,13},{6,2},{7,3},{8,0},{9,1},{10,... | collective-permute-start | bytes 589832 | tf_op jit(solution)/shard_map/ppermute | solution.py:40
  53.1 5.5 %collective-permute-done.10 = f32[384,128]{1,0:T(8,128)} collective-permute-done((f32[384,128]{1,0:T(8,128)S(1)}, f32[384,128]{1,0:T(8,128)}, u32[]{:S(2)}, u32[]{:S(2)}) %collective-permute-start.10) | collective-permute-done | bytes 196640 | tf_op jit(solution)/shard_map/ppermute | solution.py:40
  58.6 2.0 %fusion.7 = f32[384,128]{1,0:T(8,128)S(1)} fusion(f32[384,128]{1,0:T(8,128)} %collective-permute-done.10, f32[384,128]{1,0:T(8,128)S(1)} %collective-permute-done.9, f32[384,128]{1,0:T(8,128)S(1)} %collective-permute-done.8, f32[384,128]{1,0:T(8,128)S(1)} %add_multiply_fusion.1, f32[96,1536]{1,0:T(8,128)S(1)} %get-tuple-element.36, ...), kind=kOutput, calls=%fused_computation.15 | convolution fusion | flops 455344128 | bytes 3342336 | tf_op jit(solution)/shard_map/dot_general | solution.py:14
  60.7 1.6 %collective-permute-start.11 = (f32[192,128]{1,0:T(8,128)S(1)}, f32[192,128]{1,0:T(8,128)S(1)}, u32[]{:S(2)}, u32[]{:S(2)}) collective-permute-start(f32[192,128]{1,0:T(8,128)S(1)} %slice.75), channel_id=1, source_target_pairs={{0,1},{1,0},{2,3},{3,2},{4,5},{5,4},{6,7},{7,6},{8,9},{9,8},{10,11... | collective-permute-start | bytes 294920 | tf_op jit(solution)/shard_map/ppermute | solution.py:40
  62.2 2.0 %fusion.15 = f32[384,128]{1,0:T(8,128)S(1)} fusion(f32[384,128]{1,0:T(8,128)S(1)} %collective-permute-done.21, f32[384,128]{1,0:T(8,128)} %collective-permute-done.19, f32[384,128]{1,0:T(8,128)S(1)} %collective-permute-done.20, f32[384,128]{1,0:T(8,128)S(1)} %add_multiply_fusion, f32[96,1536]{1,0:T(8,128)S(1)} %get-tuple-element.36, ...), kind=kOutput, calls=%fused_computation.23 | convolution fusion | flops 455344128 | bytes 3342336 | tf_op jit(solution)/shard_map/dot_general | solution.py:14
  65.0 1.3 %collective-permute-start.22 = (f32[96,128]{1,0:T(8,128)S(1)}, f32[96,128]{1,0:T(8,128)S(1)}, u32[]{:S(2)}, u32[]{:S(2)}) collective-permute-start(f32[96,128]{1,0:T(8,128)S(1)} %get-tuple-element.54), channel_id=1, source_target_pairs={{0,2},{1,3},{2,0},{3,1},{4,6},{5,7},{6,4},{7,5},{8,10},{9,11},{10,... | collective-permute-start | bytes 147464 | tf_op jit(solution)/shard_map/ppermute | solution.py:40
  66.3 1.5 %collective-permute-done.24 = f32[96,128]{1,0:T(8,128)S(1)} collective-permute-done((f32[96,128]{1,0:T(8,128)S(1)}, f32[96,128]{1,0:T(8,128)S(1)}, u32[]{:S(2)}, u32[]{:S(2)}) %collective-permute-start.24) | collective-permute-done | bytes 49184 | tf_op jit(solution)/shard_map/ppermute | solution.py:40
  (61 shorter events, 11.3 us)
Async XLA Ops:
  0.0 4.5 %collective-permute-start = (f32[192,1536]{1,0:T(8,128)}, f32[192,1536]{1,0:T(8,128)S(1)}, u32[]{:S(2)}, u32[]{:S(2)}) collective-permute-start(f32[192,1536]{1,0:T(8,128)} %param.2), channel_id=1, source_target_pairs={{0,2},{1,3},{2,0},{3,1},{4,6},{5,7},{6,4},{7,5},{8,10},{9,11},{10,... | collective-permute-start | bytes 3538952 | tf_op jit(solution)/shard_map/ppermute | solution.py:40
  1.3 7.4 %collective-permute-start.3 = (f32[96,128]{1,0:T(8,128)S(1)}, f32[96,128]{1,0:T(8,128)S(1)}, u32[]{:S(2)}, u32[]{:S(2)}) collective-permute-start(f32[96,128]{1,0:T(8,128)S(1)} %get-tuple-element.57), channel_id=1, source_target_pairs={{0,3},{1,2},{2,1},{3,0},{4,7},{5,6},{6,5},{7,4},{8,11},{9,10},{10,... | collective-permute-start | bytes 147464 | tf_op jit(solution)/shard_map/ppermute | solution.py:40
  4.0 5.2 %collective-permute-start.1 = (f32[96,128]{1,0:T(8,128)S(1)}, f32[96,128]{1,0:T(8,128)S(1)}, u32[]{:S(2)}, u32[]{:S(2)}) collective-permute-start(f32[96,128]{1,0:T(8,128)S(1)} %get-tuple-element.57), channel_id=1, source_target_pairs={{0,2},{1,3},{2,0},{3,1},{4,6},{5,7},{6,4},{7,5},{8,10},{9,11},{10,... | collective-permute-start | bytes 147464 | tf_op jit(solution)/shard_map/ppermute | solution.py:40
  4.0 5.2 %collective-permute-start.2 = (f32[96,128]{1,0:T(8,128)S(1)}, f32[96,128]{1,0:T(8,128)S(1)}, u32[]{:S(2)}, u32[]{:S(2)}) collective-permute-start(f32[96,128]{1,0:T(8,128)S(1)} %get-tuple-element.55), channel_id=1, source_target_pairs={{0,1},{1,0},{2,3},{3,2},{4,5},{5,4},{6,7},{7,6},{8,9},{9,8},{10,11... | collective-permute-start | bytes 147464 | tf_op jit(solution)/shard_map/ppermute | solution.py:40
  7.0 7.4 %collective-permute-start.14 = (f32[96,128]{1,0:T(8,128)S(1)}, f32[96,128]{1,0:T(8,128)S(1)}, u32[]{:S(2)}, u32[]{:S(2)}) collective-permute-start(f32[96,128]{1,0:T(8,128)S(1)} %get-tuple-element.25), channel_id=1, source_target_pairs={{0,3},{1,2},{2,1},{3,0},{4,7},{5,6},{6,5},{7,4},{8,11},{9,10},{10,... | collective-permute-start | bytes 147464 | tf_op jit(solution)/shard_map/ppermute | solution.py:40
  8.4 6.0 %collective-permute-start.12 = (f32[96,128]{1,0:T(8,128)S(1)}, f32[96,128]{1,0:T(8,128)S(1)}, u32[]{:S(2)}, u32[]{:S(2)}) collective-permute-start(f32[96,128]{1,0:T(8,128)S(1)} %get-tuple-element.25), channel_id=1, source_target_pairs={{0,2},{1,3},{2,0},{3,1},{4,6},{5,7},{6,4},{7,5},{8,10},{9,11},{10,... | collective-permute-start | bytes 147464 | tf_op jit(solution)/shard_map/ppermute | solution.py:40
  8.7 5.2 %collective-permute-start.13 = (f32[96,128]{1,0:T(8,128)S(1)}, f32[96,128]{1,0:T(8,128)S(1)}, u32[]{:S(2)}, u32[]{:S(2)}) collective-permute-start(f32[96,128]{1,0:T(8,128)S(1)} %get-tuple-element.24), channel_id=1, source_target_pairs={{0,1},{1,0},{2,3},{3,2},{4,5},{5,4},{6,7},{7,6},{8,9},{9,8},{10,11... | collective-permute-start | bytes 147464 | tf_op jit(solution)/shard_map/ppermute | solution.py:40
  10.8 8.8 %collective-permute-start.6 = (f32[384,128]{1,0:T(8,128)S(1)}, f32[384,128]{1,0:T(8,128)S(1)}, u32[]{:S(2)}, u32[]{:S(2)}) collective-permute-start(f32[384,128]{1,0:T(8,128)S(1)} %get-tuple-element.45), channel_id=1, source_target_pairs={{0,12},{1,13},{2,14},{3,15},{4,8},{5,9},{6,10},{7,11},{8,4},{9,5},... | collective-permute-start | bytes 589832 | tf_op jit(solution)/shard_map/ppermute | solution.py:40
  13.5 10.5 %collective-permute-start.5 = (f32[384,128]{1,0:T(8,128)S(1)}, f32[384,128]{1,0:T(8,128)S(1)}, u32[]{:S(2)}, u32[]{:S(2)}) collective-permute-start(f32[384,128]{1,0:T(8,128)S(1)} %get-tuple-element.46), channel_id=1, source_target_pairs={{0,8},{1,9},{2,6},{3,7},{4,12},{5,13},{6,2},{7,3},{8,0},{9,1},{10,... | collective-permute-start | bytes 589832 | tf_op jit(solution)/shard_map/ppermute | solution.py:40
  13.9 10.0 %collective-permute-start.4 = (f32[384,128]{1,0:T(8,128)S(1)}, f32[384,128]{1,0:T(8,128)S(1)}, u32[]{:S(2)}, u32[]{:S(2)}) collective-permute-start(f32[384,128]{1,0:T(8,128)S(1)} %get-tuple-element.47), channel_id=1, source_target_pairs={{0,4},{1,5},{2,10},{3,11},{4,0},{5,1},{6,14},{7,15},{8,12},{9,13},... | collective-permute-start | bytes 589832 | tf_op jit(solution)/shard_map/ppermute | solution.py:40
  15.6 21.6 %collective-permute-start.15 = (f32[384,128]{1,0:T(8,128)S(1)}, f32[384,128]{1,0:T(8,128)S(1)}, u32[]{:S(2)}, u32[]{:S(2)}) collective-permute-start(f32[384,128]{1,0:T(8,128)S(1)} %get-tuple-element.48), channel_id=1, source_target_pairs={{0,4},{1,5},{2,10},{3,11},{4,0},{5,1},{6,14},{7,15},{8,12},{9,13},... | collective-permute-start | bytes 589832 | tf_op jit(solution)/shard_map/ppermute | solution.py:40
  17.3 10.0 %collective-permute-start.16 = (f32[384,128]{1,0:T(8,128)S(1)}, f32[384,128]{1,0:T(8,128)S(1)}, u32[]{:S(2)}, u32[]{:S(2)}) collective-permute-start(f32[384,128]{1,0:T(8,128)S(1)} %get-tuple-element.49), channel_id=1, source_target_pairs={{0,4},{1,5},{2,10},{3,11},{4,0},{5,1},{6,14},{7,15},{8,12},{9,13},... | collective-permute-start | bytes 589832 | tf_op jit(solution)/shard_map/ppermute | solution.py:40
  24.6 11.0 %collective-permute-start.7 = (f32[384,128]{1,0:T(8,128)S(1)}, f32[384,128]{1,0:T(8,128)S(1)}, u32[]{:S(2)}, u32[]{:S(2)}) collective-permute-start(f32[384,128]{1,0:T(8,128)S(1)} %fusion.6), channel_id=1, source_target_pairs={{0,16},{1,17},{2,18},{3,19},{4,20},{5,21},{6,22},{7,23},{8,24},{9,... | collective-permute-start | bytes 589832 | tf_op jit(solution)/shard_map/ppermute | solution.py:40
  28.0 9.3 %collective-permute-start.17 = (f32[384,128]{1,0:T(8,128)S(1)}, f32[384,128]{1,0:T(8,128)S(1)}, u32[]{:S(2)}, u32[]{:S(2)}) collective-permute-start(f32[384,128]{1,0:T(8,128)S(1)} %convolution_add_fusion), channel_id=1, source_target_pairs={{0,8},{1,9},{2,6},{3,7},{4,12},{5,13},{6,2},{7,3},{8,0},{9,1},{10,... | collective-permute-start | bytes 589832 | tf_op jit(solution)/shard_map/ppermute | solution.py:40
  35.6 7.2 %collective-permute-start.9 = (f32[384,128]{1,0:T(8,128)S(1)}, f32[384,128]{1,0:T(8,128)S(1)}, u32[]{:S(2)}, u32[]{:S(2)}) collective-permute-start(f32[384,128]{1,0:T(8,128)S(1)} %add_multiply_fusion.1), channel_id=1, source_target_pairs={{0,4},{1,5},{2,10},{3,11},{4,0},{5,1},{6,14},{7,15},{8,12},{9,13},... | collective-permute-start | bytes 589832 | tf_op jit(solution)/shard_map/ppermute | solution.py:40
  37.2 9.9 %collective-permute-start.8 = (f32[384,128]{1,0:T(8,128)S(1)}, f32[384,128]{1,0:T(8,128)S(1)}, u32[]{:S(2)}, u32[]{:S(2)}) collective-permute-start(f32[384,128]{1,0:T(8,128)S(1)} %add_multiply_fusion.1), channel_id=1, source_target_pairs={{0,8},{1,9},{2,6},{3,7},{4,12},{5,13},{6,2},{7,3},{8,0},{9,1},{10,... | collective-permute-start | bytes 589832 | tf_op jit(solution)/shard_map/ppermute | solution.py:40
  37.9 11.6 %collective-permute-start.18 = (f32[384,128]{1,0:T(8,128)S(1)}, f32[384,128]{1,0:T(8,128)S(1)}, u32[]{:S(2)}, u32[]{:S(2)}) collective-permute-start(f32[384,128]{1,0:T(8,128)S(1)} %fusion.5), channel_id=1, source_target_pairs={{0,16},{1,17},{2,18},{3,19},{4,20},{5,21},{6,22},{7,23},{8,24},{9,... | collective-permute-start | bytes 589832 | tf_op jit(solution)/shard_map/ppermute | solution.py:40
  47.1 11.6 %collective-permute-start.10 = (f32[384,128]{1,0:T(8,128)S(1)}, f32[384,128]{1,0:T(8,128)}, u32[]{:S(2)}, u32[]{:S(2)}) collective-permute-start(f32[384,128]{1,0:T(8,128)S(1)} %collective-permute-done.8), channel_id=1, source_target_pairs={{0,4},{1,5},{2,10},{3,11},{4,0},{5,1},{6,14},{7,15},{8,12},{9,13},... | collective-permute-start | bytes 589832 | tf_op jit(solution)/shard_map/ppermute | solution.py:40
  49.5 12.7 %collective-permute-start.21 = (f32[384,128]{1,0:T(8,128)S(1)}, f32[384,128]{1,0:T(8,128)S(1)}, u32[]{:S(2)}, u32[]{:S(2)}) collective-permute-start(f32[384,128]{1,0:T(8,128)S(1)} %add_multiply_fusion), channel_id=1, source_target_pairs={{0,12},{1,13},{2,14},{3,15},{4,8},{5,9},{6,10},{7,11},{8,4},{9,5},... | collective-permute-start | bytes 589832 | tf_op jit(solution)/shard_map/ppermute | solution.py:40
  51.1 11.1 %collective-permute-start.20 = (f32[384,128]{1,0:T(8,128)S(1)}, f32[384,128]{1,0:T(8,128)S(1)}, u32[]{:S(2)}, u32[]{:S(2)}) collective-permute-start(f32[384,128]{1,0:T(8,128)S(1)} %add_multiply_fusion), channel_id=1, source_target_pairs={{0,8},{1,9},{2,6},{3,7},{4,12},{5,13},{6,2},{7,3},{8,0},{9,1},{10,... | collective-permute-start | bytes 589832 | tf_op jit(solution)/shard_map/ppermute | solution.py:40
  52.5 9.8 %collective-permute-start.19 = (f32[384,128]{1,0:T(8,128)S(1)}, f32[384,128]{1,0:T(8,128)}, u32[]{:S(2)}, u32[]{:S(2)}) collective-permute-start(f32[384,128]{1,0:T(8,128)S(1)} %add_multiply_fusion), channel_id=1, source_target_pairs={{0,4},{1,5},{2,10},{3,11},{4,0},{5,1},{6,14},{7,15},{8,12},{9,13},... | collective-permute-start | bytes 589832 | tf_op jit(solution)/shard_map/ppermute | solution.py:40
  60.7 5.6 %collective-permute-start.11 = (f32[192,128]{1,0:T(8,128)S(1)}, f32[192,128]{1,0:T(8,128)S(1)}, u32[]{:S(2)}, u32[]{:S(2)}) collective-permute-start(f32[192,128]{1,0:T(8,128)S(1)} %slice.75), channel_id=1, source_target_pairs={{0,1},{1,0},{2,3},{3,2},{4,5},{5,4},{6,7},{7,6},{8,9},{9,8},{10,11... | collective-permute-start | bytes 294920 | tf_op jit(solution)/shard_map/ppermute | solution.py:40
  64.4 4.6 %collective-permute-start.23 = (f32[96,128]{1,0:T(8,128)S(1)}, f32[96,128]{1,0:T(8,128)S(1)}, u32[]{:S(2)}, u32[]{:S(2)}) collective-permute-start(f32[96,128]{1,0:T(8,128)S(1)} %get-tuple-element.53), channel_id=1, source_target_pairs={{0,1},{1,0},{2,3},{3,2},{4,5},{5,4},{6,7},{7,6},{8,9},{9,8},{10,11... | collective-permute-start | bytes 147464 | tf_op jit(solution)/shard_map/ppermute | solution.py:40
  65.0 4.0 %collective-permute-start.22 = (f32[96,128]{1,0:T(8,128)S(1)}, f32[96,128]{1,0:T(8,128)S(1)}, u32[]{:S(2)}, u32[]{:S(2)}) collective-permute-start(f32[96,128]{1,0:T(8,128)S(1)} %get-tuple-element.54), channel_id=1, source_target_pairs={{0,2},{1,3},{2,0},{3,1},{4,6},{5,7},{6,4},{7,5},{8,10},{9,11},{10,... | collective-permute-start | bytes 147464 | tf_op jit(solution)/shard_map/ppermute | solution.py:40
  (3 other events, 11.0 us)
